TPU v7x, 32 devices: a whole 2x2x4 slice. The times are simulated.
32 devices in a mesh: rad: 4 (over z), azi: 2 (over y), ax: 4 (over x, core).
Axes of the slice: x: 2, y: 2, z: 4, core: 2. Of those that a mesh axis runs over, the one named last changes fastest.
Arguments:
- primal: float32 [5, 64, 64, 512], P(None, 'rad', 'azi', 'ax'), may hold values from -1 to 4, as said below
- adjoint: float32 [5, 64, 64, 512], P(None, 'rad', 'azi', 'ax'), may hold values from -6 to 6
- refine_flag: int32 [4, 4, 32], P('rad', 'azi', 'ax'), may hold values 0 or 1
- owner_map: int32 [4, 4, 32], P('rad', 'azi', 'ax'), may hold values from 0 to 31
- migrate_weight: int32 [4, 4, 32], P('rad', 'azi', 'ax'), may hold values from 1 to 16
- neighbor_list: int32 [4, 4, 32, 6], P('rad', 'azi', 'ax'), may hold values from 0 to 511
Outputs:
- indicator: float32 [64, 64, 512], P('rad', 'azi', 'ax')
- block_cost: float32 [4, 4, 32], P('rad', 'azi', 'ax')
- owner_load: float32 [4, 2, 4], P('rad', 'azi', 'ax')
Inputs may be any that keep to these rules, and one draw needn't show every extreme that they name: `primal`: density (field 0) lies in [0.5, 2], momenta (fields 1 to 3) in [-1, 1], energy (field 4) in [2, 4].
All inputs are finite; a program needn't handle non-finite values. No bound on the sum of `refine_flag` on one device may be relied on, other than what follows from the above.
Results may differ from a plain program's by a relative error of at most 0.00002.
Values sent between devices are 32-bit elements; how exact they have to be, the bound alone decides.
No kernel may reach another device: no remote copies, remote signals or barrier semaphores. Data moves between devices by JAX's collectives and lax.ppermute only.
A program may use at most 64 MiB of HBM per device.

v0:
```python
import jax
import jax.numpy as jnp
from jax import lax
from jax.sharding import PartitionSpec as P

BLK = 16


def with_halo(block, sides, width, periodic):
    for axis, dim in sides:
        count = lax.axis_size(axis)
        forward = [(i, i + 1) for i in range(count - 1)]
        if periodic:
            forward.append((count - 1, 0))
        backward = [(target, source) for source, target in forward]
        low = lax.ppermute(
            lax.slice_in_dim(block, block.shape[dim] - width, None, axis=dim), axis, forward
        )
        high = lax.ppermute(lax.slice_in_dim(block, 0, width, axis=dim), axis, backward)
        block = jnp.concatenate([low, block, high], axis=dim)
    return block


def euler_flux(face_state, along):
    density = face_state[0]
    momenta = face_state[1:4]
    energy = face_state[4]
    velocity = momenta[along] / density
    kinetic = (
        0.5
        * (momenta[0] * momenta[0] + momenta[1] * momenta[1] + momenta[2] * momenta[2])
        / density
    )
    pressure = 0.4 * (energy - kinetic)
    columns = [
        momenta[along],
        momenta[0] * velocity,
        momenta[1] * velocity,
        momenta[2] * velocity,
        (energy + pressure) * velocity,
    ]
    columns[1 + along] = columns[1 + along] + pressure
    return jnp.stack(columns)


def window(extended, along, start, count, padded_axes):
    pieces = [slice(None)] * 4
    for spatial in padded_axes:
        pieces[spatial] = slice(2, extended.shape[spatial] - 2)
    pieces[along] = slice(start, start + count)
    return extended[tuple(pieces)]


def axis_terms(ext_primal, ext_adjoint, along, padded_axes):
    length = ext_primal.shape[along] - 4
    high = (
        7.0 * window(ext_primal, along, 1, length + 1, padded_axes)
        - window(ext_primal, along, 0, length + 1, padded_axes)
    ) / 12.0
    low = (
        7.0 * window(ext_primal, along, 2, length + 1, padded_axes)
        - window(ext_primal, along, 3, length + 1, padded_axes)
    ) / 12.0
    fluxes = euler_flux(high + low, along - 1)
    balance = lax.slice_in_dim(fluxes, 1, length + 1, axis=along) - lax.slice_in_dim(
        fluxes, 0, length, axis=along
    )
    fourth = (
        window(ext_adjoint, along, 0, length, padded_axes)
        - 4.0 * window(ext_adjoint, along, 1, length, padded_axes)
        + 6.0 * window(ext_adjoint, along, 2, length, padded_axes)
        - 4.0 * window(ext_adjoint, along, 3, length, padded_axes)
        + window(ext_adjoint, along, 4, length, padded_axes)
    ) / 12.0
    return (balance, fourth)


def on_device(primal, adjoint, refine_flag, owner_map, migrate_weight, neighbor_list):
    wrap_primal, wrap_adjoint = (
        with_halo(primal, (("azi", 2),), 2, True),
        with_halo(adjoint, (("azi", 2),), 2, True),
    )
    full_primal, full_adjoint = (
        with_halo(wrap_primal, (("rad", 1), ("ax", 3)), 2, False),
        with_halo(wrap_adjoint, (("rad", 1), ("ax", 3)), 2, False),
    )
    sources = [(full_primal, full_adjoint, (1, 2, 3))] * 3
    balance = jnp.zeros(primal.shape, jnp.float32)
    weight = jnp.zeros(primal.shape, jnp.float32)
    for along in (1, 2, 3):
        ext_primal, ext_adjoint, padded_axes = sources[along - 1]
        part_balance, part_weight = axis_terms(ext_primal, ext_adjoint, along, padded_axes)
        balance = balance + part_balance
        weight = weight + part_weight
    indicator = jnp.abs(jnp.sum(weight * balance, axis=0))
    rows_rad, rows_azi, rows_ax = indicator.shape
    per_rad = rows_rad // BLK
    per_azi = rows_azi // BLK
    per_ax = rows_ax // BLK
    block_mean = indicator.reshape(per_rad, BLK, per_azi, BLK, per_ax, BLK).mean(axis=(1, 3, 5))
    all_means = lax.all_gather(block_mean.reshape(-1), ("rad", "azi", "ax"), axis=0, tiled=True)
    size_rad = lax.axis_size("rad")
    size_azi = lax.axis_size("azi")
    size_ax = lax.axis_size("ax")
    blocks_azi = per_azi * size_azi
    blocks_ax = per_ax * size_ax
    block_rad = neighbor_list // (blocks_azi * blocks_ax)
    block_azi = neighbor_list // blocks_ax % blocks_azi
    block_ax = neighbor_list % blocks_ax
    owner_dev = (
        block_rad // per_rad * size_azi + block_azi // per_azi
    ) * size_ax + block_ax // per_ax
    local_pos = (block_rad % per_rad * per_azi + block_azi % per_azi) * per_ax + block_ax % per_ax
    position = owner_dev * (per_rad * per_azi * per_ax) + local_pos
    beside_all = jnp.mean(jnp.take(all_means, position), axis=-1)
    smooth = 0.5 * block_mean + 0.5 * beside_all
    own_index = (
        lax.axis_index("rad") * size_azi + lax.axis_index("azi")
    ) * size_ax + lax.axis_index("ax")
    moved = (owner_map != own_index).astype(jnp.float32)
    block_cost = (
        smooth * (1.0 + 7.0 * refine_flag.astype(jnp.float32))
        + 0.25 * migrate_weight.astype(jnp.float32) * moved
    )
    devices = size_rad * size_azi * size_ax
    owner_flat = owner_map.reshape(-1)
    one_hot = (owner_flat[:, None] == jnp.arange(devices, dtype=jnp.int32)[None, :]).astype(
        jnp.float32
    )
    partial_load = jnp.sum(one_hot * block_cost.reshape(-1)[:, None], axis=0)
    mine = lax.psum_scatter(partial_load, ("rad", "azi", "ax"), scatter_dimension=0, tiled=True)
    owner_load = (mine / (per_rad * per_azi * per_ax)).reshape(1, 1, 1)
    return (indicator, block_cost, owner_load)


def solution(mesh):
    return jax.shard_map(
        on_device,
        mesh=mesh,
        in_specs=(
            P(None, "rad", "azi", "ax"),
            P(None, "rad", "azi", "ax"),
            P("rad", "azi", "ax"),
            P("rad", "azi", "ax"),
            P("rad", "azi", "ax"),
            P("rad", "azi", "ax", None),
        ),
        out_specs=(P("rad", "azi", "ax"), P("rad", "azi", "ax"), P("rad", "azi", "ax")),
        check_vma=False,
    )
```

profile of v0, /device:TPU:0, one launch (start us, length us, event | category | flops | bytes accessed | tf_op | source)
XLA Modules:
  0.0 193.1 jit_solution(1023090408130029628)
XLA Ops:
  0.6 1.2 fusion.52
  1.9 3.0 %collective-permute-start.6 = (f32[5,16,2,128]{3,1,2,0:T(8,128)S(1)}, f32[5,16,2,128]{3,1,2,0:T(8,128)S(1)}, u32[]{:S(2)}, u32[]{:S(2)}) collective-permute-start(f32[5,16,2,128]{3,1,2,0:T(8,128)S(1)} %copy.199), channel_id=1, source_target_pairs={{0,4},{4,0},{1,5},{5,1},{2,6},{6,2},{3,7},{7,3},{8,12},{12,8},{9,1... | collective-permute-start | bytes 245768 | tf_op jit(solution)/shard_map/ppermute | solution.py:16
  4.9 0.1 collective-permute-start.7
  5.0 1.1 fusion.51
  6.2 2.0 %collective-permute-start.1 = (f32[5,16,2,128]{3,1,2,0:T(8,128)S(1)}, f32[5,16,2,128]{3,1,2,0:T(8,128)}, u32[]{:S(2)}, u32[]{:S(2)}) collective-permute-start(f32[5,16,2,128]{3,1,2,0:T(8,128)S(1)} %copy.184), channel_id=1, source_target_pairs={{4,0},{0,4},{5,1},{1,5},{6,2},{2,6},{7,3},{3,7},{12,8},{8,12},{13,... | collective-permute-start | bytes 245768 | tf_op jit(solution)/shard_map/ppermute | solution.py:19
  8.2 0.6 copy.183
  8.8 0.1 collective-permute-start
  8.9 1.2 constant_dynamic-update-slice_fusion.1
  10.1 0.1 copy.177
  10.7 3.9 %collective-permute-start.8 = (f32[5,2,36,128]{3,2,1,0:T(8,128)S(1)}, f32[5,2,36,128]{3,2,1,0:T(8,128)S(1)}, u32[]{:S(2)}, u32[]{:S(2)}) collective-permute-start(f32[5,2,36,128]{3,2,1,0:T(8,128)S(1)} %get-tuple-element.38), channel_id=1, source_target_pairs={{0,8},{8,16},{16,24},{1,9},{9,17},{17,25},{2,10},{10,18},{18,26},{... | collective-permute-start | bytes 552968 | tf_op jit(solution)/shard_map/ppermute | solution.py:16
  14.6 1.3 collective-permute-start.9
  15.9 0.8 constant_dynamic-update-slice_fusion.2
  16.7 0.3 fusion.5
  17.0 0.1 add_dynamic-update-slice_fusion.2
  17.2 0.9 copy.155
  18.2 1.6 constant_dynamic-update-slice_fusion
  19.8 0.8 pad_maximum_fusion.21
  20.6 5.2 %collective-permute-start.2 = (f32[5,2,36,128]{3,2,1,0:T(8,128)}, f32[5,2,36,128]{3,2,1,0:T(8,128)}, u32[]{:S(2)}, u32[]{:S(2)}) collective-permute-start(f32[5,2,36,128]{3,2,1,0:T(8,128)} %get-tuple-element.34), channel_id=1, source_target_pairs={{0,8},{8,16},{16,24},{1,9},{9,17},{17,25},{2,10},{10,18},{18,26},{... | collective-permute-start | bytes 552968 | tf_op jit(solution)/shard_map/ppermute | solution.py:16
  25.8 1.3 collective-permute-start.3
  27.2 1.7 fusion.50
  28.9 0.3 maximum_maximum_fusion.2
  29.2 0.6 fusion.3
  29.8 0.8 slice_dynamic-update-slice_fusion.1
  30.6 0.4 copy-done.2
  31.0 1.0 add_dynamic-update-slice_fusion.1
  32.0 0.3 pad_maximum_fusion.2
  32.3 2.6 %fusion.49 = (f32[5,20,36,2]{3,2,1,0:T(8,128)}, f32[5,20,36,2]{3,2,1,0:T(8,128)}) fusion(f32[5,20,36,128]{3,2,1,0:T(8,128)S(1)} %pad_maximum_fusion.2), kind=kLoop, calls=%fused_computation.157 | loop fusion | bytes 115200 | tf_op jit(solution)/shard_map/slice | solution.py:17
  34.9 3.2 %copy.171 = f32[5,20,36,2]{2,1,3,0:T(8,128)} copy(f32[5,20,36,2]{3,2,1,0:T(8,128)} %get-tuple-element.28) | data formatting | bytes 57600 | tf_op jit(solution)/shard_map/slice | solution.py:17
  38.0 1.9 collective-permute-start.10
  39.9 3.2 %copy.173 = f32[5,20,36,2]{2,1,3,0:T(8,128)} copy(f32[5,20,36,2]{3,2,1,0:T(8,128)} %get-tuple-element.29) | data formatting | bytes 57600 | tf_op jit(solution)/shard_map/slice | solution.py:19
  43.1 1.3 collective-permute-start.11
  44.4 1.7 multiply_dynamic-update-slice_fusion.5
  46.1 1.7 multiply_dynamic-update-slice_fusion.4
  47.8 1.3 pad_maximum_fusion.1
  49.1 2.6 %fusion.48 = (f32[5,20,36,2]{3,2,1,0:T(8,128)}, f32[5,20,36,2]{3,2,1,0:T(8,128)}) fusion(f32[5,20,36,128]{3,2,1,0:T(8,128)S(1)} %pad_maximum_fusion.1), kind=kLoop, calls=%fused_computation.156 | loop fusion | bytes 115200 | tf_op jit(solution)/shard_map/slice | solution.py:17
  51.7 3.2 %copy.159 = f32[5,20,36,2]{2,1,3,0:T(8,128)} copy(f32[5,20,36,2]{3,2,1,0:T(8,128)} %get-tuple-element.26) | data formatting | bytes 57600 | tf_op jit(solution)/shard_map/slice | solution.py:17
  54.9 4.8 %collective-permute-start.4 = (f32[5,20,36,2]{2,1,3,0:T(8,128)}, f32[5,20,36,2]{2,1,3,0:T(8,128)}, u32[]{:S(2)}, u32[]{:S(2)}) collective-permute-start(f32[5,20,36,2]{2,1,3,0:T(8,128)} %copy.159), channel_id=1, source_target_pairs={{0,1},{1,2},{2,3},{4,5},{5,6},{6,7},{8,9},{9,10},{10,11},{12,13},{... | collective-permute-start | bytes 86408 | tf_op jit(solution)/shard_map/ppermute | solution.py:16
  59.6 3.2 %copy.161 = f32[5,20,36,2]{2,1,3,0:T(8,128)} copy(f32[5,20,36,2]{3,2,1,0:T(8,128)} %get-tuple-element.27) | data formatting | bytes 57600 | tf_op jit(solution)/shard_map/slice | solution.py:19
  62.8 1.5 collective-permute-start.5
  64.3 1.8 multiply_dynamic-update-slice_fusion.3
  66.1 3.2 %maximum_maximum_fusion.1 = (f32[5,18,36,128]{3,2,1,0:T(8,128)}, f32[5,18,36,128]{3,2,1,0:T(8,128)}) fusion(f32[5,16,2,128]{3,2,1,0:T(2,128)S(1)} %get-tuple-element.51, f32[5,16,32,128]{3,2,1,0:T(8,128)S(1)} %copy-done, f32[5,16,2,128]{3,2,1,0:T(2,128)S(1)} %copy.155, f32[5,2,36,128]{3,2,1,0:T(8,128)} %collective-permute-done.2, ...), kind=kLoop, calls=%fused_computation.11 | loop fusion | flops 2488320 | bytes 5160960 | tf_op jit(solution)/shard_map/concatenate | solution.py:20
  69.3 3.0 %copy.172 = f32[5,20,36,2]{3,2,1,0:T(8,128)} copy(f32[5,20,36,2]{2,1,3,0:T(8,128)} %collective-permute-done.10) | data formatting | bytes 57600 | tf_op jit(solution)/shard_map/ppermute | solution.py:16
  72.3 3.1 %copy.174 = f32[5,20,36,2]{3,2,1,0:T(8,128)} copy(f32[5,20,36,2]{2,1,3,0:T(8,128)} %collective-permute-done.11) | data formatting | bytes 57600 | tf_op jit(solution)/shard_map/ppermute | solution.py:19
  75.4 5.5 %maximum_maximum_fusion = (f32[5,20,36,130]{3,2,1,0:T(8,128)S(1)}, f32[5,20,36,130]{3,2,1,0:T(8,128)S(1)}) fusion(f32[5,2,36,128]{3,2,1,0:T(8,128)S(1)} %copy-done.6, f32[5,16,2,128]{3,2,1,0:T(2,128)S(1)} %copy.166, f32[5,16,32,128]{3,2,1,0:T(8,128)S(1)} %copy-done.1, f32[5,16,2,128]{3,2,1,0:T(2,128)S(1)} %copy.165, ...), kind=kLoop, calls=%fused_computation.1 | loop fusion | flops 4680000 | bytes 5644800 | tf_op jit(solution)/shard_map/concatenate | solution.py:20
  80.9 1.8 fusion.1
  82.7 0.1 multiply_dynamic-update-slice_fusion.2
  82.9 0.3 add_dynamic-update-slice_fusion
  83.3 0.1 multiply_dynamic-update-slice_fusion
  83.4 1.5 copy-done.4
  84.9 3.0 %copy.160 = f32[5,20,36,2]{3,2,1,0:T(8,128)} copy(f32[5,20,36,2]{2,1,3,0:T(8,128)} %collective-permute-done.4) | data formatting | bytes 57600 | tf_op jit(solution)/shard_map/ppermute | solution.py:16
  87.9 3.2 %copy.162 = f32[5,20,36,2]{3,2,1,0:T(8,128)} copy(f32[5,20,36,2]{2,1,3,0:T(8,128)} %collective-permute-done.5) | data formatting | bytes 57600 | tf_op jit(solution)/shard_map/ppermute | solution.py:19
  91.1 11.0 %fusion.26 = f32[16,32,128]{2,1,0:T(8,128)} fusion(f32[5,16,32,129]{3,2,1,0:T(8,128)} %copy-done.4, f32[5,16,32,128]{3,1,2,0:T(8,128)} %get-tuple-element.41, f32[5,16,32,128]{3,1,2,0:T(8,128)} %get-tuple-element.40, f32[5,17,32,128]{3,2,1,0:T(8,128)} %multiply_dynamic-update-slice_fusion.3, f32[5,20,36,2]{3,2,1,0:T(8,128)} %copy.162, ...), kind=kLoop, calls=%fused_computation.68 | loop fusion | flops 16646144 | bytes 17891584 | tf_op jit(solution)/shard_map/reduce_sum | solution.py:95
  102.1 1.4 copy.182
  103.6 0.3 abs_reduce_fusion
  103.9 0.1 reduce_sum.45
  104.0 0.1 reduce_sum.46
  104.2 0.2 dynamic-update-slice
  104.4 43.2 %all-reduce = f32[512]{0:T(512)S(1)} all-reduce(f32[512]{0:T(512)S(1)} %dynamic-update-slice), channel_id=1, replica_groups=mesh['rad'=4,'azi'=2,'ax'=4] {'rad','azi','ax'}, use_global_device_ids=true, to_apply=%add | all-reduce | flops 512 | bytes 4096
  147.6 1.3 gather_fusion
  148.9 0.1 select_reduce_fusion.1
  149.2 0.1 select_reduce_fusion
  149.3 40.4 %all-reduce.1 = f32[32]{0:T(128)S(1)} all-reduce(f32[32]{0:T(128)S(1)} %select_reduce_fusion), channel_id=2, replica_groups=mesh['rad'=4,'azi'=2,'ax'=4] {'rad','azi','ax'}, use_global_device_ids=true, to_apply=%region_5.6.clone | all-reduce | flops 32 | bytes 256
  189.6 1.2 copy.181
  190.8 0.6 dynamic-slice
  (59 shorter events, 1.1 us)
Async XLA Ops:
  0.6 8.3 %copy-start = (f32[5,16,32,128]{3,2,1,0:T(8,128)S(1)}, f32[5,16,32,128]{3,2,1,0:T(8,128)}, u32[]{:S(2)}) copy-start(f32[5,16,32,128]{3,2,1,0:T(8,128)} %param.7) | copy-start | bytes 3932164
  1.9 8.6 %collective-permute-start.6 = (f32[5,16,2,128]{3,1,2,0:T(8,128)S(1)}, f32[5,16,2,128]{3,1,2,0:T(8,128)S(1)}, u32[]{:S(2)}, u32[]{:S(2)}) collective-permute-start(f32[5,16,2,128]{3,1,2,0:T(8,128)S(1)} %copy.199), channel_id=1, source_target_pairs={{0,4},{4,0},{1,5},{5,1},{2,6},{6,2},{3,7},{7,3},{8,12},{12,8},{9,1... | collective-permute-start | bytes 245768 | tf_op jit(solution)/shard_map/ppermute | solution.py:16
  4.9 5.6 %collective-permute-start.7 = (f32[5,16,2,128]{3,1,2,0:T(8,128)S(1)}, f32[5,16,2,128]{3,1,2,0:T(8,128)S(1)}, u32[]{:S(2)}, u32[]{:S(2)}) collective-permute-start(f32[5,16,2,128]{3,1,2,0:T(8,128)S(1)} %copy.198), channel_id=1, source_target_pairs={{4,0},{0,4},{5,1},{1,5},{6,2},{2,6},{7,3},{3,7},{12,8},{8,12},{13,... | collective-permute-start | bytes 245768 | tf_op jit(solution)/shard_map/ppermute | solution.py:19
  6.2 12.0 %collective-permute-start.1 = (f32[5,16,2,128]{3,1,2,0:T(8,128)S(1)}, f32[5,16,2,128]{3,1,2,0:T(8,128)}, u32[]{:S(2)}, u32[]{:S(2)}) collective-permute-start(f32[5,16,2,128]{3,1,2,0:T(8,128)S(1)} %copy.184), channel_id=1, source_target_pairs={{4,0},{0,4},{5,1},{1,5},{6,2},{2,6},{7,3},{3,7},{12,8},{8,12},{13,... | collective-permute-start | bytes 245768 | tf_op jit(solution)/shard_map/ppermute | solution.py:19
  8.2 2.0 %copy-start.7 = (s32[1,2,8,6]{2,1,3,0:T(2,128)S(1)}, s32[1,2,8,6]{2,1,3,0:T(2,128)}, u32[]{:S(2)}) copy-start(s32[1,2,8,6]{2,1,3,0:T(2,128)} %param.11) | copy-start | bytes 1156
  8.2 2.2 %copy-start.8 = (s32[1,2,8]{2,1,0:T(2,128)S(1)}, s32[1,2,8]{2,1,0:T(2,128)}, u32[]{:S(2)}) copy-start(s32[1,2,8]{2,1,0:T(2,128)} %param.9) | copy-start | bytes 196
  8.8 1.8 copy-start.1
  8.8 8.4 %collective-permute-start = (f32[5,16,2,128]{3,1,2,0:T(8,128)}, f32[5,16,2,128]{3,1,2,0:T(8,128)}, u32[]{:S(2)}, u32[]{:S(2)}) collective-permute-start(f32[5,16,2,128]{3,1,2,0:T(8,128)} %copy.183), channel_id=1, source_target_pairs={{0,4},{4,0},{1,5},{5,1},{2,6},{6,2},{3,7},{7,3},{8,12},{12,8},{9,1... | collective-permute-start | bytes 245768 | tf_op jit(solution)/shard_map/ppermute | solution.py:16
  10.7 18.2 %collective-permute-start.8 = (f32[5,2,36,128]{3,2,1,0:T(8,128)S(1)}, f32[5,2,36,128]{3,2,1,0:T(8,128)S(1)}, u32[]{:S(2)}, u32[]{:S(2)}) collective-permute-start(f32[5,2,36,128]{3,2,1,0:T(8,128)S(1)} %get-tuple-element.38), channel_id=1, source_target_pairs={{0,8},{8,16},{16,24},{1,9},{9,17},{17,25},{2,10},{10,18},{18,26},{... | collective-permute-start | bytes 552968 | tf_op jit(solution)/shard_map/ppermute | solution.py:16
  14.6 14.3 %collective-permute-start.9 = (f32[5,2,36,128]{3,2,1,0:T(8,128)S(1)}, f32[5,2,36,128]{3,2,1,0:T(8,128)S(1)}, u32[]{:S(2)}, u32[]{:S(2)}) collective-permute-start(f32[5,2,36,128]{3,2,1,0:T(8,128)S(1)} %get-tuple-element.39), channel_id=1, source_target_pairs={{8,0},{16,8},{24,16},{9,1},{17,9},{25,17},{10,2},{18,10},{26,18},{... | collective-permute-start | bytes 552968 | tf_op jit(solution)/shard_map/ppermute | solution.py:19
  20.6 27.2 %collective-permute-start.2 = (f32[5,2,36,128]{3,2,1,0:T(8,128)}, f32[5,2,36,128]{3,2,1,0:T(8,128)}, u32[]{:S(2)}, u32[]{:S(2)}) collective-permute-start(f32[5,2,36,128]{3,2,1,0:T(8,128)} %get-tuple-element.34), channel_id=1, source_target_pairs={{0,8},{8,16},{16,24},{1,9},{9,17},{17,25},{2,10},{10,18},{18,26},{... | collective-permute-start | bytes 552968 | tf_op jit(solution)/shard_map/ppermute | solution.py:16
  25.8 22.0 %collective-permute-start.3 = (f32[5,2,36,128]{3,2,1,0:T(8,128)}, f32[5,2,36,128]{3,2,1,0:T(8,128)}, u32[]{:S(2)}, u32[]{:S(2)}) collective-permute-start(f32[5,2,36,128]{3,2,1,0:T(8,128)} %get-tuple-element.35), channel_id=1, source_target_pairs={{8,0},{16,8},{24,16},{9,1},{17,9},{25,17},{10,2},{18,10},{26,18},{... | collective-permute-start | bytes 552968 | tf_op jit(solution)/shard_map/ppermute | solution.py:19
  28.9 3.1 %copy-start.5 = (f32[5,2,36,128]{3,2,1,0:T(8,128)}, f32[5,2,36,128]{3,2,1,0:T(8,128)S(1)}, u32[]{:S(2)}) copy-start(f32[5,2,36,128]{3,2,1,0:T(8,128)S(1)} %collective-permute-done.9) | copy-start | bytes 552964
  29.8 1.2 copy-start.2
  38.0 31.3 %collective-permute-start.10 = (f32[5,20,36,2]{2,1,3,0:T(8,128)}, f32[5,20,36,2]{2,1,3,0:T(8,128)}, u32[]{:S(2)}, u32[]{:S(2)}) collective-permute-start(f32[5,20,36,2]{2,1,3,0:T(8,128)} %copy.171), channel_id=1, source_target_pairs={{0,1},{1,2},{2,3},{4,5},{5,6},{6,7},{8,9},{9,10},{10,11},{12,13},{... | collective-permute-start | bytes 86408 | tf_op jit(solution)/shard_map/ppermute | solution.py:16
  43.1 29.2 %collective-permute-start.11 = (f32[5,20,36,2]{2,1,3,0:T(8,128)}, f32[5,20,36,2]{2,1,3,0:T(8,128)}, u32[]{:S(2)}, u32[]{:S(2)}) collective-permute-start(f32[5,20,36,2]{2,1,3,0:T(8,128)} %copy.173), channel_id=1, source_target_pairs={{1,0},{2,1},{3,2},{5,4},{6,5},{7,6},{9,8},{10,9},{11,10},{13,12},{... | collective-permute-start | bytes 86408 | tf_op jit(solution)/shard_map/ppermute | solution.py:19
  54.9 30.0 %collective-permute-start.4 = (f32[5,20,36,2]{2,1,3,0:T(8,128)}, f32[5,20,36,2]{2,1,3,0:T(8,128)}, u32[]{:S(2)}, u32[]{:S(2)}) collective-permute-start(f32[5,20,36,2]{2,1,3,0:T(8,128)} %copy.159), channel_id=1, source_target_pairs={{0,1},{1,2},{2,3},{4,5},{5,6},{6,7},{8,9},{9,10},{10,11},{12,13},{... | collective-permute-start | bytes 86408 | tf_op jit(solution)/shard_map/ppermute | solution.py:16
  62.8 25.1 %collective-permute-start.5 = (f32[5,20,36,2]{2,1,3,0:T(8,128)}, f32[5,20,36,2]{2,1,3,0:T(8,128)}, u32[]{:S(2)}, u32[]{:S(2)}) collective-permute-start(f32[5,20,36,2]{2,1,3,0:T(8,128)} %copy.161), channel_id=1, source_target_pairs={{1,0},{2,1},{3,2},{5,4},{6,5},{7,6},{9,8},{10,9},{11,10},{13,12},{... | collective-permute-start | bytes 86408 | tf_op jit(solution)/shard_map/ppermute | solution.py:19
  72.3 3.1 %copy-start.6 = (f32[5,2,36,128]{3,2,1,0:T(8,128)S(1)}, f32[5,2,36,128]{3,2,1,0:T(8,128)}, u32[]{:S(2)}) copy-start(f32[5,2,36,128]{3,2,1,0:T(8,128)} %copy-done.5) | copy-start | bytes 552964
  83.4 1.5 copy-start.4
  87.9 3.2 %copy-start.3 = (f32[5,18,36,128]{3,2,1,0:T(8,128)S(1)}, f32[5,18,36,128]{3,2,1,0:T(8,128)}, u32[]{:S(2)}) copy-start(f32[5,18,36,128]{3,2,1,0:T(8,128)} %get-tuple-element.32) | copy-start | bytes 4976644
  147.6 1.5 copy-start.9
  147.6 1.5 copy-start.10
  149.1 42.9 %copy-start.11 = (f32[1,2,8]{2,1,0:T(2,128)}, f32[1,2,8]{2,1,0:T(2,128)S(1)}, u32[]{:S(2)}) copy-start(f32[1,2,8]{2,1,0:T(2,128)S(1)} %fusion.47) | copy-start | bytes 196
where the time goes:
time: 194 us; the launch traced here: 193 us
  blocking collectives  83.5 us (43%)
  local copies, waits for them, and re-layouts  47.5 us (24%)
  other arithmetic  32.9 us (17%)
  starting transfers between devices  26.4 us (14%)
  between operations  2.8 us (1%)
    unnamed x2, blocking collectives  83.5 us
    ppermute x6, starting transfers between devices, with_halo(): lax.ppermute(lax.slice_in_dim(block, block.shape[dim] - width, None, axis...  19 us
    slice x6, local copies, waits for them, and re-layouts, with_halo(): lax.slice_in_dim(block, block.shape[dim] - width, None, axis=dim)  13.8 us
    reduce_sum x1, other arithmetic, on_device(): indicator = jnp.abs(jnp.sum(weight * balance, axis=0))  11 us
    concatenate x5, other arithmetic, with_halo(): block = jnp.concatenate([low, block, high], axis=dim)  10.6 us
    unnamed x39, local copies, waits for them, and re-layouts  8.15 us
    ppermute x6, starting transfers between devices, with_halo(): lax.ppermute(lax.slice_in_dim(block, 0, width, axis=dim), axis, backward)  7.4 us
    ppermute x4, local copies, waits for them, and re-layouts, with_halo(): lax.ppermute(lax.slice_in_dim(block, block.shape[dim] - width, None, axis...  7.04 us
  transfers between devices with their start and end apart: 12, of which 0 were waited for; matrix products, arithmetic and copies ran while one was open for 30% of the time, Pallas kernels for 0%

commit v1 on v0

v1 whole, which is shorter than its diff:
```python
import functools

import jax
import jax.numpy as jnp
from jax import lax
from jax.experimental import pallas as pl
from jax.experimental.pallas import tpu as pltpu
from jax.sharding import PartitionSpec as P

BLK = 16
F = 5
LO = 16
AXES = ("rad", "azi", "ax")


def line_pairs(count, first):
    pairs = []
    for i in range(first, count - 1, 2):
        pairs += [(i, i + 1), (i + 1, i)]
    return pairs


def ring(count, step):
    return [(i, (i + step) % count) for i in range(count)]


def pack_kernel(dims, prim, adj, rad_a, rad_b, azi_s, ax_s, buf, sems):
    nr, na, nx = dims
    odd = lax.rem(lax.axis_index("rad"), 2)
    first = jnp.where(odd == 0, nr - 2, 0)
    copies = []
    for t, src in enumerate((prim, adj)):
        rows = pl.ds(t * F, F)
        for i, (a, b) in enumerate(
            (
                (src.at[:, pl.ds(first, 2)], rad_a.at[rows]),
                (src.at[:, pl.ds(nr - 2 - first, 2)], rad_b.at[rows]),
                (src.at[:, :, pl.ds(0, 2)], azi_s.at[rows, :, pl.ds(0, 2)]),
                (src.at[:, :, pl.ds(na - 2, 2)], azi_s.at[rows, :, pl.ds(2, 2)]),
            )
        ):
            copies.append(pltpu.make_async_copy(a, b, sems.at[t, i]))
    loads = []
    for t, src in enumerate((prim, adj)):
        for f in range(F):
            loads.append(pltpu.make_async_copy(src.at[f], buf.at[t * F + f], sems.at[2 + t, f]))
    for c in copies + loads:
        c.start()
    slot = lax.broadcasted_iota(jnp.int32, (8, nx), 1) // 4
    tiles = na // 8
    per = nx // 4
    for f in range(2 * F):
        loads[f].wait()
        for h in range(nr * tiles // per):
            acc = jnp.zeros((8, nx), jnp.float32)
            for j in range(per):
                k = h * per + j
                x = buf[f, k // tiles, pl.ds(8 * (k % tiles), 8), :]
                y = pltpu.roll(x, (4 * j + 2) % nx, 1)
                acc = jnp.where(slot == j, y, acc)
            ax_s[f, h] = acc
    for c in copies:
        c.wait()


def flux(s, along):
    inv = 1.0 / s[0]
    v = s[1 + along] * inv
    kin = (s[1] * s[1] + s[2] * s[2] + s[3] * s[3]) * inv
    p = 0.4 * s[4] - 0.2 * kin
    out = [s[1 + along], s[1] * v, s[2] * v, s[3] * v, (s[4] + p) * v]
    out[1 + along] = out[1 + along] + p
    return out


def face(m1, c, p1, p2):
    return 7.0 * (c + p1) - (m1 + p2)


def main_kernel(
    dims, shape, prim, adj, rad_a, rad_b, azi_l, azi_r, ax_a, ax_b, ax_s, row,
    ind, send, ext, got, fm, frad, fazi, sems,
):
    nr, na, nx = dims
    n_rad, n_azi, n_ax = shape
    i_rad = lax.axis_index("rad")
    i_ax = lax.axis_index("ax")
    odd = lax.rem(i_rad, 2)
    tiles = na // 8
    per = nx // 4
    cells = pl.ds(LO, na)
    copies = []
    for t, src in enumerate((prim, adj)):
        fs = pl.ds(t * F, F)
        at_a = jnp.where(odd == 0, nr + 2, 0)
        for i, (a, b) in enumerate(
            (
                (src, ext.at[fs, pl.ds(2, nr), cells]),
                (rad_a.at[fs], ext.at[fs, pl.ds(at_a, 2), cells]),
                (rad_b.at[fs], ext.at[fs, pl.ds(nr + 2 - at_a, 2), cells]),
                (azi_l.at[fs, :, pl.ds(2, 2)], ext.at[fs, pl.ds(2, nr), pl.ds(LO - 2, 2)]),
                (azi_r.at[fs, :, pl.ds(0, 2)], ext.at[fs, pl.ds(2, nr), pl.ds(LO + na, 2)]),
            )
        ):
            copies.append(pltpu.make_async_copy(a, b, sems.at[t, i]))
    for c in copies:
        c.start()

    lane = lax.broadcasted_iota(jnp.int32, (8, nx), 1)
    part = lane % 4
    even_ax = lax.rem(i_ax, 2) == 0
    halves = nr * tiles // per
    for h in range(halves):
        face_in = []
        for f in range(2 * F):
            a, b = ax_a[f, h], ax_b[f, h]
            left = jnp.where(even_ax, b, a)
            right = jnp.where(even_ax, a, b)
            left = jnp.where(i_ax == 0, 0.0, left)
            right = jnp.where(i_ax == n_ax - 1, 0.0, right)
            got[f, h] = jnp.where(part < 2, left, right)
            if f < F:
                q = jnp.where(part < 2, left, ax_s[f, h])
                face_in.append(
                    face(pltpu.roll(q, 1, 1), q, pltpu.roll(q, nx - 1, 1), pltpu.roll(q, nx - 2, 1))
                )
        ok = part == 1
        face_in[0] = jnp.where(ok, face_in[0], 1.0)
        for f, x in enumerate(flux(face_in, 2)):
            fm[f, h] = x
    for c in copies:
        c.wait()

    zero = jnp.zeros((2 * F, 2, na, nx), jnp.float32)

    @pl.when(i_rad == 0)
    def _():
        ext[:, 0:2, LO:LO + na, :] = zero

    @pl.when(i_rad == n_rad - 1)
    def _():
        ext[:, nr + 2:nr + 4, LO:LO + na, :] = zero

    def rad_flux(r, a):
        rows = pl.ds(LO + 8 * a, 8)
        s = [face(*(ext[f, r + o, rows, :] for o in range(4))) for f in range(F)]
        return flux(s, 0)

    for a in range(tiles):
        for f, x in enumerate(rad_flux(0, a)):
            frad[f, a] = x

    def azi_flux(r, a):
        s = [face(*(ext[f, r + 2, pl.ds(LO + 8 * a + o, 8), :] for o in (-1, 0, 1, 2))) for f in range(F)]
        return flux(s, 1)

    def body(r, sums):
        for a in range(-1, tiles):
            for f, x in enumerate(azi_flux(r, a)):
                fazi[f, pl.ds(LO + 8 * a, 8), :] = x
        out = []
        for a in range(tiles):
            rows = pl.ds(LO + 8 * a, 8)
            k = r * tiles + a
            h = k // per
            j = lax.rem(k, per)
            turn = lax.rem(2 * nx - (4 * j + 2), nx)
            turn_f = lax.rem(2 * nx - (4 * j + 2), nx)
            up = rad_flux(r + 1, a)
            bal = []
            for f in range(F):
                bal.append(up[f] - frad[f, a])
                frad[f, a] = up[f]
            for f in range(F):
                bal[f] = bal[f] + (fazi[f, rows, :] - fazi[f, pl.ds(LO + 8 * a - 1, 8), :])
            s = []
            for f in range(F):
                x = ext[f, r + 2, rows, :]
                hal = pltpu.roll(got[f, h], turn, 1)
                s.append(
                    face(
                        pltpu.roll(jnp.where(lane == nx - 1, hal, x), 1, 1),
                        x,
                        pltpu.roll(jnp.where(lane == 0, hal, x), nx - 1, 1),
                        pltpu.roll(jnp.where(lane < 2, hal, x), nx - 2, 1),
                    )
                )
            for f, x in enumerate(flux(s, 2)):
                edge = pltpu.roll(fm[f, h], turn_f, 1)
                low = pltpu.roll(jnp.where(lane == nx - 1, edge, x), 1, 1)
                bal[f] = bal[f] + (x - low)
            total = None
            for f in range(F):
                g = F + f
                z = ext[g, r + 2, rows, :]
                hal = pltpu.roll(got[g, h], turn, 1)
                up1 = pltpu.roll(jnp.where(lane == 0, hal, z), nx - 1, 1)
                up2 = pltpu.roll(jnp.where(lane < 2, hal, z), nx - 2, 1)
                dn1 = pltpu.roll(jnp.where(lane == nx - 1, hal, z), 1, 1)
                dn2 = pltpu.roll(jnp.where(lane >= nx - 2, hal, z), 2, 1)
                two = (
                    (ext[g, r, rows, :] + ext[g, r + 4, rows, :])
                    + (ext[g, r + 2, pl.ds(LO + 8 * a - 2, 8), :] + ext[g, r + 2, pl.ds(LO + 8 * a + 2, 8), :])
                    + (dn2 + up2)
                )
                one = (
                    (ext[g, r + 1, rows, :] + ext[g, r + 3, rows, :])
                    + (ext[g, r + 2, pl.ds(LO + 8 * a - 1, 8), :] + ext[g, r + 2, pl.ds(LO + 8 * a + 1, 8), :])
                    + (dn1 + up1)
                )
                w = (two - 4.0 * one + 18.0 * z) * bal[f]
                total = w if total is None else total + w
            total = jnp.abs(total) * (1.0 / 144.0)
            ind[r, pl.ds(8 * a, 8), :] = total
            out.append(sums[a] + total)
        return tuple(out)

    sums = lax.fori_loop(0, nr, body, tuple(jnp.zeros((8, nx), jnp.float32) for _ in range(tiles)))

    groups = nx // BLK
    halves_a = na // BLK
    per_tile = BLK // 8
    means = jnp.zeros((8, nx), jnp.float32)
    for b in range(halves_a):
        t = sums[b * per_tile]
        for i in range(1, per_tile):
            t = t + sums[b * per_tile + i]
        t = jnp.broadcast_to(jnp.sum(t, axis=0, keepdims=True), (8, nx))
        for sh in (8, 4, 2, 1):
            t = t + pltpu.roll(t, nx - sh, 1)
        t = jnp.take_along_axis(t, (lane % groups) * BLK, axis=1)
        means = jnp.where(lane // groups == b, t, means)
    means = means * (1.0 / BLK**3)
    head = jnp.broadcast_to(row[:, 0:nx], (8, nx))
    head = jnp.where(lane < groups * halves_a, means, head)
    tail = jnp.broadcast_to(row[:, nx:2 * nx], (8, nx))
    for d in range(send.shape[0] // 8):
        send[pl.ds(8 * d, 8), 0:nx] = head
        send[pl.ds(8 * d, 8), nx:2 * nx] = tail


def final_kernel(n_loc, per_ax, data, cost, load):
    n_dev = data.shape[0]
    nx = data.shape[1] // 2
    me = (lax.axis_index("rad") * lax.axis_size("azi") + lax.axis_index("azi")) * lax.axis_size(
        "ax"
    ) + lax.axis_index("ax")
    lane = lax.broadcasted_iota(jnp.int32, (8, nx), 1)
    sub = lax.broadcasted_iota(jnp.int32, (8, nx), 0)

    def group(g, carry):
        acc_load, acc_cost = carry
        rows = pl.ds(pl.multiple_of(8 * g, 8), 8)
        head = data[rows, 0:nx]
        tail = data[rows, nx:2 * nx]
        spot = head.astype(jnp.int32)
        dev = spot // n_loc
        pos = spot - dev * n_loc

        def look(d8, acc):
            table = data[pl.ds(pl.multiple_of(8 * d8, 8), 8), 0:nx]
            for i in range(8):
                t = jnp.broadcast_to(table[i:i + 1, :], (8, nx))
                v = jnp.take_along_axis(t, pos, axis=1)
                acc = jnp.where(dev == d8 * 8 + i, v, acc)
            return acc

        val = lax.fori_loop(0, n_dev // 8, look, jnp.zeros((8, nx), jnp.float32), unroll=n_dev <= 32)
        beside = None
        for j in range(6):
            x = pltpu.roll(val, nx - n_loc * (1 + j), 1)
            beside = x if beside is None else beside + x
        smooth = 0.5 * head + (0.5 / 6.0) * beside
        refine = pltpu.roll(head, nx - 7 * n_loc, 1)
        owner = tail.astype(jnp.int32)
        weight = pltpu.roll(tail, nx - n_loc, 1)
        home = sub + 8 * g
        c = smooth * (1.0 + 7.0 * refine) + jnp.where(owner != home, 0.25 * weight, 0.0)
        ok = lane < n_loc
        acc_load = acc_load + jnp.where(ok & (owner == me), c, 0.0)
        acc_cost = acc_cost + jnp.where(home == me, c, 0.0)
        return acc_load, acc_cost

    zero = jnp.zeros((8, nx), jnp.float32)
    acc_load, acc_cost = lax.fori_loop(0, n_dev // 8, group, (zero, zero), unroll=n_dev <= 32)
    own = jnp.sum(acc_cost, axis=0, keepdims=True)
    for b in range(n_loc // per_ax):
        x = own if b == 0 else pltpu.roll(own, nx - b * per_ax, 1)
        cost[0, pl.ds(b, 1), :] = x[:, 0:per_ax]
    total = jnp.sum(jnp.sum(acc_load, axis=0, keepdims=True), axis=1, keepdims=True) * (1.0 / n_loc)
    load[0] = total


def on_device(primal, adjoint, refine_flag, owner_map, migrate_weight, neighbor_list):
    _, nr, na, nx = primal.shape
    dims = (nr, na, nx)
    n_rad, n_azi, n_ax = (lax.axis_size(a) for a in AXES)
    n_dev = n_rad * n_azi * n_ax
    tiles = na // 8
    halves = nr * tiles // (nx // 4)
    f32 = functools.partial(jax.ShapeDtypeStruct, dtype=jnp.float32)
    anyspec = pl.BlockSpec(memory_space=pl.ANY)
    hbm = pl.BlockSpec(memory_space=pltpu.HBM)
    vmem = pl.BlockSpec(memory_space=pltpu.VMEM)

    rad_a, rad_b, azi_s, ax_s = pl.pallas_call(
        functools.partial(pack_kernel, dims),
        out_shape=(
            f32((2 * F, 2, na, nx)),
            f32((2 * F, 2, na, nx)),
            f32((2 * F, nr, 4, nx)),
            f32((2 * F, halves, 8, nx)),
        ),
        in_specs=[hbm, hbm],
        out_specs=(anyspec, anyspec, anyspec, vmem),
        scratch_shapes=[
            pltpu.VMEM((2 * F, nr, na, nx), jnp.float32),
            pltpu.SemaphoreType.DMA((4, F)),
        ],
        compiler_params=pltpu.CompilerParams(vmem_limit_bytes=16 << 20),
        name="pack",
    )(primal, adjoint)

    ax_a = lax.ppermute(ax_s, "ax", line_pairs(n_ax, 0))
    ax_b = lax.ppermute(ax_s, "ax", line_pairs(n_ax, 1))
    azi_l = lax.ppermute(azi_s, "azi", ring(n_azi, 1))
    azi_r = azi_l if n_azi == 2 else lax.ppermute(azi_s, "azi", ring(n_azi, -1))
    rad_a = lax.ppermute(rad_a, "rad", line_pairs(n_rad, 0))
    rad_b = lax.ppermute(rad_b, "rad", line_pairs(n_rad, 1))

    per_rad, per_azi, per_ax = nr // BLK, na // BLK, nx // BLK
    n_loc = per_rad * per_azi * per_ax
    blocks_azi, blocks_ax = per_azi * n_azi, per_ax * n_ax
    b_rad = neighbor_list // (blocks_azi * blocks_ax)
    b_azi = neighbor_list // blocks_ax % blocks_azi
    b_ax = neighbor_list % blocks_ax
    device = (b_rad // per_rad * n_azi + b_azi // per_azi) * n_ax + b_ax // per_ax
    local = (b_rad % per_rad * per_azi + b_azi % per_azi) * per_ax + b_ax % per_ax
    spot = (device * n_loc + local).reshape(n_loc, 6).T.reshape(-1)
    row = jnp.concatenate(
        [
            jnp.zeros((n_loc,), jnp.int32),
            spot,
            refine_flag.reshape(-1),
            owner_map.reshape(-1),
            migrate_weight.reshape(-1),
        ]
    ).astype(jnp.float32)
    row = jnp.pad(row, (0, 2 * nx - row.shape[0]))[None]

    indicator, send = pl.pallas_call(
        functools.partial(main_kernel, dims, (n_rad, n_azi, n_ax)),
        out_shape=(f32(dims), f32((n_dev, 2 * nx))),
        in_specs=[hbm] * 2 + [anyspec] * 4 + [vmem] * 4,
        out_specs=(vmem, vmem),
        scratch_shapes=[
            pltpu.VMEM((2 * F, nr + 4, LO + na + 8, nx), jnp.float32),
            pltpu.VMEM((2 * F, halves, 8, nx), jnp.float32),
            pltpu.VMEM((F, halves, 8, nx), jnp.float32),
            pltpu.VMEM((F, tiles, 8, nx), jnp.float32),
            pltpu.VMEM((F, LO + na, nx), jnp.float32),
            pltpu.SemaphoreType.DMA((2, 5)),
        ],
        compiler_params=pltpu.CompilerParams(vmem_limit_bytes=32 << 20),
        name="stencil",
    )(primal, adjoint, rad_a, rad_b, azi_l, azi_r, ax_a, ax_b, ax_s, row)

    data = lax.all_to_all(send, AXES, 0, 0, tiled=True)

    cost, load = pl.pallas_call(
        functools.partial(final_kernel, n_loc, per_ax),
        out_shape=(f32((per_rad, per_azi, per_ax)), f32((1, 1, 1))),
        in_specs=[vmem],
        out_specs=(vmem, vmem),
        name="blocks",
    )(data)
    return indicator, cost, load


def solution(mesh):
    spec = P("rad", "azi", "ax")
    field = P(None, "rad", "azi", "ax")
    return jax.shard_map(
        on_device,
        mesh=mesh,
        in_specs=(field, field, spec, spec, spec, P("rad", "azi", "ax", None)),
        out_specs=(spec, spec, spec),
        check_vma=False,
    )
```

time: 194 us -> 48.2 us (0.25)
  blocking collectives: 83.5 us -> 12.7 us
  local copies, waits for them, and re-layouts: 47.5 us -> 3.77 us
  other arithmetic: 32.9 us -> 0.1 us
  starting transfers between devices: 26.4 us -> 6.66 us
  Pallas kernels: 0 us -> 17.4 us
  waiting for transfers between devices: 0.03 us -> 6.57 us
  between operations: 2.8 us -> 0.73 us
    unnamed x2 -> x0, blocking collectives: 83.5 us -> none
    slice x9 -> x0, local copies, waits for them, and re-layouts: 21.8 us -> none  [the longest x6 13.8 us: with_halo(): lax.slice_in_dim(block, block.shape[dim] - width, None, axis=dim)]
    ppermute x12 -> x5, starting transfers between devices: 26.4 us -> 6.66 us  [the longest x1 3.09 us: on_device(): rad_a = lax.ppermute(rad_a, 'rad', line_pairs(n_rad, 0))]
    pallas_call x0 -> x3, Pallas kernels: none -> 17.4 us  [the longest x1 13.8 us: on_device(): pl.pallas_call(functools.partial(main_kernel, dims, (n_rad, n_azi, n_ax))...]
    ppermute x7 -> x0, local copies, waits for them, and re-layouts: 13.3 us -> none  [the longest x4 7.04 us: with_halo(): lax.ppermute(lax.slice_in_dim(block, block.shape[dim] - width, None, axis...]
    all_to_all x0 -> x1, blocking collectives: none -> 12.7 us  [on_device(): data = lax.all_to_all(send, AXES, 0, 0, tiled=True)]
    reduce_sum x5 -> x0, other arithmetic: 11.6 us -> none  [the longest x1 11 us: on_device(): indicator = jnp.abs(jnp.sum(weight * balance, axis=0))]
    concatenate x5 -> x0, other arithmetic: 10.6 us -> none  [with_halo(): block = jnp.concatenate([low, block, high], axis=dim)]
  transfers between devices with their start and end apart: 12 -> 5, of which waited for: 0 -> 2; matrix products, arithmetic and copies ran while one was open for 30% -> 1% of each run, Pallas kernels for 0% -> 0%
where the time goes in v1:
time: 48.2 us; the launch traced here: 47.9 us
  Pallas kernels  17.4 us (36%)
  blocking collectives  12.7 us (26%)
  starting transfers between devices  6.66 us (14%)
  waiting for transfers between devices  6.57 us (14%)
  local copies, waits for them, and re-layouts  3.77 us (8%)
  between operations  0.73 us (2%)
    pallas_call x1, Pallas kernels, on_device(): pl.pallas_call(functools.partial(main_kernel, dims, (n_rad, n_azi, n_ax))...  13.8 us
    all_to_all x1, blocking collectives, on_device(): data = lax.all_to_all(send, AXES, 0, 0, tiled=True)  12.7 us
    ppermute x1, waiting for transfers between devices, on_device(): rad_a = lax.ppermute(rad_a, 'rad', line_pairs(n_rad, 0))  3.7 us
    unnamed x17, local copies, waits for them, and re-layouts  3.25 us
    ppermute x1, starting transfers between devices, on_device(): rad_a = lax.ppermute(rad_a, 'rad', line_pairs(n_rad, 0))  3.09 us
    ppermute x1, waiting for transfers between devices, on_device(): azi_l = lax.ppermute(azi_s, 'azi', ring(n_azi, 1))  2.86 us
    pallas_call x1, Pallas kernels, on_device(): pl.pallas_call(functools.partial(pack_kernel, dims), out_shape=(f32((2 *...  1.76 us
    pallas_call x1, Pallas kernels, on_device(): pl.pallas_call(functools.partial(final_kernel, n_loc, per_ax), out_shape=...  1.76 us
  transfers between devices with their start and end apart: 5, of which 2 were waited for; matrix products, arithmetic and copies ran while one was open for 1% of the time, Pallas kernels for 0%

profile of v1, /device:TPU:0, one launch (start us, length us, event | category | flops | bytes accessed | tf_op | source)
XLA Modules:
  0.0 47.9 jit_solution(8828871104353914704)
XLA Ops:
  0.6 0.0 copy-start
  0.6 1.3 %copy-done = f32[5,16,32,128]{3,2,1,0:T(8,128)S(1)} copy-done((f32[5,16,32,128]{3,2,1,0:T(8,128)S(1)}, f32[5,16,32,128]{3,2,1,0:T(8,128)}, u32[]{:S(2)}) %copy-start) | copy-done | bytes 1310744
  1.9 0.0 copy-start.2
  2.0 1.3 %copy-done.2 = f32[5,16,32,128]{3,2,1,0:T(8,128)S(1)} copy-done((f32[5,16,32,128]{3,2,1,0:T(8,128)S(1)}, f32[5,16,32,128]{3,2,1,0:T(8,128)}, u32[]{:S(2)}) %copy-start.2) | copy-done | bytes 1310744
  3.3 0.0 copy-start.4
  3.3 0.0 copy-start.5
  3.3 0.0 copy-start.6
  3.3 0.0 copy-start.7
  3.3 0.0 copy-start.1
  3.3 0.0 copy-start.3
  3.3 1.8 %pack.1 = (f32[10,2,32,128]{3,2,1,0:T(8,128)}, f32[10,2,32,128]{3,2,1,0:T(8,128)}, f32[10,16,4,128]{3,2,1,0:T(4,128)}, f32[10,2,8,128]{3,2,1,0:T(8,128)S(1)}) custom-call(f32[5,16,32,128]{3,2,1,0:T(8,128)S(1)} %copy-done, f32[5,16,32,128]{3,2,1,0:T(8,128)S(1)} %copy-done.2), custom_call_target="tpu_custom_call" | custom-call | tf_op jit(solution)/shard_map/pack/pallas_call | solution.py:306
  5.1 3.1 %collective-permute-start = (f32[10,2,32,128]{3,2,1,0:T(8,128)}, f32[10,2,32,128]{3,2,1,0:T(8,128)S(1)}, u32[]{:S(2)}, u32[]{:S(2)}) collective-permute-start(f32[10,2,32,128]{3,2,1,0:T(8,128)} %get-tuple-element.11), channel_id=1, source_target_pairs={{0,8},{8,0},{16,24},{24,16},{1,9},{9,1},{17,25},{25,17},{2,10},{10... | collective-permute-start | bytes 983048 | tf_op jit(solution)/shard_map/ppermute | solution.py:328
  8.2 1.4 %collective-permute-start.1 = (f32[10,2,32,128]{3,2,1,0:T(8,128)}, f32[10,2,32,128]{3,2,1,0:T(8,128)}, u32[]{:S(2)}, u32[]{:S(2)}) collective-permute-start(f32[10,2,32,128]{3,2,1,0:T(8,128)} %get-tuple-element.12), channel_id=1, source_target_pairs={{8,16},{16,8},{9,17},{17,9},{10,18},{18,10},{11,19},{19,11},{12,20... | collective-permute-start | bytes 983048 | tf_op jit(solution)/shard_map/ppermute | solution.py:329
  9.6 1.5 %collective-permute-start.2 = (f32[10,16,4,128]{3,2,1,0:T(4,128)}, f32[10,16,4,128]{3,2,1,0:T(4,128)S(1)}, u32[]{:S(2)}, u32[]{:S(2)}) collective-permute-start(f32[10,16,4,128]{3,2,1,0:T(4,128)} %get-tuple-element.13), channel_id=1, source_target_pairs={{0,4},{4,0},{1,5},{5,1},{2,6},{6,2},{3,7},{7,3},{8,12},{12,8},{9,1... | collective-permute-start | bytes 983048 | tf_op jit(solution)/shard_map/ppermute | solution.py:326
  11.1 0.0 collective-permute-start.3
  11.1 0.7 %collective-permute-start.4 = (f32[10,2,8,128]{3,2,1,0:T(8,128)S(1)}, f32[10,2,8,128]{3,2,1,0:T(8,128)S(1)}, u32[]{:S(2)}, u32[]{:S(2)}) collective-permute-start(f32[10,2,8,128]{3,2,1,0:T(8,128)S(1)} %get-tuple-element.14.ax_s), channel_id=1, source_target_pairs={{1,2},{2,1},{5,6},{6,5},{9,10},{10,9},{13,14},{14,13},{17,18},{18,... | collective-permute-start | bytes 245768 | tf_op jit(solution)/shard_map/ppermute | solution.py:325
  11.7 0.0 copy-done.4
  11.7 0.1 fusion.4
  11.8 0.1 reshape.26
  11.9 0.1 reshape.27
  12.0 0.0 copy-done.5
  12.0 0.1 reshape.28
  12.1 0.0 copy-done.6
  12.1 0.1 reshape.29
  12.2 0.0 copy-done.7
  12.2 0.1 reshape.30
  12.3 0.1 concatenate.3
  12.4 0.0 collective-permute-done.3.ax_a
  12.4 0.0 collective-permute-done.4.ax_b
  12.4 3.7 %collective-permute-done.rad_a = f32[10,2,32,128]{3,2,1,0:T(8,128)S(1)} collective-permute-done((f32[10,2,32,128]{3,2,1,0:T(8,128)}, f32[10,2,32,128]{3,2,1,0:T(8,128)S(1)}, u32[]{:S(2)}, u32[]{:S(2)}) %collective-permute-start) | collective-permute-done | bytes 327712 | tf_op jit(solution)/shard_map/ppermute | solution.py:328
  16.1 0.0 collective-permute-done.1.rad_b
  16.1 2.9 %collective-permute-done.2.azi_l.azi_r = f32[10,16,4,128]{3,2,1,0:T(4,128)S(1)} collective-permute-done((f32[10,16,4,128]{3,2,1,0:T(4,128)}, f32[10,16,4,128]{3,2,1,0:T(4,128)S(1)}, u32[]{:S(2)}, u32[]{:S(2)}) %collective-permute-start.2) | collective-permute-done | bytes 327712 | tf_op jit(solution)/shard_map/ppermute | solution.py:326
  18.9 0.0 copy-done.1
  18.9 0.0 copy-done.3
  18.9 13.8 %stencil.1 = (f32[16,32,128]{2,1,0:T(8,128)}, f32[32,256]{1,0:T(8,128)S(1)}) custom-call(f32[5,16,32,128]{3,2,1,0:T(8,128)S(1)} %copy-done.1, f32[5,16,32,128]{3,2,1,0:T(8,128)S(1)} %copy-done.3, f32[10,2,32,128]{3,2,1,0:T(8,128)S(1)} %collective-permute-done.rad_a, f32[10,2,32,128]{3,2,1,0:T(8,128)} %collective-permute-done.1.rad_b, ...), custom_call_target="tpu_custom_call" | custom-call | tf_op jit(solution)/shard_map/stencil/pallas_call | solution.py:351
  32.8 12.7 %all_to_all.11 = f32[32,1,256]{2,1,0:T(1,128)S(1)} all-to-all(f32[32,1,256]{2,1,0:T(1,128)S(1)} %copy.9), channel_id=1, replica_groups=mesh['rad'=4,'azi'=2,'ax'=4] {'rad','azi','ax'}, dimensions={0} | all-to-all | bytes 65536 | tf_op jit(solution)/shard_map/all_to_all | solution.py:368
  45.6 0.6 %copy.12 = f32[32,1,256]{2,0,1:T(8,128)} copy(f32[32,1,256]{2,1,0:T(1,128)S(1)} %all_to_all.11) | data formatting | bytes 65536
  46.2 1.8 %blocks.1 = (f32[1,2,8]{2,1,0:T(2,128)}, f32[1,1,1]{2,1,0:T(1,128)}) custom-call(f32[32,256]{1,0:T(8,128)} %bitcast.10), custom_call_target="tpu_custom_call" | custom-call | tf_op jit(solution)/shard_map/blocks/pallas_call | solution.py:370
  (4 shorter events, 0.0 us)
Async XLA Ops:
  0.6 1.3 %copy-start = (f32[5,16,32,128]{3,2,1,0:T(8,128)S(1)}, f32[5,16,32,128]{3,2,1,0:T(8,128)}, u32[]{:S(2)}) copy-start(f32[5,16,32,128]{3,2,1,0:T(8,128)} %prim.3) | copy-start | bytes 3932164
  1.9 1.3 %copy-start.2 = (f32[5,16,32,128]{3,2,1,0:T(8,128)S(1)}, f32[5,16,32,128]{3,2,1,0:T(8,128)}, u32[]{:S(2)}) copy-start(f32[5,16,32,128]{3,2,1,0:T(8,128)} %adj.3) | copy-start | bytes 3932164
  3.3 8.5 %copy-start.4 = (s32[1,2,8,6]{2,1,3,0:T(2,128)S(1)}, s32[1,2,8,6]{2,1,3,0:T(2,128)}, u32[]{:S(2)}) copy-start(s32[1,2,8,6]{2,1,3,0:T(2,128)} %param.11) | copy-start | bytes 1156
  3.3 8.7 %copy-start.5 = (s32[1,2,8]{2,1,0:T(2,128)S(1)}, s32[1,2,8]{2,1,0:T(2,128)}, u32[]{:S(2)}) copy-start(s32[1,2,8]{2,1,0:T(2,128)} %param.8) | copy-start | bytes 196
  3.3 8.8 %copy-start.6 = (s32[1,2,8]{2,1,0:T(2,128)S(1)}, s32[1,2,8]{2,1,0:T(2,128)}, u32[]{:S(2)}) copy-start(s32[1,2,8]{2,1,0:T(2,128)} %param.9) | copy-start | bytes 196
  3.3 8.9 %copy-start.7 = (s32[1,2,8]{2,1,0:T(2,128)S(1)}, s32[1,2,8]{2,1,0:T(2,128)}, u32[]{:S(2)}) copy-start(s32[1,2,8]{2,1,0:T(2,128)} %param.10) | copy-start | bytes 196
  3.3 15.7 %copy-start.1 = (f32[5,16,32,128]{3,2,1,0:T(8,128)S(1)}, f32[5,16,32,128]{3,2,1,0:T(8,128)}, u32[]{:S(2)}) copy-start(f32[5,16,32,128]{3,2,1,0:T(8,128)} %prim.3) | copy-start | bytes 3932164
  3.3 15.7 %copy-start.3 = (f32[5,16,32,128]{3,2,1,0:T(8,128)S(1)}, f32[5,16,32,128]{3,2,1,0:T(8,128)}, u32[]{:S(2)}) copy-start(f32[5,16,32,128]{3,2,1,0:T(8,128)} %adj.3) | copy-start | bytes 3932164
  5.1 11.0 %collective-permute-start = (f32[10,2,32,128]{3,2,1,0:T(8,128)}, f32[10,2,32,128]{3,2,1,0:T(8,128)S(1)}, u32[]{:S(2)}, u32[]{:S(2)}) collective-permute-start(f32[10,2,32,128]{3,2,1,0:T(8,128)} %get-tuple-element.11), channel_id=1, source_target_pairs={{0,8},{8,0},{16,24},{24,16},{1,9},{9,1},{17,25},{25,17},{2,10},{10... | collective-permute-start | bytes 983048 | tf_op jit(solution)/shard_map/ppermute | solution.py:328
  8.2 7.9 %collective-permute-start.1 = (f32[10,2,32,128]{3,2,1,0:T(8,128)}, f32[10,2,32,128]{3,2,1,0:T(8,128)}, u32[]{:S(2)}, u32[]{:S(2)}) collective-permute-start(f32[10,2,32,128]{3,2,1,0:T(8,128)} %get-tuple-element.12), channel_id=1, source_target_pairs={{8,16},{16,8},{9,17},{17,9},{10,18},{18,10},{11,19},{19,11},{12,20... | collective-permute-start | bytes 983048 | tf_op jit(solution)/shard_map/ppermute | solution.py:329
  9.6 9.4 %collective-permute-start.2 = (f32[10,16,4,128]{3,2,1,0:T(4,128)}, f32[10,16,4,128]{3,2,1,0:T(4,128)S(1)}, u32[]{:S(2)}, u32[]{:S(2)}) collective-permute-start(f32[10,16,4,128]{3,2,1,0:T(4,128)} %get-tuple-element.13), channel_id=1, source_target_pairs={{0,4},{4,0},{1,5},{5,1},{2,6},{6,2},{3,7},{7,3},{8,12},{12,8},{9,1... | collective-permute-start | bytes 983048 | tf_op jit(solution)/shard_map/ppermute | solution.py:326
  11.1 1.3 %collective-permute-start.3 = (f32[10,2,8,128]{3,2,1,0:T(8,128)S(1)}, f32[10,2,8,128]{3,2,1,0:T(8,128)S(1)}, u32[]{:S(2)}, u32[]{:S(2)}) collective-permute-start(f32[10,2,8,128]{3,2,1,0:T(8,128)S(1)} %get-tuple-element.14.ax_s), channel_id=1, source_target_pairs={{0,1},{1,0},{2,3},{3,2},{4,5},{5,4},{6,7},{7,6},{8,9},{9,8},{10,11... | collective-permute-start | bytes 245768 | tf_op jit(solution)/shard_map/ppermute | solution.py:324
  11.1 1.3 %collective-permute-start.4 = (f32[10,2,8,128]{3,2,1,0:T(8,128)S(1)}, f32[10,2,8,128]{3,2,1,0:T(8,128)S(1)}, u32[]{:S(2)}, u32[]{:S(2)}) collective-permute-start(f32[10,2,8,128]{3,2,1,0:T(8,128)S(1)} %get-tuple-element.14.ax_s), channel_id=1, source_target_pairs={{1,2},{2,1},{5,6},{6,5},{9,10},{10,9},{13,14},{14,13},{17,18},{18,... | collective-permute-start | bytes 245768 | tf_op jit(solution)/shard_map/ppermute | solution.py:325

commit v2 on v1

v2 whole, which is shorter than its diff:
```python
import functools

import jax
import jax.numpy as jnp
from jax import lax
from jax.experimental import pallas as pl
from jax.experimental.pallas import tpu as pltpu
from jax.sharding import PartitionSpec as P

BLK = 16
F = 5
AXES = ("rad", "azi", "ax")


def line_pairs(count, first):
    pairs = []
    for i in range(first, count - 1, 2):
        pairs += [(i, i + 1), (i + 1, i)]
    return pairs


def ring(count, step):
    return [(i, (i + step) % count) for i in range(count)]


def edge_kernel(dims, prim, adj, rad_a, rad_b, azi_s, sems):
    nr, na, nx = dims
    odd = lax.rem(lax.axis_index("rad"), 2)
    first = jnp.where(odd == 0, nr - 2, 0)
    copies = []
    for t, src in enumerate((prim, adj)):
        rows = pl.ds(t * F, F)
        for i, (a, b) in enumerate(
            (
                (src.at[:, pl.ds(first, 2)], rad_a.at[rows]),
                (src.at[:, pl.ds(nr - 2 - first, 2)], rad_b.at[rows]),
                (src.at[:, :, pl.ds(0, 2)], azi_s.at[rows, :, pl.ds(0, 2)]),
                (src.at[:, :, pl.ds(na - 2, 2)], azi_s.at[rows, :, pl.ds(2, 2)]),
            )
        ):
            copies.append(pltpu.make_async_copy(a, b, sems.at[t, i]))
    for c in copies:
        c.start()
    for c in copies:
        c.wait()


def lane_kernel(dims, prim, adj, ax_s):
    nr, na, nx = dims
    slot = lax.broadcasted_iota(jnp.int32, (8, nx), 1) >> 2
    tiles = na // 8
    per = nx // 4
    for t, src in enumerate((prim, adj)):
        for f in range(F):
            for h in range(nr * tiles // per):
                acc = jnp.zeros((8, nx), jnp.float32)
                for j in range(per):
                    k = h * per + j
                    x = src[f, k // tiles, pl.ds(8 * (k % tiles), 8), :]
                    acc = jnp.where(slot == j, pltpu.roll(x, (4 * j + 2) % nx, 1), acc)
                ax_s[t * F + f, h] = acc


def flux(s, along):
    inv = 1.0 / s[0]
    v = s[1 + along] * inv
    kin = (s[1] * s[1] + s[2] * s[2] + s[3] * s[3]) * inv
    p = 0.4 * s[4] - 0.2 * kin
    out = [s[1 + along], s[1] * v, s[2] * v, s[3] * v, (s[4] + p) * v]
    out[1 + along] = out[1 + along] + p
    return out


def face(m1, c, p1, p2):
    return 7.0 * (c + p1) - (m1 + p2)


def split3(x):
    hi = x.astype(jnp.bfloat16)
    x = x - hi.astype(jnp.float32)
    mid = x.astype(jnp.bfloat16)
    x = x - mid.astype(jnp.float32)
    return hi, mid, x.astype(jnp.bfloat16)


def taps(rows, cols, table):
    out = jnp.zeros(rows.shape, jnp.float32)
    for step, value in table.items():
        out = jnp.where(rows - cols == step, value, out)
    return out


UPPER = {-1: -1.0, 0: 7.0, 1: 7.0, 2: -1.0}
LOWER = {-2: -1.0, -1: 7.0, 0: 7.0, 1: -1.0}
FOURTH = {-2: 1.0, -1: -4.0, 0: 6.0, 1: -4.0, 2: 1.0}


def axial_kernel(dims, n_ax, prim, adj, ax_a, ax_b, bw, got, lhs, rhs, sums):
    nr, na, nx = dims
    i_ax = lax.axis_index("ax")
    even_ax = lax.rem(i_ax, 2) == 0
    lane = lax.broadcasted_iota(jnp.int32, (8, nx), 1)
    part = lane & 3
    slot = lane >> 2
    tiles = na // 8
    per = nx // 4
    halves = nr * tiles // per
    size = nr * na

    i = lax.broadcasted_iota(jnp.int32, (nx, nx), 0)
    c = lax.broadcasted_iota(jnp.int32, (nx, nx), 1)
    p = i & 3
    halo = jnp.where(p < 2, p - 2, p - 2 + nx)
    for n, table in enumerate((UPPER, LOWER, FOURTH)):
        own = taps(i, c, table).astype(jnp.bfloat16)
        far = taps(halo, c, table).astype(jnp.bfloat16)
        for k in range(3):
            rhs[pl.ds(2 * k * nx, nx), pl.ds(n * nx, nx)] = own
            rhs[pl.ds((2 * k + 1) * nx, nx), pl.ds(n * nx, nx)] = far

    for h in range(halves):
        for f in range(2 * F):
            a, b = ax_a[f, h], ax_b[f, h]
            g = jnp.where(part < 2, jnp.where(even_ax, b, a), jnp.where(even_ax, a, b))
            for k, x in enumerate(split3(g)):
                got[k, f, h] = x.astype(jnp.float32)

    def build(t, src, f):
        g0 = t * F + f
        for r in range(nr):
            h, j0 = r * tiles // per, r * tiles % per
            rows = pl.ds(pl.multiple_of(g0 * size, size) + r * na, na)
            for k, x in enumerate(split3(src[f, r])):
                lhs[rows, pl.ds(2 * k * nx, nx)] = x
                g = got[k, g0, h]
                y = [jnp.where(slot == j0 + a, g, 0.0) for a in range(tiles)]
                lhs[rows, pl.ds((2 * k + 1) * nx, nx)] = jnp.concatenate(y, axis=0).astype(jnp.bfloat16)

    for t, src in enumerate((prim, adj)):
        lax.fori_loop(0, F, lambda f, c, t=t, src=src: (build(t, src, f), c)[1], 0)
    sums[...] = jnp.dot(
        lhs[0:F * size, :], rhs[:, 0:2 * nx], preferred_element_type=jnp.float32
    )
    bw[F:2 * F] = jnp.dot(
        lhs[F * size:2 * F * size, :], rhs[:, 2 * nx:3 * nx], preferred_element_type=jnp.float32
    ).reshape(F, nr, na, nx)

    def body(r, carry):
        for a in range(tiles):
            at = [pl.ds(f * size + pl.multiple_of(r * na, na) + 8 * a, 8) for f in range(F)]
            up = flux([sums[q, 0:nx] for q in at], 2)
            low = flux([sums[q, nx:2 * nx] for q in at], 2)
            for f in range(F):
                bw[f, r, pl.ds(8 * a, 8), :] = up[f] - low[f]
        return carry

    lax.fori_loop(0, nr, body, 0)


def main_kernel(
    dims, prim, adj, bw, rad_a, rad_b, azi_l, azi_r, row, ind, send, far, low, top, frad, fazi
):
    nr, na, nx = dims
    odd = lax.rem(lax.axis_index("rad"), 2)
    tiles = na // 8
    last = 8 * (tiles - 1)
    lane = lax.broadcasted_iota(jnp.int32, (8, nx), 1)
    for f in range(2 * F):
        for i in range(2):
            a, b = rad_a[f, i], rad_b[f, i]
            far[f, i] = jnp.where(odd == 0, b, a)
            far[f, 2 + i] = jnp.where(odd == 0, a, b)

    def edges(r, carry):
        for t, src in enumerate((prim, adj)):
            for f in range(F):
                g = t * F + f
                low[g, r, 14:16, :] = azi_l[g, r, 2:4, :]
                low[g, r, 16:24, :] = src[f, r, 0:8, :]
                top[g, r, 0:8, :] = src[f, r, last:last + 8, :]
                top[g, r, 8:10, :] = azi_r[g, r, 0:2, :]
        return carry

    lax.fori_loop(0, nr, edges, 0)

    def cell(g, r, a, dr=0, da=0):
        if isinstance(r, int):
            if r + dr < 0:
                return far[g, 2 + r + dr, pl.ds(8 * a, 8), :]
            if r + dr >= nr:
                return far[g, 2 + r + dr - nr, pl.ds(8 * a, 8), :]
        if da < 0 and a == 0:
            return low[g, r, pl.ds(16 + da, 8), :]
        if da > 0 and a == tiles - 1:
            return top[g, r, pl.ds(da, 8), :]
        src = (prim, adj)[g // F]
        return src[g % F, r + dr, pl.ds(8 * a + da, 8), :]

    def rad_flux(r, a):
        return flux([face(*(cell(f, r, a, dr=o) for o in (-1, 0, 1, 2))) for f in range(F)], 0)

    def azi_flux(r, a):
        return flux([face(*(cell(f, r, a, da=o) for o in (-1, 0, 1, 2))) for f in range(F)], 1)

    def low_flux(r):
        return flux([face(*(low[f, r, pl.ds(8 + o, 8), :] for o in (-1, 0, 1, 2))) for f in range(F)], 1)

    for a in range(tiles):
        for f, x in enumerate(rad_flux(-1, a)):
            frad[f, a] = x

    def plane(r, sums):
        for f, x in enumerate(low_flux(r)):
            fazi[f, 0:8, :] = x
        for a in range(tiles):
            for f, x in enumerate(azi_flux(r, a)):
                fazi[f, pl.ds(8 + 8 * a, 8), :] = x
        out = []
        for a in range(tiles):
            mine = pl.ds(8 * a, 8)
            up = rad_flux(r, a)
            total = None
            for f in range(F):
                bal = bw[f, r, mine, :] + (up[f] - frad[f, a])
                frad[f, a] = up[f]
                bal = bal + (fazi[f, pl.ds(8 * a + 8, 8), :] - fazi[f, pl.ds(8 * a + 7, 8), :])
                g = F + f
                two = (cell(g, r, a, dr=-2) + cell(g, r, a, dr=2)) + (
                    cell(g, r, a, da=-2) + cell(g, r, a, da=2)
                )
                one = (cell(g, r, a, dr=-1) + cell(g, r, a, dr=1)) + (
                    cell(g, r, a, da=-1) + cell(g, r, a, da=1)
                )
                w = (two - 4.0 * one + 12.0 * cell(g, r, a) + bw[g, r, mine, :]) * bal
                total = w if total is None else total + w
            total = jnp.abs(total) * (1.0 / 144.0)
            ind[r, mine, :] = total
            out.append(sums[a] + total)
        return tuple(out)

    sums = tuple(jnp.zeros((8, nx), jnp.float32) for _ in range(tiles))
    for r in (0, 1):
        sums = plane(r, sums)
    sums = lax.fori_loop(2, nr - 2, plane, sums)
    for r in (nr - 2, nr - 1):
        sums = plane(r, sums)

    groups = nx // BLK
    halves_a = na // BLK
    per_tile = BLK // 8
    means = jnp.zeros((8, nx), jnp.float32)
    for b in range(halves_a):
        t = sums[b * per_tile]
        for i in range(1, per_tile):
            t = t + sums[b * per_tile + i]
        t = jnp.broadcast_to(jnp.sum(t, axis=0, keepdims=True), (8, nx))
        for sh in (8, 4, 2, 1):
            t = t + pltpu.roll(t, nx - sh, 1)
        t = jnp.take_along_axis(t, (lane % groups) * BLK, axis=1)
        means = jnp.where(lane // groups == b, t, means)
    means = means * (1.0 / BLK**3)
    head = jnp.broadcast_to(row[:, 0:nx], (8, nx))
    head = jnp.where(lane < groups * halves_a, means, head)
    tail = jnp.broadcast_to(row[:, nx:2 * nx], (8, nx))
    for d in range(send.shape[0] // 8):
        send[pl.ds(8 * d, 8), 0:nx] = head
        send[pl.ds(8 * d, 8), nx:2 * nx] = tail


def final_kernel(n_loc, per_ax, data, cost, load):
    n_dev = data.shape[0]
    nx = data.shape[1] // 2
    me = (lax.axis_index("rad") * lax.axis_size("azi") + lax.axis_index("azi")) * lax.axis_size(
        "ax"
    ) + lax.axis_index("ax")
    lane = lax.broadcasted_iota(jnp.int32, (8, nx), 1)
    sub = lax.broadcasted_iota(jnp.int32, (8, nx), 0)

    def group(g, carry):
        acc_load, acc_cost = carry
        rows = pl.ds(pl.multiple_of(8 * g, 8), 8)
        head = data[rows, 0:nx]
        tail = data[rows, nx:2 * nx]
        spot = head.astype(jnp.int32)
        dev = spot // n_loc
        pos = spot - dev * n_loc

        def look(d8, acc):
            table = data[pl.ds(pl.multiple_of(8 * d8, 8), 8), 0:nx]
            for i in range(8):
                t = jnp.broadcast_to(table[i:i + 1, :], (8, nx))
                v = jnp.take_along_axis(t, pos, axis=1)
                acc = jnp.where(dev == d8 * 8 + i, v, acc)
            return acc

        val = lax.fori_loop(0, n_dev // 8, look, jnp.zeros((8, nx), jnp.float32), unroll=n_dev <= 32)
        beside = None
        for j in range(6):
            x = pltpu.roll(val, nx - n_loc * (1 + j), 1)
            beside = x if beside is None else beside + x
        smooth = 0.5 * head + (0.5 / 6.0) * beside
        refine = pltpu.roll(head, nx - 7 * n_loc, 1)
        owner = tail.astype(jnp.int32)
        weight = pltpu.roll(tail, nx - n_loc, 1)
        home = sub + 8 * g
        c = smooth * (1.0 + 7.0 * refine) + jnp.where(owner != home, 0.25 * weight, 0.0)
        ok = lane < n_loc
        acc_load = acc_load + jnp.where(ok & (owner == me), c, 0.0)
        acc_cost = acc_cost + jnp.where(home == me, c, 0.0)
        return acc_load, acc_cost

    zero = jnp.zeros((8, nx), jnp.float32)
    acc_load, acc_cost = lax.fori_loop(0, n_dev // 8, group, (zero, zero), unroll=n_dev <= 32)
    own = jnp.sum(acc_cost, axis=0, keepdims=True)
    for b in range(n_loc // per_ax):
        x = own if b == 0 else pltpu.roll(own, nx - b * per_ax, 1)
        cost[0, pl.ds(b, 1), :] = x[:, 0:per_ax]
    total = jnp.sum(jnp.sum(acc_load, axis=0, keepdims=True), axis=1, keepdims=True) * (1.0 / n_loc)
    load[0] = total


def on_device(primal, adjoint, refine_flag, owner_map, migrate_weight, neighbor_list):
    _, nr, na, nx = primal.shape
    dims = (nr, na, nx)
    n_rad, n_azi, n_ax = (lax.axis_size(a) for a in AXES)
    n_dev = n_rad * n_azi * n_ax
    tiles = na // 8
    halves = nr * tiles // (nx // 4)
    f32 = functools.partial(jax.ShapeDtypeStruct, dtype=jnp.float32)
    anyspec = pl.BlockSpec(memory_space=pl.ANY)
    hbm = pl.BlockSpec(memory_space=pltpu.HBM)
    vmem = pl.BlockSpec(memory_space=pltpu.VMEM)

    rad_a, rad_b, azi_s = pl.pallas_call(
        functools.partial(edge_kernel, dims),
        out_shape=(f32((2 * F, 2, na, nx)), f32((2 * F, 2, na, nx)), f32((2 * F, nr, 4, nx))),
        in_specs=[hbm, hbm],
        out_specs=(vmem, vmem, vmem),
        scratch_shapes=[pltpu.SemaphoreType.DMA((2, 4))],
        name="edges",
    )(primal, adjoint)
    ax_s = pl.pallas_call(
        functools.partial(lane_kernel, dims),
        out_shape=f32((2 * F, halves, 8, nx)),
        in_specs=[vmem, vmem],
        out_specs=vmem,
        compiler_params=pltpu.CompilerParams(vmem_limit_bytes=16 << 20),
        name="lanes",
    )(primal, adjoint)

    ax_a = lax.ppermute(ax_s, "ax", line_pairs(n_ax, 0))
    ax_b = lax.ppermute(ax_s, "ax", line_pairs(n_ax, 1))
    azi_l = lax.ppermute(azi_s, "azi", ring(n_azi, 1))
    azi_r = azi_l if n_azi == 2 else lax.ppermute(azi_s, "azi", ring(n_azi, -1))
    rad_a = lax.ppermute(rad_a, "rad", line_pairs(n_rad, 0))
    rad_b = lax.ppermute(rad_b, "rad", line_pairs(n_rad, 1))

    per_rad, per_azi, per_ax = nr // BLK, na // BLK, nx // BLK
    n_loc = per_rad * per_azi * per_ax
    blocks_azi, blocks_ax = per_azi * n_azi, per_ax * n_ax
    b_rad = neighbor_list // (blocks_azi * blocks_ax)
    b_azi = neighbor_list // blocks_ax % blocks_azi
    b_ax = neighbor_list % blocks_ax
    device = (b_rad // per_rad * n_azi + b_azi // per_azi) * n_ax + b_ax // per_ax
    local = (b_rad % per_rad * per_azi + b_azi % per_azi) * per_ax + b_ax % per_ax
    spot = (device * n_loc + local).reshape(n_loc, 6).T.reshape(-1)
    row = jnp.concatenate(
        [
            jnp.zeros((n_loc,), jnp.int32),
            spot,
            refine_flag.reshape(-1),
            owner_map.reshape(-1),
            migrate_weight.reshape(-1),
        ]
    ).astype(jnp.float32)
    row = jnp.pad(row, (0, 2 * nx - row.shape[0]))[None]

    bw = pl.pallas_call(
        functools.partial(axial_kernel, dims, n_ax),
        out_shape=f32((2 * F, nr, na, nx)),
        in_specs=[vmem] * 4,
        out_specs=vmem,
        scratch_shapes=[
            pltpu.VMEM((3, 2 * F, halves, 8, nx), jnp.float32),
            pltpu.VMEM((2 * F * nr * na, 6 * nx), jnp.bfloat16),
            pltpu.VMEM((6 * nx, 3 * nx), jnp.bfloat16),
            pltpu.VMEM((F * nr * na, 2 * nx), jnp.float32),
        ],
        compiler_params=pltpu.CompilerParams(vmem_limit_bytes=40 << 20),
        name="axial",
    )(primal, adjoint, ax_a, ax_b)

    indicator, send = pl.pallas_call(
        functools.partial(main_kernel, dims),
        out_shape=(f32(dims), f32((n_dev, 2 * nx))),
        in_specs=[vmem] * 8,
        out_specs=(vmem, vmem),
        scratch_shapes=[
            pltpu.VMEM((2 * F, 4, na, nx), jnp.float32),
            pltpu.VMEM((2 * F, nr, 24, nx), jnp.float32),
            pltpu.VMEM((2 * F, nr, 16, nx), jnp.float32),
            pltpu.VMEM((F, tiles, 8, nx), jnp.float32),
            pltpu.VMEM((F, 8 + na, nx), jnp.float32),
        ],
        compiler_params=pltpu.CompilerParams(vmem_limit_bytes=32 << 20),
        name="stencil",
    )(primal, adjoint, bw, rad_a, rad_b, azi_l, azi_r, row)

    data = lax.all_to_all(send, AXES, 0, 0, tiled=True)

    cost, load = pl.pallas_call(
        functools.partial(final_kernel, n_loc, per_ax),
        out_shape=(f32((per_rad, per_azi, per_ax)), f32((1, 1, 1))),
        in_specs=[vmem],
        out_specs=(vmem, vmem),
        name="blocks",
    )(data)
    return indicator, cost, load


def solution(mesh):
    spec = P("rad", "azi", "ax")
    field = P(None, "rad", "azi", "ax")
    return jax.shard_map(
        on_device,
        mesh=mesh,
        in_specs=(field, field, spec, spec, spec, P("rad", "azi", "ax", None)),
        out_specs=(spec, spec, spec),
        check_vma=False,
    )
```

time: 48.2 us -> 39.5 us (0.82)
  waiting for transfers between devices: 6.57 us -> 0.32 us
  Pallas kernels: 17.4 us -> 14 us
  starting transfers between devices: 6.66 us -> 9.65 us
  local copies, waits for them, and re-layouts: 3.77 us -> 1.16 us
  blocking collectives: 12.7 us -> 13.3 us
    ppermute x1, waiting for transfers between devices: 3.7 us -> 0.01 us  [on_device(): rad_a = lax.ppermute(rad_a, 'rad', line_pairs(n_rad, 0))]
    pallas_call x2 -> x4, Pallas kernels: 15.6 us -> 12.3 us  [the longest x1 4.83 us: on_device(): pl.pallas_call(functools.partial(main_kernel, dims), out_shape=(f32(dims)...]
    ppermute x1, starting transfers between devices: 0.01 us -> 2.91 us  [on_device(): ax_a = lax.ppermute(ax_s, 'ax', line_pairs(n_ax, 0))]
    ppermute x1, waiting for transfers between devices: 2.86 us -> 0.01 us  [on_device(): azi_l = lax.ppermute(azi_s, 'azi', ring(n_azi, 1))]
    unnamed x17 -> x13, local copies, waits for them, and re-layouts: 3.25 us -> 0.63 us
    all_to_all x1, blocking collectives: 12.7 us -> 13.3 us  [on_device(): data = lax.all_to_all(send, AXES, 0, 0, tiled=True)]
  transfers between devices with their start and end apart: 5 -> 5, of which waited for: 2 -> 1; matrix products, arithmetic and copies ran while one was open for 1% -> 2% of each run, Pallas kernels for 0% -> 13%
where the time goes in v2:
time: 39.5 us; the launch traced here: 39.3 us
  Pallas kernels  14 us (35%)
  blocking collectives  13.3 us (34%)
  starting transfers between devices  9.65 us (24%)
  local copies, waits for them, and re-layouts  1.16 us (3%)
  between operations  0.72 us (2%)
    all_to_all x1, blocking collectives, on_device(): data = lax.all_to_all(send, AXES, 0, 0, tiled=True)  13.3 us
    pallas_call x1, Pallas kernels, on_device(): pl.pallas_call(functools.partial(main_kernel, dims), out_shape=(f32(dims)...  4.83 us
    pallas_call x1, Pallas kernels, on_device(): pl.pallas_call(functools.partial(axial_kernel, dims, n_ax), out_shape=f32...  4.25 us
    ppermute x1, starting transfers between devices, on_device(): rad_a = lax.ppermute(rad_a, 'rad', line_pairs(n_rad, 0))  3.09 us
    ppermute x1, starting transfers between devices, on_device(): ax_a = lax.ppermute(ax_s, 'ax', line_pairs(n_ax, 0))  2.91 us
    pallas_call x1, Pallas kernels, on_device(): pl.pallas_call(functools.partial(edge_kernel, dims), out_shape=(f32((2 *...  2.45 us
    pallas_call x1, Pallas kernels, on_device(): pl.pallas_call(functools.partial(final_kernel, n_loc, per_ax), out_shape=...  1.76 us
    ppermute x1, starting transfers between devices, on_device(): azi_l = lax.ppermute(azi_s, 'azi', ring(n_azi, 1))  1.58 us
  transfers between devices with their start and end apart: 5, of which 1 were waited for; matrix products, arithmetic and copies ran while one was open for 2% of the time, Pallas kernels for 13%

profile of v2, /device:TPU:0, one launch (start us, length us, event | category | flops | bytes accessed | tf_op | source)
XLA Modules:
  0.0 39.3 jit_solution(14582848870406057614)
XLA Ops:
  0.6 0.0 copy-start.1
  0.6 0.0 copy-start
  0.6 2.5 %edges.1 = (f32[10,2,32,128]{3,2,1,0:T(8,128)}, f32[10,2,32,128]{3,2,1,0:T(8,128)}, f32[10,16,4,128]{3,2,1,0:T(4,128)}) custom-call(f32[5,16,32,128]{3,2,1,0:T(8,128)} %prim.7, f32[5,16,32,128]{3,2,1,0:T(8,128)} %adj.7), custom_call_target="tpu_custom_call" | custom-call | tf_op jit(solution)/shard_map/edges/pallas_call | solution.py:334
  3.1 3.1 %collective-permute-start.2 = (f32[10,2,32,128]{3,2,1,0:T(8,128)}, f32[10,2,32,128]{3,2,1,0:T(8,128)S(1)}, u32[]{:S(2)}, u32[]{:S(2)}) collective-permute-start(f32[10,2,32,128]{3,2,1,0:T(8,128)} %get-tuple-element.10), channel_id=1, source_target_pairs={{0,8},{8,0},{16,24},{24,16},{1,9},{9,1},{17,25},{25,17},{2,10},{10... | collective-permute-start | bytes 983048 | tf_op jit(solution)/shard_map/ppermute | solution.py:355
  6.2 1.4 %collective-permute-start.3 = (f32[10,2,32,128]{3,2,1,0:T(8,128)}, f32[10,2,32,128]{3,2,1,0:T(8,128)}, u32[]{:S(2)}, u32[]{:S(2)}) collective-permute-start(f32[10,2,32,128]{3,2,1,0:T(8,128)} %get-tuple-element.11), channel_id=1, source_target_pairs={{8,16},{16,8},{9,17},{17,9},{10,18},{18,10},{11,19},{19,11},{12,20... | collective-permute-start | bytes 983048 | tf_op jit(solution)/shard_map/ppermute | solution.py:356
  7.6 0.0 copy-start.2
  7.6 0.0 copy-start.3
  7.6 0.0 copy-start.4
  7.6 0.0 copy-start.5
  7.6 1.6 %collective-permute-start.4 = (f32[10,16,4,128]{3,2,1,0:T(4,128)}, f32[10,16,4,128]{3,2,1,0:T(4,128)S(1)}, u32[]{:S(2)}, u32[]{:S(2)}) collective-permute-start(f32[10,16,4,128]{3,2,1,0:T(4,128)} %get-tuple-element.12), channel_id=1, source_target_pairs={{0,4},{4,0},{1,5},{5,1},{2,6},{6,2},{3,7},{7,3},{8,12},{12,8},{9,1... | collective-permute-start | bytes 983048 | tf_op jit(solution)/shard_map/ppermute | solution.py:353
  9.2 0.0 copy-done.1
  9.2 0.0 copy-done
  9.2 0.7 %lanes.1 = f32[10,2,8,128]{3,2,1,0:T(8,128)S(1)} custom-call(f32[5,16,32,128]{3,2,1,0:T(8,128)S(1)} %copy-done, f32[5,16,32,128]{3,2,1,0:T(8,128)S(1)} %copy-done.1), custom_call_target="tpu_custom_call" | custom-call | tf_op jit(solution)/shard_map/lanes/pallas_call | solution.py:342
  9.9 0.7 %collective-permute-start.1 = (f32[10,2,8,128]{3,2,1,0:T(8,128)S(1)}, f32[10,2,8,128]{3,2,1,0:T(8,128)S(1)}, u32[]{:S(2)}, u32[]{:S(2)}) collective-permute-start(f32[10,2,8,128]{3,2,1,0:T(8,128)S(1)} %lanes.1), channel_id=1, source_target_pairs={{1,2},{2,1},{5,6},{6,5},{9,10},{10,9},{13,14},{14,13},{17,18},{18,... | collective-permute-start | bytes 245768 | tf_op jit(solution)/shard_map/ppermute | solution.py:352
  10.6 2.9 %collective-permute-start = (f32[10,2,8,128]{3,2,1,0:T(8,128)S(1)}, f32[10,2,8,128]{3,2,1,0:T(8,128)S(1)}, u32[]{:S(2)}, u32[]{:S(2)}) collective-permute-start(f32[10,2,8,128]{3,2,1,0:T(8,128)S(1)} %lanes.1), channel_id=1, source_target_pairs={{0,1},{1,0},{2,3},{3,2},{4,5},{5,4},{6,7},{7,6},{8,9},{9,8},{10,11... | collective-permute-start | bytes 245768 | tf_op jit(solution)/shard_map/ppermute | solution.py:351
  13.5 0.0 copy-done.2
  13.5 0.1 fusion.4
  13.6 0.0 copy-done.3
  13.6 0.1 reshape.28
  13.7 0.0 copy-done.4
  13.7 0.1 reshape.29
  13.8 0.0 copy-done.5
  13.8 0.1 reshape.30
  13.9 0.1 reshape.26
  14.0 0.1 reshape.27
  14.0 0.1 concatenate.3
  14.1 0.0 collective-permute-done.1.ax_b
  14.1 0.3 collective-permute-done.ax_a
  14.4 4.3 %axial.1.bw = f32[10,16,32,128]{3,2,1,0:T(8,128)S(1)} custom-call(f32[5,16,32,128]{3,2,1,0:T(8,128)S(1)} %copy-done, f32[5,16,32,128]{3,2,1,0:T(8,128)S(1)} %copy-done.1, f32[10,2,8,128]{3,2,1,0:T(8,128)S(1)} %collective-permute-done.ax_a, f32[10,2,8,128]{3,2,1,0:T(8,128)S(1)} %collective-permute-done.1.ax_b), custom_call_target="tpu_custom_call" | custom-call | tf_op jit(solution)/shard_map/axial/pallas_call | solution.py:378
  18.7 0.0 collective-permute-done.2.rad_a
  18.7 0.0 collective-permute-done.3.rad_b
  18.7 0.0 collective-permute-done.4.azi_l.azi_r
  18.7 4.8 %stencil.1 = (f32[16,32,128]{2,1,0:T(8,128)}, f32[32,256]{1,0:T(8,128)S(1)}) custom-call(f32[5,16,32,128]{3,2,1,0:T(8,128)S(1)} %copy-done, f32[5,16,32,128]{3,2,1,0:T(8,128)S(1)} %copy-done.1, f32[10,16,32,128]{3,2,1,0:T(8,128)S(1)} %axial.1.bw, f32[10,2,32,128]{3,2,1,0:T(8,128)S(1)} %collective-permute-done.2.rad_a, ...), custom_call_target="tpu_custom_call" | custom-call | tf_op jit(solution)/shard_map/stencil/pallas_call | solution.py:393
  23.6 13.3 %all_to_all.11 = f32[32,1,256]{2,1,0:T(1,128)S(1)} all-to-all(f32[32,1,256]{2,1,0:T(1,128)S(1)} %copy.9), channel_id=1, replica_groups=mesh['rad'=4,'azi'=2,'ax'=4] {'rad','azi','ax'}, dimensions={0} | all-to-all | bytes 65536 | tf_op jit(solution)/shard_map/all_to_all | solution.py:409
  36.9 0.6 %copy.12 = f32[32,1,256]{2,0,1:T(8,128)} copy(f32[32,1,256]{2,1,0:T(1,128)S(1)} %all_to_all.11) | data formatting | bytes 65536
  37.5 1.8 %blocks.1 = (f32[1,2,8]{2,1,0:T(2,128)}, f32[1,1,1]{2,1,0:T(1,128)}) custom-call(f32[32,256]{1,0:T(8,128)} %bitcast.10), custom_call_target="tpu_custom_call" | custom-call | tf_op jit(solution)/shard_map/blocks/pallas_call | solution.py:411
  (4 shorter events, 0.0 us)
Async XLA Ops:
  0.6 8.6 %copy-start.1 = (f32[5,16,32,128]{3,2,1,0:T(8,128)S(1)}, f32[5,16,32,128]{3,2,1,0:T(8,128)}, u32[]{:S(2)}) copy-start(f32[5,16,32,128]{3,2,1,0:T(8,128)} %adj.7) | copy-start | bytes 3932164
  0.6 8.6 %copy-start = (f32[5,16,32,128]{3,2,1,0:T(8,128)S(1)}, f32[5,16,32,128]{3,2,1,0:T(8,128)}, u32[]{:S(2)}) copy-start(f32[5,16,32,128]{3,2,1,0:T(8,128)} %prim.7) | copy-start | bytes 3932164
  3.1 15.6 %collective-permute-start.2 = (f32[10,2,32,128]{3,2,1,0:T(8,128)}, f32[10,2,32,128]{3,2,1,0:T(8,128)S(1)}, u32[]{:S(2)}, u32[]{:S(2)}) collective-permute-start(f32[10,2,32,128]{3,2,1,0:T(8,128)} %get-tuple-element.10), channel_id=1, source_target_pairs={{0,8},{8,0},{16,24},{24,16},{1,9},{9,1},{17,25},{25,17},{2,10},{10... | collective-permute-start | bytes 983048 | tf_op jit(solution)/shard_map/ppermute | solution.py:355
  6.2 12.5 %collective-permute-start.3 = (f32[10,2,32,128]{3,2,1,0:T(8,128)}, f32[10,2,32,128]{3,2,1,0:T(8,128)}, u32[]{:S(2)}, u32[]{:S(2)}) collective-permute-start(f32[10,2,32,128]{3,2,1,0:T(8,128)} %get-tuple-element.11), channel_id=1, source_target_pairs={{8,16},{16,8},{9,17},{17,9},{10,18},{18,10},{11,19},{19,11},{12,20... | collective-permute-start | bytes 983048 | tf_op jit(solution)/shard_map/ppermute | solution.py:356
  7.6 5.9 %copy-start.2 = (s32[1,2,8,6]{2,1,3,0:T(2,128)S(1)}, s32[1,2,8,6]{2,1,3,0:T(2,128)}, u32[]{:S(2)}) copy-start(s32[1,2,8,6]{2,1,3,0:T(2,128)} %param.11) | copy-start | bytes 1156
  7.6 6.0 %copy-start.3 = (s32[1,2,8]{2,1,0:T(2,128)S(1)}, s32[1,2,8]{2,1,0:T(2,128)}, u32[]{:S(2)}) copy-start(s32[1,2,8]{2,1,0:T(2,128)} %param.8) | copy-start | bytes 196
  7.6 6.1 %copy-start.4 = (s32[1,2,8]{2,1,0:T(2,128)S(1)}, s32[1,2,8]{2,1,0:T(2,128)}, u32[]{:S(2)}) copy-start(s32[1,2,8]{2,1,0:T(2,128)} %param.9) | copy-start | bytes 196
  7.6 6.2 %copy-start.5 = (s32[1,2,8]{2,1,0:T(2,128)S(1)}, s32[1,2,8]{2,1,0:T(2,128)}, u32[]{:S(2)}) copy-start(s32[1,2,8]{2,1,0:T(2,128)} %param.10) | copy-start | bytes 196
  7.6 11.1 %collective-permute-start.4 = (f32[10,16,4,128]{3,2,1,0:T(4,128)}, f32[10,16,4,128]{3,2,1,0:T(4,128)S(1)}, u32[]{:S(2)}, u32[]{:S(2)}) collective-permute-start(f32[10,16,4,128]{3,2,1,0:T(4,128)} %get-tuple-element.12), channel_id=1, source_target_pairs={{0,4},{4,0},{1,5},{5,1},{2,6},{6,2},{3,7},{7,3},{8,12},{12,8},{9,1... | collective-permute-start | bytes 983048 | tf_op jit(solution)/shard_map/ppermute | solution.py:353
  9.9 4.2 %collective-permute-start.1 = (f32[10,2,8,128]{3,2,1,0:T(8,128)S(1)}, f32[10,2,8,128]{3,2,1,0:T(8,128)S(1)}, u32[]{:S(2)}, u32[]{:S(2)}) collective-permute-start(f32[10,2,8,128]{3,2,1,0:T(8,128)S(1)} %lanes.1), channel_id=1, source_target_pairs={{1,2},{2,1},{5,6},{6,5},{9,10},{10,9},{13,14},{14,13},{17,18},{18,... | collective-permute-start | bytes 245768 | tf_op jit(solution)/shard_map/ppermute | solution.py:352
  10.6 3.8 %collective-permute-start = (f32[10,2,8,128]{3,2,1,0:T(8,128)S(1)}, f32[10,2,8,128]{3,2,1,0:T(8,128)S(1)}, u32[]{:S(2)}, u32[]{:S(2)}) collective-permute-start(f32[10,2,8,128]{3,2,1,0:T(8,128)S(1)} %lanes.1), channel_id=1, source_target_pairs={{0,1},{1,0},{2,3},{3,2},{4,5},{5,4},{6,7},{7,6},{8,9},{9,8},{10,11... | collective-permute-start | bytes 245768 | tf_op jit(solution)/shard_map/ppermute | solution.py:351

commit v3 on v2

--- a/solution.py
+++ b/solution.py
@@ -12,10 +12,21 @@
 AXES = ("rad", "azi", "ax")
 
 
-def line_pairs(count, first):
+def pair_round(sizes, along, first):
+    n = sizes[along]
+    step = [sizes[1] * sizes[2], sizes[2], 1]
+    used = range(first, n - 1, 2)
+    partner = {i: i + 1 for i in used} | {i + 1: i for i in used}
+    idle = [i for i in range(n) if i not in partner]
+    if along == 2 and len(idle) == 2:
+        partner |= {idle[0]: idle[1], idle[1]: idle[0]}
     pairs = []
-    for i in range(first, count - 1, 2):
-        pairs += [(i, i + 1), (i + 1, i)]
+    for me in range(sizes[0] * step[0]):
+        i = me // step[along] % n
+        if i in partner:
+            pairs.append((me, me + (partner[i] - i) * step[along]))
+        elif along != 2 and sizes[2] % 2 == 0:
+            pairs.append((me, me ^ 1))
     return pairs
 
 
@@ -121,7 +132,9 @@
     for h in range(halves):
         for f in range(2 * F):
             a, b = ax_a[f, h], ax_b[f, h]
-            g = jnp.where(part < 2, jnp.where(even_ax, b, a), jnp.where(even_ax, a, b))
+            left = jnp.where(i_ax == 0, 0.0, jnp.where(even_ax, b, a))
+            right = jnp.where(i_ax == n_ax - 1, 0.0, jnp.where(even_ax, a, b))
+            g = jnp.where(part < 2, left, right)
             for k, x in enumerate(split3(g)):
                 got[k, f, h] = x.astype(jnp.float32)
 
@@ -158,18 +171,19 @@
 
 
 def main_kernel(
-    dims, prim, adj, bw, rad_a, rad_b, azi_l, azi_r, row, ind, send, far, low, top, frad, fazi
+    dims, n_rad, prim, adj, bw, rad_a, rad_b, azi_l, azi_r, row, ind, send, far, low, top, frad, fazi
 ):
     nr, na, nx = dims
-    odd = lax.rem(lax.axis_index("rad"), 2)
+    i_rad = lax.axis_index("rad")
+    odd = lax.rem(i_rad, 2)
     tiles = na // 8
     last = 8 * (tiles - 1)
     lane = lax.broadcasted_iota(jnp.int32, (8, nx), 1)
     for f in range(2 * F):
         for i in range(2):
             a, b = rad_a[f, i], rad_b[f, i]
-            far[f, i] = jnp.where(odd == 0, b, a)
-            far[f, 2 + i] = jnp.where(odd == 0, a, b)
+            far[f, i] = jnp.where(i_rad == 0, 0.0, jnp.where(odd == 0, b, a))
+            far[f, 2 + i] = jnp.where(i_rad == n_rad - 1, 0.0, jnp.where(odd == 0, a, b))
 
     def edges(r, carry):
         for t, src in enumerate((prim, adj)):
@@ -262,38 +276,45 @@
     head = jnp.broadcast_to(row[:, 0:nx], (8, nx))
     head = jnp.where(lane < groups * halves_a, means, head)
     tail = jnp.broadcast_to(row[:, nx:2 * nx], (8, nx))
+    both = jnp.where(lax.broadcasted_iota(jnp.int32, (8, nx), 0) & 1 == 0, head, tail)
     for d in range(send.shape[0] // 8):
-        send[pl.ds(8 * d, 8), 0:nx] = head
-        send[pl.ds(8 * d, 8), nx:2 * nx] = tail
-
-
-def final_kernel(n_loc, per_ax, data, cost, load):
-    n_dev = data.shape[0]
-    nx = data.shape[1] // 2
+        send[pl.ds(8 * d, 8), :] = both
+
+
+def final_kernel(n_loc, per_ax, data, cost, load, means):
+    n_dev, nx = data.shape[0] // 2, data.shape[1]
     me = (lax.axis_index("rad") * lax.axis_size("azi") + lax.axis_index("azi")) * lax.axis_size(
         "ax"
     ) + lax.axis_index("ax")
     lane = lax.broadcasted_iota(jnp.int32, (8, nx), 1)
     sub = lax.broadcasted_iota(jnp.int32, (8, nx), 0)
+    small = n_dev <= 32
+    groups = n_dev // 8
+    ok = lane < n_loc
+
+    def rows(g, part):
+        return data[pl.ds(16 * g + part, 8, stride=2), :]
+
+    def table(g, carry):
+        x = jnp.where(ok, rows(g, 0), 0.0)
+        x = pltpu.roll(x, 0, 1, stride=n_loc, stride_axis=0)
+        means[g] = jnp.broadcast_to(jnp.sum(x, axis=0, keepdims=True), (8, nx))
+        return carry
+
+    lax.fori_loop(0, groups, table, 0, unroll=small)
 
     def group(g, carry):
         acc_load, acc_cost = carry
-        rows = pl.ds(pl.multiple_of(8 * g, 8), 8)
-        head = data[rows, 0:nx]
-        tail = data[rows, nx:2 * nx]
+        head = rows(g, 0)
+        tail = rows(g, 1)
         spot = head.astype(jnp.int32)
-        dev = spot // n_loc
-        pos = spot - dev * n_loc
-
-        def look(d8, acc):
-            table = data[pl.ds(pl.multiple_of(8 * d8, 8), 8), 0:nx]
-            for i in range(8):
-                t = jnp.broadcast_to(table[i:i + 1, :], (8, nx))
-                v = jnp.take_along_axis(t, pos, axis=1)
-                acc = jnp.where(dev == d8 * 8 + i, v, acc)
-            return acc
-
-        val = lax.fori_loop(0, n_dev // 8, look, jnp.zeros((8, nx), jnp.float32), unroll=n_dev <= 32)
+        pos = spot & (nx - 1)
+        line = spot >> (nx.bit_length() - 1)
+
+        def look(q, acc):
+            return jnp.where(line == q, jnp.take_along_axis(means[q], pos, axis=1), acc)
+
+        val = lax.fori_loop(0, groups, look, jnp.zeros((8, nx), jnp.float32), unroll=small)
         beside = None
         for j in range(6):
             x = pltpu.roll(val, nx - n_loc * (1 + j), 1)
@@ -304,13 +325,12 @@
         weight = pltpu.roll(tail, nx - n_loc, 1)
         home = sub + 8 * g
         c = smooth * (1.0 + 7.0 * refine) + jnp.where(owner != home, 0.25 * weight, 0.0)
-        ok = lane < n_loc
         acc_load = acc_load + jnp.where(ok & (owner == me), c, 0.0)
         acc_cost = acc_cost + jnp.where(home == me, c, 0.0)
         return acc_load, acc_cost
 
     zero = jnp.zeros((8, nx), jnp.float32)
-    acc_load, acc_cost = lax.fori_loop(0, n_dev // 8, group, (zero, zero), unroll=n_dev <= 32)
+    acc_load, acc_cost = lax.fori_loop(0, groups, group, (zero, zero), unroll=small)
     own = jnp.sum(acc_cost, axis=0, keepdims=True)
     for b in range(n_loc // per_ax):
         x = own if b == 0 else pltpu.roll(own, nx - b * per_ax, 1)
@@ -322,7 +342,7 @@
 def on_device(primal, adjoint, refine_flag, owner_map, migrate_weight, neighbor_list):
     _, nr, na, nx = primal.shape
     dims = (nr, na, nx)
-    n_rad, n_azi, n_ax = (lax.axis_size(a) for a in AXES)
+    sizes = n_rad, n_azi, n_ax = tuple(lax.axis_size(a) for a in AXES)
     n_dev = n_rad * n_azi * n_ax
     tiles = na // 8
     halves = nr * tiles // (nx // 4)
@@ -348,12 +368,12 @@
         name="lanes",
     )(primal, adjoint)
 
-    ax_a = lax.ppermute(ax_s, "ax", line_pairs(n_ax, 0))
-    ax_b = lax.ppermute(ax_s, "ax", line_pairs(n_ax, 1))
+    ax_a = lax.ppermute(ax_s, AXES, pair_round(sizes, 2, 0))
+    ax_b = lax.ppermute(ax_s, AXES, pair_round(sizes, 2, 1))
     azi_l = lax.ppermute(azi_s, "azi", ring(n_azi, 1))
     azi_r = azi_l if n_azi == 2 else lax.ppermute(azi_s, "azi", ring(n_azi, -1))
-    rad_a = lax.ppermute(rad_a, "rad", line_pairs(n_rad, 0))
-    rad_b = lax.ppermute(rad_b, "rad", line_pairs(n_rad, 1))
+    rad_a = lax.ppermute(rad_a, AXES, pair_round(sizes, 0, 0))
+    rad_b = lax.ppermute(rad_b, AXES, pair_round(sizes, 0, 1))
 
     per_rad, per_azi, per_ax = nr // BLK, na // BLK, nx // BLK
     n_loc = per_rad * per_azi * per_ax
@@ -391,8 +411,8 @@
     )(primal, adjoint, ax_a, ax_b)
 
     indicator, send = pl.pallas_call(
-        functools.partial(main_kernel, dims),
-        out_shape=(f32(dims), f32((n_dev, 2 * nx))),
+        functools.partial(main_kernel, dims, n_rad),
+        out_shape=(f32(dims), f32((2 * n_dev, nx))),
         in_specs=[vmem] * 8,
         out_specs=(vmem, vmem),
         scratch_shapes=[
@@ -413,6 +433,7 @@
         out_shape=(f32((per_rad, per_azi, per_ax)), f32((1, 1, 1))),
         in_specs=[vmem],
         out_specs=(vmem, vmem),
+        scratch_shapes=[pltpu.VMEM((n_dev // 8, 8, nx), jnp.float32)],
         name="blocks",
     )(data)
     return indicator, cost, load

time: 39.5 us -> 35.2 us (0.89)
  starting transfers between devices: 9.65 us -> 6.35 us
  blocking collectives: 13.3 us -> 11.1 us
  waiting for transfers between devices: 0.32 us -> 2.23 us
  local copies, waits for them, and re-layouts: 1.16 us -> 0.52 us
    ppermute x4, starting transfers between devices: 8.07 us -> 4.76 us  [the longest x1 3.09 us: on_device(): rad_a = lax.ppermute(rad_a, AXES, pair_round(sizes, 0, 0))]
    all_to_all x1, blocking collectives: 13.3 us -> 11.1 us  [on_device(): data = lax.all_to_all(send, AXES, 0, 0, tiled=True)]
    ppermute x4, waiting for transfers between devices: 0.31 us -> 2.22 us  [the longest x1 2.22 us: on_device(): ax_b = lax.ppermute(ax_s, AXES, pair_round(sizes, 2, 1))]
    unnamed x13 -> x12, local copies, waits for them, and re-layouts: 0.63 us -> 0.03 us
  transfers between devices with their start and end apart: 5 -> 5, of which waited for: 1 -> 1; matrix products, arithmetic and copies ran while one was open for 2% -> 2% of each run, Pallas kernels for 13% -> 14%
where the time goes in v3:
time: 35.2 us; the launch traced here: 35 us
  Pallas kernels  13.9 us (39%)
  blocking collectives  11.1 us (32%)
  starting transfers between devices  6.35 us (18%)
  waiting for transfers between devices  2.23 us (6%)
  between operations  0.72 us (2%)
  local copies, waits for them, and re-layouts  0.52 us (1%)
    all_to_all x1, blocking collectives, on_device(): data = lax.all_to_all(send, AXES, 0, 0, tiled=True)  11.1 us
    pallas_call x1, Pallas kernels, on_device(): pl.pallas_call(functools.partial(main_kernel, dims, n_rad), out_shape=(f3...  4.83 us
    pallas_call x1, Pallas kernels, on_device(): pl.pallas_call(functools.partial(axial_kernel, dims, n_ax), out_shape=f32...  4.26 us
    ppermute x1, starting transfers between devices, on_device(): rad_a = lax.ppermute(rad_a, AXES, pair_round(sizes, 0, 0))  3.09 us
    pallas_call x1, Pallas kernels, on_device(): pl.pallas_call(functools.partial(edge_kernel, dims), out_shape=(f32((2 *...  2.45 us
    ppermute x1, waiting for transfers between devices, on_device(): ax_b = lax.ppermute(ax_s, AXES, pair_round(sizes, 2, 1))  2.22 us
    pallas_call x1, Pallas kernels, on_device(): pl.pallas_call(functools.partial(final_kernel, n_loc, per_ax), out_shape=...  1.66 us
    ppermute x1, starting transfers between devices, on_device(): azi_l = lax.ppermute(azi_s, 'azi', ring(n_azi, 1))  1.58 us
  transfers between devices with their start and end apart: 5, of which 1 were waited for; matrix products, arithmetic and copies ran while one was open for 2% of the time, Pallas kernels for 14%

profile of v3, /device:TPU:0, one launch (start us, length us, event | category | flops | bytes accessed | tf_op | source)
XLA Modules:
  0.0 35.0 jit_solution(2939108607306881653)
XLA Ops:
  0.6 0.0 copy-start.1
  0.6 0.0 copy-start
  0.6 2.5 %edges.1 = (f32[10,2,32,128]{3,2,1,0:T(8,128)}, f32[10,2,32,128]{3,2,1,0:T(8,128)}, f32[10,16,4,128]{3,2,1,0:T(4,128)}) custom-call(f32[5,16,32,128]{3,2,1,0:T(8,128)} %prim.7, f32[5,16,32,128]{3,2,1,0:T(8,128)} %adj.7), custom_call_target="tpu_custom_call" | custom-call | tf_op jit(solution)/shard_map/edges/pallas_call | solution.py:354
  3.1 3.1 %collective-permute-start.2 = (f32[10,2,32,128]{3,2,1,0:T(8,128)}, f32[10,2,32,128]{3,2,1,0:T(8,128)S(1)}, u32[]{:S(2)}, u32[]{:S(2)}) collective-permute-start(f32[10,2,32,128]{3,2,1,0:T(8,128)} %get-tuple-element.10), channel_id=1, source_target_pairs={{0,8},{1,9},{2,10},{3,11},{4,12},{5,13},{6,14},{7,15},{8,0},{9,1},... | collective-permute-start | bytes 983048 | tf_op jit(solution)/shard_map/ppermute | solution.py:375
  6.2 0.0 collective-permute-start.3
  6.2 0.0 copy-start.2
  6.2 0.0 copy-start.3
  6.2 0.0 copy-start.4
  6.2 0.0 copy-start.5
  6.2 1.6 %collective-permute-start.4 = (f32[10,16,4,128]{3,2,1,0:T(4,128)}, f32[10,16,4,128]{3,2,1,0:T(4,128)S(1)}, u32[]{:S(2)}, u32[]{:S(2)}) collective-permute-start(f32[10,16,4,128]{3,2,1,0:T(4,128)} %get-tuple-element.12), channel_id=1, source_target_pairs={{0,4},{4,0},{1,5},{5,1},{2,6},{6,2},{3,7},{7,3},{8,12},{12,8},{9,1... | collective-permute-start | bytes 983048 | tf_op jit(solution)/shard_map/ppermute | solution.py:373
  7.8 0.0 copy-done.1
  7.8 0.0 copy-done
  7.8 0.7 %lanes.1 = f32[10,2,8,128]{3,2,1,0:T(8,128)S(1)} custom-call(f32[5,16,32,128]{3,2,1,0:T(8,128)S(1)} %copy-done, f32[5,16,32,128]{3,2,1,0:T(8,128)S(1)} %copy-done.1), custom_call_target="tpu_custom_call" | custom-call | tf_op jit(solution)/shard_map/lanes/pallas_call | solution.py:362
  8.6 1.4 %collective-permute-start.1 = (f32[10,2,8,128]{3,2,1,0:T(8,128)S(1)}, f32[10,2,8,128]{3,2,1,0:T(8,128)S(1)}, u32[]{:S(2)}, u32[]{:S(2)}) collective-permute-start(f32[10,2,8,128]{3,2,1,0:T(8,128)S(1)} %lanes.1), channel_id=1, source_target_pairs={{0,3},{1,2},{2,1},{3,0},{4,7},{5,6},{6,5},{7,4},{8,11},{9,10},{10,... | collective-permute-start | bytes 245768 | tf_op jit(solution)/shard_map/ppermute | solution.py:372
  9.9 0.3 collective-permute-start
  10.2 0.0 copy-done.2
  10.2 0.1 fusion.4
  10.3 0.0 copy-done.3
  10.3 0.1 reshape.28
  10.4 0.0 copy-done.4
  10.4 0.1 reshape.29
  10.5 0.0 copy-done.5
  10.5 0.1 reshape.30
  10.6 0.1 reshape.26
  10.7 0.1 reshape.27
  10.7 0.1 concatenate.3
  10.8 2.2 %collective-permute-done.1.ax_b = f32[10,2,8,128]{3,2,1,0:T(8,128)S(1)} collective-permute-done((f32[10,2,8,128]{3,2,1,0:T(8,128)S(1)}, f32[10,2,8,128]{3,2,1,0:T(8,128)S(1)}, u32[]{:S(2)}, u32[]{:S(2)}) %collective-permute-start.1) | collective-permute-done | bytes 81952 | tf_op jit(solution)/shard_map/ppermute | solution.py:372
  13.1 0.0 collective-permute-done.ax_a
  13.1 4.3 %axial.1.bw = f32[10,16,32,128]{3,2,1,0:T(8,128)S(1)} custom-call(f32[5,16,32,128]{3,2,1,0:T(8,128)S(1)} %copy-done, f32[5,16,32,128]{3,2,1,0:T(8,128)S(1)} %copy-done.1, f32[10,2,8,128]{3,2,1,0:T(8,128)S(1)} %collective-permute-done.ax_a, f32[10,2,8,128]{3,2,1,0:T(8,128)S(1)} %collective-permute-done.1.ax_b), custom_call_target="tpu_custom_call" | custom-call | tf_op jit(solution)/shard_map/axial/pallas_call | solution.py:398
  17.3 0.0 collective-permute-done.2.rad_a
  17.3 0.0 collective-permute-done.3.rad_b
  17.4 0.0 collective-permute-done.4.azi_l.azi_r
  17.4 4.8 %stencil.1 = (f32[16,32,128]{2,1,0:T(8,128)}, f32[64,128]{1,0:T(8,128)S(1)}) custom-call(f32[5,16,32,128]{3,2,1,0:T(8,128)S(1)} %copy-done, f32[5,16,32,128]{3,2,1,0:T(8,128)S(1)} %copy-done.1, f32[10,16,32,128]{3,2,1,0:T(8,128)S(1)} %axial.1.bw, f32[10,2,32,128]{3,2,1,0:T(8,128)S(1)} %collective-permute-done.2.rad_a, ...), custom_call_target="tpu_custom_call" | custom-call | tf_op jit(solution)/shard_map/stencil/pallas_call | solution.py:413
  22.2 11.1 %all_to_all.11 = f32[32,2,128]{2,1,0:T(2,128)} all-to-all(f32[32,2,128]{2,1,0:T(2,128)S(1)} %bitcast.6), channel_id=1, replica_groups=mesh['rad'=4,'azi'=2,'ax'=4] {'rad','azi','ax'}, dimensions={0} | all-to-all | bytes 65536 | tf_op jit(solution)/shard_map/all_to_all | solution.py:429
  33.3 1.7 %blocks.1 = (f32[1,2,8]{2,1,0:T(2,128)}, f32[1,1,1]{2,1,0:T(1,128)}) custom-call(f32[64,128]{1,0:T(8,128)} %bitcast.8), custom_call_target="tpu_custom_call" | custom-call | tf_op jit(solution)/shard_map/blocks/pallas_call | solution.py:431
  (3 shorter events, 0.0 us)
Async XLA Ops:
  0.6 7.2 %copy-start.1 = (f32[5,16,32,128]{3,2,1,0:T(8,128)S(1)}, f32[5,16,32,128]{3,2,1,0:T(8,128)}, u32[]{:S(2)}) copy-start(f32[5,16,32,128]{3,2,1,0:T(8,128)} %adj.7) | copy-start | bytes 3932164
  0.6 7.2 %copy-start = (f32[5,16,32,128]{3,2,1,0:T(8,128)S(1)}, f32[5,16,32,128]{3,2,1,0:T(8,128)}, u32[]{:S(2)}) copy-start(f32[5,16,32,128]{3,2,1,0:T(8,128)} %prim.7) | copy-start | bytes 3932164
  3.1 14.2 %collective-permute-start.2 = (f32[10,2,32,128]{3,2,1,0:T(8,128)}, f32[10,2,32,128]{3,2,1,0:T(8,128)S(1)}, u32[]{:S(2)}, u32[]{:S(2)}) collective-permute-start(f32[10,2,32,128]{3,2,1,0:T(8,128)} %get-tuple-element.10), channel_id=1, source_target_pairs={{0,8},{1,9},{2,10},{3,11},{4,12},{5,13},{6,14},{7,15},{8,0},{9,1},... | collective-permute-start | bytes 983048 | tf_op jit(solution)/shard_map/ppermute | solution.py:375
  6.2 11.1 %collective-permute-start.3 = (f32[10,2,32,128]{3,2,1,0:T(8,128)}, f32[10,2,32,128]{3,2,1,0:T(8,128)}, u32[]{:S(2)}, u32[]{:S(2)}) collective-permute-start(f32[10,2,32,128]{3,2,1,0:T(8,128)} %get-tuple-element.11), channel_id=1, source_target_pairs={{0,1},{1,0},{2,3},{3,2},{4,5},{5,4},{6,7},{7,6},{8,16},{9,17},{10,... | collective-permute-start | bytes 983048 | tf_op jit(solution)/shard_map/ppermute | solution.py:376
  6.2 4.0 %copy-start.2 = (s32[1,2,8,6]{2,1,3,0:T(2,128)S(1)}, s32[1,2,8,6]{2,1,3,0:T(2,128)}, u32[]{:S(2)}) copy-start(s32[1,2,8,6]{2,1,3,0:T(2,128)} %param.11) | copy-start | bytes 1156
  6.2 4.1 %copy-start.3 = (s32[1,2,8]{2,1,0:T(2,128)S(1)}, s32[1,2,8]{2,1,0:T(2,128)}, u32[]{:S(2)}) copy-start(s32[1,2,8]{2,1,0:T(2,128)} %param.8) | copy-start | bytes 196
  6.2 4.2 %copy-start.4 = (s32[1,2,8]{2,1,0:T(2,128)S(1)}, s32[1,2,8]{2,1,0:T(2,128)}, u32[]{:S(2)}) copy-start(s32[1,2,8]{2,1,0:T(2,128)} %param.9) | copy-start | bytes 196
  6.2 4.3 %copy-start.5 = (s32[1,2,8]{2,1,0:T(2,128)S(1)}, s32[1,2,8]{2,1,0:T(2,128)}, u32[]{:S(2)}) copy-start(s32[1,2,8]{2,1,0:T(2,128)} %param.10) | copy-start | bytes 196
  6.2 11.1 %collective-permute-start.4 = (f32[10,16,4,128]{3,2,1,0:T(4,128)}, f32[10,16,4,128]{3,2,1,0:T(4,128)S(1)}, u32[]{:S(2)}, u32[]{:S(2)}) collective-permute-start(f32[10,16,4,128]{3,2,1,0:T(4,128)} %get-tuple-element.12), channel_id=1, source_target_pairs={{0,4},{4,0},{1,5},{5,1},{2,6},{6,2},{3,7},{7,3},{8,12},{12,8},{9,1... | collective-permute-start | bytes 983048 | tf_op jit(solution)/shard_map/ppermute | solution.py:373
  8.6 4.5 %collective-permute-start.1 = (f32[10,2,8,128]{3,2,1,0:T(8,128)S(1)}, f32[10,2,8,128]{3,2,1,0:T(8,128)S(1)}, u32[]{:S(2)}, u32[]{:S(2)}) collective-permute-start(f32[10,2,8,128]{3,2,1,0:T(8,128)S(1)} %lanes.1), channel_id=1, source_target_pairs={{0,3},{1,2},{2,1},{3,0},{4,7},{5,6},{6,5},{7,4},{8,11},{9,10},{10,... | collective-permute-start | bytes 245768 | tf_op jit(solution)/shard_map/ppermute | solution.py:372
  9.9 3.1 %collective-permute-start = (f32[10,2,8,128]{3,2,1,0:T(8,128)S(1)}, f32[10,2,8,128]{3,2,1,0:T(8,128)S(1)}, u32[]{:S(2)}, u32[]{:S(2)}) collective-permute-start(f32[10,2,8,128]{3,2,1,0:T(8,128)S(1)} %lanes.1), channel_id=1, source_target_pairs={{0,1},{1,0},{2,3},{3,2},{4,5},{5,4},{6,7},{7,6},{8,9},{9,8},{10,11... | collective-permute-start | bytes 245768 | tf_op jit(solution)/shard_map/ppermute | solution.py:371

commit v4 on v3

--- a/solution.py
+++ b/solution.py
@@ -106,7 +106,66 @@
 FOURTH = {-2: 1.0, -1: -4.0, 0: 6.0, 1: -4.0, 2: 1.0}
 
 
-def axial_kernel(dims, n_ax, prim, adj, ax_a, ax_b, bw, got, lhs, rhs, sums):
+def block_row(grid, near, refine, owner, weight, nx):
+    (per_rad, per_azi, per_ax), (n_azi, n_ax) = grid
+    n_loc = per_rad * per_azi * per_ax
+    blocks_azi, blocks_ax = per_azi * n_azi, per_ax * n_ax
+    lane = lax.broadcasted_iota(jnp.int32, (per_azi, nx), 1)
+
+    def place(number):
+        b_rad = lax.div(number, blocks_azi * blocks_ax)
+        b_azi = lax.rem(lax.div(number, blocks_ax), blocks_azi)
+        b_ax = lax.rem(number, blocks_ax)
+        device = (lax.div(b_rad, per_rad) * n_azi + lax.div(b_azi, per_azi)) * n_ax + lax.div(b_ax, per_ax)
+        local = (lax.rem(b_rad, per_rad) * per_azi + lax.rem(b_azi, per_azi)) * per_ax + lax.rem(b_ax, per_ax)
+        return device * n_loc + local
+
+    def spread(x, at):
+        x = jnp.concatenate([x, jnp.zeros((per_azi, nx - per_ax), jnp.int32)], axis=1)
+        x = jnp.where(lane < per_ax, x, 0).astype(jnp.float32)
+        rows = [x[b:b + 1] if at + b * per_ax == 0 else pltpu.roll(x[b:b + 1], at + b * per_ax, 1) for b in range(per_azi)]
+        return sum(rows[1:], rows[0])
+
+    head = spread(refine[0], 7 * n_loc)
+    for j in range(6):
+        head = head + spread(place(near[0, j]), (1 + j) * n_loc)
+    tail = spread(owner[0], 0) + spread(weight[0], n_loc)
+    return head, tail
+
+
+def own_kernel(
+    dims, grid, prim, adj, ax_s, near, refine, owner, weight, sums, fourth, row, lhs, rhs
+):
+    del ax_s
+    nr, na, nx = dims
+    head, tail = block_row(grid, near, refine, owner, weight, nx)
+    row[:, 0:nx] = head
+    row[:, nx:2 * nx] = tail
+    size = nr * na
+    i = lax.broadcasted_iota(jnp.int32, (nx, nx), 0)
+    c = lax.broadcasted_iota(jnp.int32, (nx, nx), 1)
+    for n, table in enumerate((UPPER, LOWER, FOURTH)):
+        own = taps(i, c, table).astype(jnp.bfloat16)
+        for k in range(3):
+            rhs[pl.ds(k * nx, nx), pl.ds(n * nx, nx)] = own
+
+    def build(t, src, f):
+        for r in range(nr):
+            rows = pl.ds(pl.multiple_of((t * F + f) * size, size) + r * na, na)
+            for k, x in enumerate(split3(src[f, r])):
+                lhs[rows, pl.ds(k * nx, nx)] = x
+
+    for t, src in enumerate((prim, adj)):
+        lax.fori_loop(0, F, lambda f, c, t=t, src=src: (build(t, src, f), c)[1], 0)
+    sums[...] = jnp.dot(
+        lhs[0:F * size, :], rhs[:, 0:2 * nx], preferred_element_type=jnp.float32
+    )
+    fourth[...] = jnp.dot(
+        lhs[F * size:2 * F * size, :], rhs[:, 2 * nx:3 * nx], preferred_element_type=jnp.float32
+    )
+
+
+def axial_kernel(dims, n_ax, sums, fourth, ax_a, ax_b, bw, got, lhs, rhs, far):
     nr, na, nx = dims
     i_ax = lax.axis_index("ax")
     even_ax = lax.rem(i_ax, 2) == 0
@@ -117,52 +176,50 @@
     per = nx // 4
     halves = nr * tiles // per
     size = nr * na
-
-    i = lax.broadcasted_iota(jnp.int32, (nx, nx), 0)
+    third = per // 3
+
+    i = lax.broadcasted_iota(jnp.int32, (nx, nx), 0) & 3
     c = lax.broadcasted_iota(jnp.int32, (nx, nx), 1)
-    p = i & 3
-    halo = jnp.where(p < 2, p - 2, p - 2 + nx)
+    cells = jnp.where(i < 2, i - 2, i - 2 + nx)
     for n, table in enumerate((UPPER, LOWER, FOURTH)):
-        own = taps(i, c, table).astype(jnp.bfloat16)
-        far = taps(halo, c, table).astype(jnp.bfloat16)
-        for k in range(3):
-            rhs[pl.ds(2 * k * nx, nx), pl.ds(n * nx, nx)] = own
-            rhs[pl.ds((2 * k + 1) * nx, nx), pl.ds(n * nx, nx)] = far
+        rhs[:, pl.ds(n * nx, nx)] = taps(cells, c, table).astype(jnp.bfloat16)
 
     for h in range(halves):
         for f in range(2 * F):
             a, b = ax_a[f, h], ax_b[f, h]
             left = jnp.where(i_ax == 0, 0.0, jnp.where(even_ax, b, a))
             right = jnp.where(i_ax == n_ax - 1, 0.0, jnp.where(even_ax, a, b))
-            g = jnp.where(part < 2, left, right)
-            for k, x in enumerate(split3(g)):
-                got[k, f, h] = x.astype(jnp.float32)
-
-    def build(t, src, f):
-        g0 = t * F + f
+            for k, x in enumerate(split3(jnp.where(part < 2, left, right))):
+                x = x.astype(jnp.float32)
+                got[k, f, h] = pltpu.roll(x, 4 * third * k, 1) if k else x
+
+    def build(g, carry):
         for r in range(nr):
             h, j0 = r * tiles // per, r * tiles % per
-            rows = pl.ds(pl.multiple_of(g0 * size, size) + r * na, na)
-            for k, x in enumerate(split3(src[f, r])):
-                lhs[rows, pl.ds(2 * k * nx, nx)] = x
-                g = got[k, g0, h]
-                y = [jnp.where(slot == j0 + a, g, 0.0) for a in range(tiles)]
-                lhs[rows, pl.ds((2 * k + 1) * nx, nx)] = jnp.concatenate(y, axis=0).astype(jnp.bfloat16)
-
-    for t, src in enumerate((prim, adj)):
-        lax.fori_loop(0, F, lambda f, c, t=t, src=src: (build(t, src, f), c)[1], 0)
-    sums[...] = jnp.dot(
-        lhs[0:F * size, :], rhs[:, 0:2 * nx], preferred_element_type=jnp.float32
-    )
-    bw[F:2 * F] = jnp.dot(
-        lhs[F * size:2 * F * size, :], rhs[:, 2 * nx:3 * nx], preferred_element_type=jnp.float32
+            rows = pl.ds(pl.multiple_of(g * size, size) + r * na, na)
+            y = []
+            for a in range(tiles):
+                x = jnp.zeros((8, nx), jnp.float32)
+                for k in range(3):
+                    x = jnp.where(slot == (j0 + a + third * k) % per, got[k, g, h], x)
+                y.append(x)
+            lhs[rows, :] = jnp.concatenate(y, axis=0).astype(jnp.bfloat16)
+        return carry
+
+    lax.fori_loop(0, 2 * F, build, 0)
+    far[...] = jnp.dot(lhs[0:F * size, :], rhs[:, 0:2 * nx], preferred_element_type=jnp.float32)
+    bw[F:2 * F] = (
+        fourth[...]
+        + jnp.dot(
+            lhs[F * size:2 * F * size, :], rhs[:, 2 * nx:3 * nx], preferred_element_type=jnp.float32
+        )
     ).reshape(F, nr, na, nx)
 
     def body(r, carry):
         for a in range(tiles):
             at = [pl.ds(f * size + pl.multiple_of(r * na, na) + 8 * a, 8) for f in range(F)]
-            up = flux([sums[q, 0:nx] for q in at], 2)
-            low = flux([sums[q, nx:2 * nx] for q in at], 2)
+            up = flux([sums[q, 0:nx] + far[q, 0:nx] for q in at], 2)
+            low = flux([sums[q, nx:2 * nx] + far[q, nx:2 * nx] for q in at], 2)
             for f in range(F):
                 bw[f, r, pl.ds(8 * a, 8), :] = up[f] - low[f]
         return carry
@@ -357,6 +414,7 @@
         in_specs=[hbm, hbm],
         out_specs=(vmem, vmem, vmem),
         scratch_shapes=[pltpu.SemaphoreType.DMA((2, 4))],
+        compiler_params=pltpu.CompilerParams(vmem_limit_bytes=60 << 20),
         name="edges",
     )(primal, adjoint)
     ax_s = pl.pallas_call(
@@ -377,24 +435,20 @@
 
     per_rad, per_azi, per_ax = nr // BLK, na // BLK, nx // BLK
     n_loc = per_rad * per_azi * per_ax
-    blocks_azi, blocks_ax = per_azi * n_azi, per_ax * n_ax
-    b_rad = neighbor_list // (blocks_azi * blocks_ax)
-    b_azi = neighbor_list // blocks_ax % blocks_azi
-    b_ax = neighbor_list % blocks_ax
-    device = (b_rad // per_rad * n_azi + b_azi // per_azi) * n_ax + b_ax // per_ax
-    local = (b_rad % per_rad * per_azi + b_azi % per_azi) * per_ax + b_ax % per_ax
-    spot = (device * n_loc + local).reshape(n_loc, 6).T.reshape(-1)
-    row = jnp.concatenate(
-        [
-            jnp.zeros((n_loc,), jnp.int32),
-            spot,
-            refine_flag.reshape(-1),
-            owner_map.reshape(-1),
-            migrate_weight.reshape(-1),
-        ]
-    ).astype(jnp.float32)
-    row = jnp.pad(row, (0, 2 * nx - row.shape[0]))[None]
-
+    near = neighbor_list.transpose(0, 3, 1, 2)
+    cells = F * nr * na
+    sums, fourth, row = pl.pallas_call(
+        functools.partial(own_kernel, dims, ((per_rad, per_azi, per_ax), (n_azi, n_ax))),
+        out_shape=(f32((cells, 2 * nx)), f32((cells, nx)), f32((1, 2 * nx))),
+        in_specs=[vmem] * 7,
+        out_specs=(vmem, vmem, vmem),
+        scratch_shapes=[
+            pltpu.VMEM((2 * cells, 3 * nx), jnp.bfloat16),
+            pltpu.VMEM((3 * nx, 3 * nx), jnp.bfloat16),
+        ],
+        compiler_params=pltpu.CompilerParams(vmem_limit_bytes=16 << 20),
+        name="own",
+    )(primal, adjoint, ax_s, near, refine_flag, owner_map, migrate_weight)
     bw = pl.pallas_call(
         functools.partial(axial_kernel, dims, n_ax),
         out_shape=f32((2 * F, nr, na, nx)),
@@ -402,13 +456,13 @@
         out_specs=vmem,
         scratch_shapes=[
             pltpu.VMEM((3, 2 * F, halves, 8, nx), jnp.float32),
-            pltpu.VMEM((2 * F * nr * na, 6 * nx), jnp.bfloat16),
-            pltpu.VMEM((6 * nx, 3 * nx), jnp.bfloat16),
-            pltpu.VMEM((F * nr * na, 2 * nx), jnp.float32),
+            pltpu.VMEM((2 * cells, nx), jnp.bfloat16),
+            pltpu.VMEM((nx, 3 * nx), jnp.bfloat16),
+            pltpu.VMEM((cells, 2 * nx), jnp.float32),
         ],
-        compiler_params=pltpu.CompilerParams(vmem_limit_bytes=40 << 20),
+        compiler_params=pltpu.CompilerParams(vmem_limit_bytes=16 << 20),
         name="axial",
-    )(primal, adjoint, ax_a, ax_b)
+    )(sums, fourth, ax_a, ax_b)
 
     indicator, send = pl.pallas_call(
         functools.partial(main_kernel, dims, n_rad),
@@ -434,6 +488,7 @@
         in_specs=[vmem],
         out_specs=(vmem, vmem),
         scratch_shapes=[pltpu.VMEM((n_dev // 8, 8, nx), jnp.float32)],
+        compiler_params=pltpu.CompilerParams(vmem_limit_bytes=4 << 20),
         name="blocks",
     )(data)
     return indicator, cost, load

time: 35.2 us -> 33.1 us (0.940)
  Pallas kernels: 13.9 us -> 11.9 us
  blocking collectives: 11.1 us -> 11.8 us
  local copies, waits for them, and re-layouts: 0.52 us -> 0.03 us
    pallas_call x1, Pallas kernels: 4.26 us -> 1.9 us  [on_device(): pl.pallas_call(functools.partial(axial_kernel, dims, n_ax), out_shape=f32...]
    pallas_call x0 -> x1, Pallas kernels: none -> 2.29 us  [on_device(): pl.pallas_call(functools.partial(own_kernel, dims, ((per_rad, per_azi, pe...]
    ppermute x1, waiting for transfers between devices: 2.22 us -> 0.63 us  [on_device(): ax_b = lax.ppermute(ax_s, AXES, pair_round(sizes, 2, 1))]
    ppermute x1, waiting for transfers between devices: 0.01 us -> 1.5 us  [on_device(): azi_l = lax.ppermute(azi_s, 'azi', ring(n_azi, 1))]
    pallas_call x1, Pallas kernels: 4.83 us -> 3.66 us  [on_device(): pl.pallas_call(functools.partial(main_kernel, dims, n_rad), out_shape=(f3...]
    pallas_call x1, Pallas kernels: 1.66 us -> 0.9 us  [on_device(): pl.pallas_call(functools.partial(final_kernel, n_loc, per_ax), out_shape=...]
    all_to_all x1, blocking collectives: 11.1 us -> 11.8 us  [on_device(): data = lax.all_to_all(send, AXES, 0, 0, tiled=True)]
    reshape x5 -> x0, local copies, waits for them, and re-layouts: 0.4 us -> none  [the longest x2 0.16 us: on_device(): spot = (device * n_loc + local).reshape(n_loc, 6).T.reshape(-1)]
  transfers between devices with their start and end apart: 5 -> 5, of which waited for: 1 -> 2; matrix products, arithmetic and copies ran while one was open for 2% -> 0% of each run, Pallas kernels for 14% -> 15%
where the time goes in v4:
time: 33.1 us; the launch traced here: 33 us
  Pallas kernels  11.9 us (36%)
  blocking collectives  11.8 us (36%)
  starting transfers between devices  6.35 us (19%)
  waiting for transfers between devices  2.14 us (6%)
  between operations  0.72 us (2%)
    all_to_all x1, blocking collectives, on_device(): data = lax.all_to_all(send, AXES, 0, 0, tiled=True)  11.8 us
    pallas_call x1, Pallas kernels, on_device(): pl.pallas_call(functools.partial(main_kernel, dims, n_rad), out_shape=(f3...  3.66 us
    ppermute x1, starting transfers between devices, on_device(): rad_a = lax.ppermute(rad_a, AXES, pair_round(sizes, 0, 0))  3.09 us
    pallas_call x1, Pallas kernels, on_device(): pl.pallas_call(functools.partial(edge_kernel, dims), out_shape=(f32((2 *...  2.46 us
    pallas_call x1, Pallas kernels, on_device(): pl.pallas_call(functools.partial(own_kernel, dims, ((per_rad, per_azi, pe...  2.29 us
    pallas_call x1, Pallas kernels, on_device(): pl.pallas_call(functools.partial(axial_kernel, dims, n_ax), out_shape=f32...  1.9 us
    ppermute x1, starting transfers between devices, on_device(): azi_l = lax.ppermute(azi_s, 'azi', ring(n_azi, 1))  1.58 us
    ppermute x1, waiting for transfers between devices, on_device(): azi_l = lax.ppermute(azi_s, 'azi', ring(n_azi, 1))  1.5 us
  transfers between devices with their start and end apart: 5, of which 2 were waited for; matrix products, arithmetic and copies ran while one was open for 0% of the time, Pallas kernels for 15%

profile of v4, /device:TPU:0, one launch (start us, length us, event | category | flops | bytes accessed | tf_op | source)
XLA Modules:
  0.0 33.0 jit_solution(762744155324721469)
XLA Ops:
  0.6 0.0 copy-start
  0.6 0.0 copy-start.1
  0.6 2.5 %edges.1 = (f32[10,2,32,128]{3,2,1,0:T(8,128)}, f32[10,2,32,128]{3,2,1,0:T(8,128)}, f32[10,16,4,128]{3,2,1,0:T(4,128)}) custom-call(f32[5,16,32,128]{3,2,1,0:T(8,128)} %prim.7, f32[5,16,32,128]{3,2,1,0:T(8,128)} %adj.7), custom_call_target="tpu_custom_call" | custom-call | tf_op jit(solution)/shard_map/edges/pallas_call | solution.py:411
  3.1 3.1 %collective-permute-start.2 = (f32[10,2,32,128]{3,2,1,0:T(8,128)}, f32[10,2,32,128]{3,2,1,0:T(8,128)S(1)}, u32[]{:S(2)}, u32[]{:S(2)}) collective-permute-start(f32[10,2,32,128]{3,2,1,0:T(8,128)} %get-tuple-element.15), channel_id=1, source_target_pairs={{0,8},{1,9},{2,10},{3,11},{4,12},{5,13},{6,14},{7,15},{8,0},{9,1},... | collective-permute-start | bytes 983048 | tf_op jit(solution)/shard_map/ppermute | solution.py:433
  6.2 0.0 collective-permute-start.3
  6.2 0.0 copy-start.2
  6.2 0.0 copy-start.3
  6.2 0.0 copy-start.4
  6.2 0.0 copy-start.5
  6.2 1.6 %collective-permute-start.4 = (f32[10,16,4,128]{3,2,1,0:T(4,128)}, f32[10,16,4,128]{3,2,1,0:T(4,128)S(1)}, u32[]{:S(2)}, u32[]{:S(2)}) collective-permute-start(f32[10,16,4,128]{3,2,1,0:T(4,128)} %get-tuple-element.17), channel_id=1, source_target_pairs={{0,4},{4,0},{1,5},{5,1},{2,6},{6,2},{3,7},{7,3},{8,12},{12,8},{9,1... | collective-permute-start | bytes 983048 | tf_op jit(solution)/shard_map/ppermute | solution.py:431
  7.8 0.0 copy-done
  7.8 0.0 copy-done.1
  7.8 0.7 %lanes.1.ax_s = f32[10,2,8,128]{3,2,1,0:T(8,128)S(1)} custom-call(f32[5,16,32,128]{3,2,1,0:T(8,128)S(1)} %copy-done, f32[5,16,32,128]{3,2,1,0:T(8,128)S(1)} %copy-done.1), custom_call_target="tpu_custom_call" | custom-call | tf_op jit(solution)/shard_map/lanes/pallas_call | solution.py:420
  8.6 0.3 collective-permute-start
  8.8 1.4 %collective-permute-start.1 = (f32[10,2,8,128]{3,2,1,0:T(8,128)S(1)}, f32[10,2,8,128]{3,2,1,0:T(8,128)S(1)}, u32[]{:S(2)}, u32[]{:S(2)}) collective-permute-start(f32[10,2,8,128]{3,2,1,0:T(8,128)S(1)} %lanes.1.ax_s), channel_id=1, source_target_pairs={{0,3},{1,2},{2,1},{3,0},{4,7},{5,6},{6,5},{7,4},{8,11},{9,10},{10,... | collective-permute-start | bytes 245768 | tf_op jit(solution)/shard_map/ppermute | solution.py:430
  10.2 0.0 copy-done.2
  10.2 0.0 copy-done.3
  10.2 0.0 copy-done.4
  10.2 0.0 copy-done.5
  10.2 2.3 %own.1 = (f32[2560,256]{1,0:T(8,128)S(1)}, f32[2560,128]{1,0:T(8,128)S(1)}, f32[1,256]{1,0:T(1,128)S(1)}) custom-call(f32[5,16,32,128]{3,2,1,0:T(8,128)S(1)} %copy-done, f32[5,16,32,128]{3,2,1,0:T(8,128)S(1)} %copy-done.1, f32[10,2,8,128]{3,2,1,0:T(8,128)S(1)} %lanes.1.ax_s, s32[1,6,2,8]{3,2,1,0:T(2,128)S(1)} %bitcast.5, s32[1,2,8]{2,1,0:T(2,128)S(1)} %copy-done.3, ...), custom_call_target="tpu_custom_call" | custom-call | tf_op jit(solution)/shard_map/own/pallas_call | solution.py:440
  12.5 0.0 collective-permute-done.ax_a
  12.6 0.6 %collective-permute-done.1.ax_b = f32[10,2,8,128]{3,2,1,0:T(8,128)S(1)} collective-permute-done((f32[10,2,8,128]{3,2,1,0:T(8,128)S(1)}, f32[10,2,8,128]{3,2,1,0:T(8,128)S(1)}, u32[]{:S(2)}, u32[]{:S(2)}) %collective-permute-start.1) | collective-permute-done | bytes 81952 | tf_op jit(solution)/shard_map/ppermute | solution.py:430
  13.2 1.9 %axial.1.bw = f32[10,16,32,128]{3,2,1,0:T(8,128)S(1)} custom-call(f32[2560,256]{1,0:T(8,128)S(1)} %get-tuple-element.13.sums, f32[2560,128]{1,0:T(8,128)S(1)} %get-tuple-element.14.fourth, f32[10,2,8,128]{3,2,1,0:T(8,128)S(1)} %collective-permute-done.ax_a, f32[10,2,8,128]{3,2,1,0:T(8,128)S(1)} %collective-permute-done.1.ax_b), custom_call_target="tpu_custom_call" | custom-call | tf_op jit(solution)/shard_map/axial/pallas_call | solution.py:452
  15.1 0.0 collective-permute-done.2.rad_a
  15.1 0.0 collective-permute-done.3.rad_b
  15.1 1.5 %collective-permute-done.4.azi_l.azi_r = f32[10,16,4,128]{3,2,1,0:T(4,128)S(1)} collective-permute-done((f32[10,16,4,128]{3,2,1,0:T(4,128)}, f32[10,16,4,128]{3,2,1,0:T(4,128)S(1)}, u32[]{:S(2)}, u32[]{:S(2)}) %collective-permute-start.4) | collective-permute-done | bytes 327712 | tf_op jit(solution)/shard_map/ppermute | solution.py:431
  16.6 3.7 %stencil.1 = (f32[16,32,128]{2,1,0:T(8,128)}, f32[64,128]{1,0:T(8,128)S(1)}) custom-call(f32[5,16,32,128]{3,2,1,0:T(8,128)S(1)} %copy-done, f32[5,16,32,128]{3,2,1,0:T(8,128)S(1)} %copy-done.1, f32[10,16,32,128]{3,2,1,0:T(8,128)S(1)} %axial.1.bw, f32[10,2,32,128]{3,2,1,0:T(8,128)S(1)} %collective-permute-done.2.rad_a, ...), custom_call_target="tpu_custom_call" | custom-call | tf_op jit(solution)/shard_map/stencil/pallas_call | solution.py:467
  20.3 11.8 %all_to_all.11 = f32[32,2,128]{2,1,0:T(2,128)S(1)} all-to-all(f32[32,2,128]{2,1,0:T(2,128)S(1)} %bitcast.4), channel_id=1, replica_groups=mesh['rad'=4,'azi'=2,'ax'=4] {'rad','azi','ax'}, dimensions={0} | all-to-all | bytes 65536 | tf_op jit(solution)/shard_map/all_to_all | solution.py:483
  32.0 0.9 %blocks.1 = (f32[1,2,8]{2,1,0:T(2,128)}, f32[1,1,1]{2,1,0:T(1,128)}) custom-call(f32[64,128]{1,0:T(8,128)S(1)} %bitcast.3), custom_call_target="tpu_custom_call" | custom-call | tf_op jit(solution)/shard_map/blocks/pallas_call | solution.py:485
Async XLA Ops:
  0.6 7.2 %copy-start = (f32[5,16,32,128]{3,2,1,0:T(8,128)S(1)}, f32[5,16,32,128]{3,2,1,0:T(8,128)}, u32[]{:S(2)}) copy-start(f32[5,16,32,128]{3,2,1,0:T(8,128)} %prim.7) | copy-start | bytes 3932164
  0.6 7.2 %copy-start.1 = (f32[5,16,32,128]{3,2,1,0:T(8,128)S(1)}, f32[5,16,32,128]{3,2,1,0:T(8,128)}, u32[]{:S(2)}) copy-start(f32[5,16,32,128]{3,2,1,0:T(8,128)} %adj.7) | copy-start | bytes 3932164
  3.1 12.0 %collective-permute-start.2 = (f32[10,2,32,128]{3,2,1,0:T(8,128)}, f32[10,2,32,128]{3,2,1,0:T(8,128)S(1)}, u32[]{:S(2)}, u32[]{:S(2)}) collective-permute-start(f32[10,2,32,128]{3,2,1,0:T(8,128)} %get-tuple-element.15), channel_id=1, source_target_pairs={{0,8},{1,9},{2,10},{3,11},{4,12},{5,13},{6,14},{7,15},{8,0},{9,1},... | collective-permute-start | bytes 983048 | tf_op jit(solution)/shard_map/ppermute | solution.py:433
  6.2 8.9 %collective-permute-start.3 = (f32[10,2,32,128]{3,2,1,0:T(8,128)}, f32[10,2,32,128]{3,2,1,0:T(8,128)S(1)}, u32[]{:S(2)}, u32[]{:S(2)}) collective-permute-start(f32[10,2,32,128]{3,2,1,0:T(8,128)} %get-tuple-element.16), channel_id=1, source_target_pairs={{0,1},{1,0},{2,3},{3,2},{4,5},{5,4},{6,7},{7,6},{8,16},{9,17},{10,... | collective-permute-start | bytes 983048 | tf_op jit(solution)/shard_map/ppermute | solution.py:434
  6.2 4.0 %copy-start.2 = (s32[1,2,8,6]{2,1,3,0:T(2,128)S(1)}, s32[1,2,8,6]{2,1,3,0:T(2,128)}, u32[]{:S(2)}) copy-start(s32[1,2,8,6]{2,1,3,0:T(2,128)} %param.11) | copy-start | bytes 1156
  6.2 4.0 %copy-start.3 = (s32[1,2,8]{2,1,0:T(2,128)S(1)}, s32[1,2,8]{2,1,0:T(2,128)}, u32[]{:S(2)}) copy-start(s32[1,2,8]{2,1,0:T(2,128)} %refine.1) | copy-start | bytes 196
  6.2 4.0 %copy-start.4 = (s32[1,2,8]{2,1,0:T(2,128)S(1)}, s32[1,2,8]{2,1,0:T(2,128)}, u32[]{:S(2)}) copy-start(s32[1,2,8]{2,1,0:T(2,128)} %owner.1) | copy-start | bytes 196
  6.2 4.0 %copy-start.5 = (s32[1,2,8]{2,1,0:T(2,128)S(1)}, s32[1,2,8]{2,1,0:T(2,128)}, u32[]{:S(2)}) copy-start(s32[1,2,8]{2,1,0:T(2,128)} %weight.1) | copy-start | bytes 196
  6.2 10.4 %collective-permute-start.4 = (f32[10,16,4,128]{3,2,1,0:T(4,128)}, f32[10,16,4,128]{3,2,1,0:T(4,128)S(1)}, u32[]{:S(2)}, u32[]{:S(2)}) collective-permute-start(f32[10,16,4,128]{3,2,1,0:T(4,128)} %get-tuple-element.17), channel_id=1, source_target_pairs={{0,4},{4,0},{1,5},{5,1},{2,6},{6,2},{3,7},{7,3},{8,12},{12,8},{9,1... | collective-permute-start | bytes 983048 | tf_op jit(solution)/shard_map/ppermute | solution.py:431
  8.6 4.0 %collective-permute-start = (f32[10,2,8,128]{3,2,1,0:T(8,128)S(1)}, f32[10,2,8,128]{3,2,1,0:T(8,128)S(1)}, u32[]{:S(2)}, u32[]{:S(2)}) collective-permute-start(f32[10,2,8,128]{3,2,1,0:T(8,128)S(1)} %lanes.1.ax_s), channel_id=1, source_target_pairs={{0,1},{1,0},{2,3},{3,2},{4,5},{5,4},{6,7},{7,6},{8,9},{9,8},{10,11... | collective-permute-start | bytes 245768 | tf_op jit(solution)/shard_map/ppermute | solution.py:429
  8.8 4.3 %collective-permute-start.1 = (f32[10,2,8,128]{3,2,1,0:T(8,128)S(1)}, f32[10,2,8,128]{3,2,1,0:T(8,128)S(1)}, u32[]{:S(2)}, u32[]{:S(2)}) collective-permute-start(f32[10,2,8,128]{3,2,1,0:T(8,128)S(1)} %lanes.1.ax_s), channel_id=1, source_target_pairs={{0,3},{1,2},{2,1},{3,0},{4,7},{5,6},{6,5},{7,4},{8,11},{9,10},{10,... | collective-permute-start | bytes 245768 | tf_op jit(solution)/shard_map/ppermute | solution.py:430

commit v5 on v4

--- a/solution.py
+++ b/solution.py
@@ -165,7 +165,7 @@
     )
 
 
-def axial_kernel(dims, n_ax, sums, fourth, ax_a, ax_b, bw, got, lhs, rhs, far):
+def axial_kernel(dims, n_ax, sums, fourth, part_bw, ax_a, ax_b, bw, done, got, lhs, rhs, far, far_w):
     nr, na, nx = dims
     i_ax = lax.axis_index("ax")
     even_ax = lax.rem(i_ax, 2) == 0
@@ -208,113 +208,251 @@
 
     lax.fori_loop(0, 2 * F, build, 0)
     far[...] = jnp.dot(lhs[0:F * size, :], rhs[:, 0:2 * nx], preferred_element_type=jnp.float32)
-    bw[F:2 * F] = (
-        fourth[...]
-        + jnp.dot(
-            lhs[F * size:2 * F * size, :], rhs[:, 2 * nx:3 * nx], preferred_element_type=jnp.float32
-        )
-    ).reshape(F, nr, na, nx)
+    far_w[...] = jnp.dot(
+        lhs[F * size:2 * F * size, :], rhs[:, 2 * nx:3 * nx], preferred_element_type=jnp.float32
+    )
+
+    def tile(r, a, whole):
+        mine = pl.ds(8 * a, 8)
+        at = [pl.ds(f * size + r * na + 8 * a, 8) for f in range(F)]
+        up = flux([sums[q, 0:nx] + far[q, 0:nx] for q in at], 2)
+        low = flux([sums[q, nx:2 * nx] + far[q, nx:2 * nx] for q in at], 2)
+        total = None
+        for f in range(F):
+            bal = part_bw[f, r, mine, :] + (up[f] - low[f])
+            w = part_bw[F + f, r, mine, :] + (fourth[at[f], :] + far_w[at[f], :])
+            if whole:
+                total = w * bal if total is None else total + w * bal
+            else:
+                bw[f, r, mine, :] = bal
+                bw[F + f, r, mine, :] = w
+        if whole:
+            done[r, mine, :] = jnp.abs(total) * (1.0 / 144.0)
 
     def body(r, carry):
         for a in range(tiles):
-            at = [pl.ds(f * size + pl.multiple_of(r * na, na) + 8 * a, 8) for f in range(F)]
-            up = flux([sums[q, 0:nx] + far[q, 0:nx] for q in at], 2)
-            low = flux([sums[q, nx:2 * nx] + far[q, nx:2 * nx] for q in at], 2)
-            for f in range(F):
-                bw[f, r, pl.ds(8 * a, 8), :] = up[f] - low[f]
+            tile(r, a, 0 < a < tiles - 1)
         return carry
 
-    lax.fori_loop(0, nr, body, 0)
-
-
-def main_kernel(
-    dims, n_rad, prim, adj, bw, rad_a, rad_b, azi_l, azi_r, row, ind, send, far, low, top, frad, fazi
-):
+    for r in (0, 1, nr - 2, nr - 1):
+        for a in range(tiles):
+            tile(r, a, False)
+    lax.fori_loop(2, nr - 2, body, 0)
+
+
+def shifted(src, f, r, a, tiles, da):
+    if da < 0 and a == 0 or da > 0 and a == tiles - 1:
+        return pltpu.roll(src[f, r, pl.ds(8 * a, 8), :], -da % 8, 0)
+    return src[f, r, pl.ds(8 * a + da, 8), :]
+
+
+def inner_kernel(dims, prim, adj, dep, bw, frad, fazi):
+    del dep
     nr, na, nx = dims
-    i_rad = lax.axis_index("rad")
-    odd = lax.rem(i_rad, 2)
     tiles = na // 8
-    last = 8 * (tiles - 1)
-    lane = lax.broadcasted_iota(jnp.int32, (8, nx), 1)
-    for f in range(2 * F):
-        for i in range(2):
-            a, b = rad_a[f, i], rad_b[f, i]
-            far[f, i] = jnp.where(i_rad == 0, 0.0, jnp.where(odd == 0, b, a))
-            far[f, 2 + i] = jnp.where(i_rad == n_rad - 1, 0.0, jnp.where(odd == 0, a, b))
-
-    def edges(r, carry):
-        for t, src in enumerate((prim, adj)):
-            for f in range(F):
-                g = t * F + f
-                low[g, r, 14:16, :] = azi_l[g, r, 2:4, :]
-                low[g, r, 16:24, :] = src[f, r, 0:8, :]
-                top[g, r, 0:8, :] = src[f, r, last:last + 8, :]
-                top[g, r, 8:10, :] = azi_r[g, r, 0:2, :]
-        return carry
-
-    lax.fori_loop(0, nr, edges, 0)
-
-    def cell(g, r, a, dr=0, da=0):
-        if isinstance(r, int):
-            if r + dr < 0:
-                return far[g, 2 + r + dr, pl.ds(8 * a, 8), :]
-            if r + dr >= nr:
-                return far[g, 2 + r + dr - nr, pl.ds(8 * a, 8), :]
-        if da < 0 and a == 0:
-            return low[g, r, pl.ds(16 + da, 8), :]
-        if da > 0 and a == tiles - 1:
-            return top[g, r, pl.ds(da, 8), :]
-        src = (prim, adj)[g // F]
-        return src[g % F, r + dr, pl.ds(8 * a + da, 8), :]
+    sub = lax.broadcasted_iota(jnp.int32, (8, nx), 0)
+    zero = jnp.zeros((8, nx), jnp.float32)
 
     def rad_flux(r, a):
-        return flux([face(*(cell(f, r, a, dr=o) for o in (-1, 0, 1, 2))) for f in range(F)], 0)
+        rows = pl.ds(8 * a, 8)
+        return flux([face(*(prim[f, r + o, rows, :] for o in (-1, 0, 1, 2))) for f in range(F)], 0)
 
     def azi_flux(r, a):
-        return flux([face(*(cell(f, r, a, da=o) for o in (-1, 0, 1, 2))) for f in range(F)], 1)
-
-    def low_flux(r):
-        return flux([face(*(low[f, r, pl.ds(8 + o, 8), :] for o in (-1, 0, 1, 2))) for f in range(F)], 1)
-
-    for a in range(tiles):
-        for f, x in enumerate(rad_flux(-1, a)):
-            frad[f, a] = x
-
-    def plane(r, sums):
-        for f, x in enumerate(low_flux(r)):
-            fazi[f, 0:8, :] = x
+        x = flux([face(*(shifted(prim, f, r, a, tiles, o) for o in (-1, 0, 1, 2))) for f in range(F)], 1)
+        if a == 0:
+            x = [jnp.where(sub < 1, 0.0, t) for t in x]
+        if a == tiles - 1:
+            x = [jnp.where(sub > 5, 0.0, t) for t in x]
+        return x
+
+    for f in range(F):
+        fazi[f, 0:8, :] = zero
+
+    def plane(r, carry):
+        here = not isinstance(r, int) or 1 <= r <= nr - 3
+        before = not isinstance(r, int) or 1 <= r - 1 <= nr - 3
         for a in range(tiles):
             for f, x in enumerate(azi_flux(r, a)):
                 fazi[f, pl.ds(8 + 8 * a, 8), :] = x
+        for a in range(tiles):
+            mine = pl.ds(8 * a, 8)
+            up = rad_flux(r, a) if here else None
+            for f in range(F):
+                bal = fazi[f, pl.ds(8 * a + 8, 8), :] - fazi[f, pl.ds(8 * a + 7, 8), :]
+                if before:
+                    bal = bal - frad[f, a]
+                if here:
+                    bal = bal + up[f]
+                    frad[f, a] = up[f]
+                bw[f, r, mine, :] = bal
+
+                def row(da):
+                    x = shifted(adj, f, r, a, tiles, da)
+                    if da < 0 and a == 0:
+                        x = jnp.where(sub < -da, 0.0, x)
+                    if da > 0 and a == tiles - 1:
+                        x = jnp.where(sub > 7 - da, 0.0, x)
+                    return x
+
+                def layer(dr):
+                    if isinstance(r, int) and not 0 <= r + dr < nr:
+                        return None
+                    return adj[f, r + dr, mine, :]
+
+                two, one = row(-2) + row(2), row(-1) + row(1)
+                for dr in (-2, 2):
+                    x = layer(dr)
+                    two = two if x is None else two + x
+                for dr in (-1, 1):
+                    x = layer(dr)
+                    one = one if x is None else one + x
+                bw[F + f, r, mine, :] = two - 4.0 * one + 12.0 * adj[f, r, mine, :]
+        return carry
+
+    for r in (0, 1):
+        plane(r, 0)
+    lax.fori_loop(2, nr - 2, plane, 0)
+    for r in (nr - 2, nr - 1):
+        plane(r, 0)
+
+
+def edge_terms(dims, n_rad, prim, adj, rad_a, rad_b, azi_l, azi_r):
+    nr, na, nx = dims
+    i_rad = lax.axis_index("rad")
+    odd = lax.rem(i_rad, 2) == 1
+    tiles = na // 8
+    sub = lax.broadcasted_iota(jnp.int32, (8, nx), 0)
+
+    def before(g, i, rows):
+        return jnp.where(i_rad == 0, 0.0, jnp.where(odd, rad_a[g, i, rows, :], rad_b[g, i, rows, :]))
+
+    def after(g, i, rows):
+        x = jnp.where(odd, rad_b[g, i, rows, :], rad_a[g, i, rows, :])
+        return jnp.where(i_rad == n_rad - 1, 0.0, x)
+
+    def radial(a):
+        rows = pl.ds(8 * a, 8)
+        low, high = [], []
+        for f in range(F):
+            b0, b1, h0, h1 = (before(f, 0, rows), before(f, 1, rows), after(f, 0, rows), after(f, 1, rows))
+            u0, u1, u2 = (prim[f, i, rows, :] for i in range(3))
+            v2, v1, v0 = (prim[f, nr - i, rows, :] for i in (3, 2, 1))
+            low.append((face(b0, b1, u0, u1), face(b1, u0, u1, u2)))
+            high.append((face(v2, v1, v0, h0), face(v1, v0, h0, h1)))
+        p, q = (flux([x[i] for x in low], 0) for i in range(2))
+        s, t = (flux([x[i] for x in high], 0) for i in range(2))
+        bal = {
+            0: [y - x for x, y in zip(p, q)],
+            1: [-y for y in q],
+            nr - 2: s,
+            nr - 1: [y - x for x, y in zip(s, t)],
+        }
+        w = {0: [], 1: [], nr - 2: [], nr - 1: []}
+        for f in range(F):
+            g = F + f
+            b0, b1, h0, h1 = (before(g, 0, rows), before(g, 1, rows), after(g, 0, rows), after(g, 1, rows))
+            w[0].append(b0 - 4.0 * b1)
+            w[1].append(b1)
+            w[nr - 2].append(h0)
+            w[nr - 1].append(h1 - 4.0 * h0)
+        return bal, w
+
+    def azimuthal(r, a):
+        if a == 0:
+            def layer(g, i):
+                return jnp.broadcast_to(azi_l[g, r, 2 + i:3 + i, :], (8, nx))
+
+            s = []
+            for f in range(F):
+                x = prim[f, r, 0:8, :]
+                l0, l1 = layer(f, 0), layer(f, 1)
+                s.append(
+                    face(
+                        jnp.where(sub == 0, l0, jnp.where(sub == 1, l1, pltpu.roll(x, 2, 0))),
+                        jnp.where(sub == 0, l1, pltpu.roll(x, 1, 0)),
+                        x,
+                        prim[f, r, 1:9, :],
+                    )
+                )
+            bal = [
+                jnp.where(sub == 0, pltpu.roll(x, 7, 0) - x, jnp.where(sub == 1, -x, 0.0))
+                for x in flux(s, 1)
+            ]
+            w = []
+            for f in range(F):
+                l0, l1 = layer(F + f, 0), layer(F + f, 1)
+                w.append(jnp.where(sub == 0, l0 - 4.0 * l1, jnp.where(sub == 1, l1, 0.0)))
+            return bal, w
+
+        def layer(g, i):
+            return jnp.broadcast_to(azi_r[g, r, i:i + 1, :], (8, nx))
+
+        s = []
+        for f in range(F):
+            x = prim[f, r, na - 8:na, :]
+            h0, h1 = layer(f, 0), layer(f, 1)
+            s.append(
+                face(
+                    prim[f, r, na - 9:na - 1, :],
+                    x,
+                    jnp.where(sub == 7, h0, pltpu.roll(x, 7, 0)),
+                    jnp.where(sub == 7, h1, jnp.where(sub == 6, h0, pltpu.roll(x, 6, 0))),
+                )
+            )
+        bal = [
+            jnp.where(sub == 7, x - pltpu.roll(x, 1, 0), jnp.where(sub == 6, x, 0.0)) for x in flux(s, 1)
+        ]
+        w = []
+        for f in range(F):
+            h0, h1 = layer(F + f, 0), layer(F + f, 1)
+            w.append(jnp.where(sub == 7, h1 - 4.0 * h0, jnp.where(sub == 6, h0, 0.0)))
+        return bal, w
+
+    return radial, azimuthal
+
+
+def main_kernel(dims, n_rad, prim, adj, bw, done, rad_a, rad_b, azi_l, azi_r, row, ind, send):
+    nr, na, nx = dims
+    tiles = na // 8
+    lane = lax.broadcasted_iota(jnp.int32, (8, nx), 1)
+    radial, azimuthal = edge_terms(dims, n_rad, prim, adj, rad_a, rad_b, azi_l, azi_r)
+
+    def outer(r, a, extra):
+        mine = pl.ds(8 * a, 8)
+        bal = [bw[f, r, mine, :] for f in range(F)]
+        w = [bw[F + f, r, mine, :] for f in range(F)]
+        for more_bal, more_w in extra:
+            bal = [x + y for x, y in zip(bal, more_bal)]
+            w = [x + y for x, y in zip(w, more_w)]
+        total = w[0] * bal[0]
+        for f in range(1, F):
+            total = total + w[f] * bal[f]
+        total = jnp.abs(total) * (1.0 / 144.0)
+        ind[r, mine, :] = total
+        return total
+
+    ends = (0, 1, nr - 2, nr - 1)
+    sums = [jnp.zeros((8, nx), jnp.float32) for _ in range(tiles)]
+    for a in range(tiles):
+        bal, w = radial(a)
+        for r in ends:
+            extra = [(bal[r], w[r])]
+            if a in (0, tiles - 1):
+                extra.append(azimuthal(r, a))
+            sums[a] = sums[a] + outer(r, a, extra)
+
+    def plane(r, sums):
         out = []
         for a in range(tiles):
-            mine = pl.ds(8 * a, 8)
-            up = rad_flux(r, a)
-            total = None
-            for f in range(F):
-                bal = bw[f, r, mine, :] + (up[f] - frad[f, a])
-                frad[f, a] = up[f]
-                bal = bal + (fazi[f, pl.ds(8 * a + 8, 8), :] - fazi[f, pl.ds(8 * a + 7, 8), :])
-                g = F + f
-                two = (cell(g, r, a, dr=-2) + cell(g, r, a, dr=2)) + (
-                    cell(g, r, a, da=-2) + cell(g, r, a, da=2)
-                )
-                one = (cell(g, r, a, dr=-1) + cell(g, r, a, dr=1)) + (
-                    cell(g, r, a, da=-1) + cell(g, r, a, da=1)
-                )
-                w = (two - 4.0 * one + 12.0 * cell(g, r, a) + bw[g, r, mine, :]) * bal
-                total = w if total is None else total + w
-            total = jnp.abs(total) * (1.0 / 144.0)
-            ind[r, mine, :] = total
-            out.append(sums[a] + total)
+            if a in (0, tiles - 1):
+                x = outer(r, a, [azimuthal(r, a)])
+            else:
+                x = done[r, pl.ds(8 * a, 8), :]
+                ind[r, pl.ds(8 * a, 8), :] = x
+            out.append(sums[a] + x)
         return tuple(out)
 
-    sums = tuple(jnp.zeros((8, nx), jnp.float32) for _ in range(tiles))
-    for r in (0, 1):
-        sums = plane(r, sums)
-    sums = lax.fori_loop(2, nr - 2, plane, sums)
-    for r in (nr - 2, nr - 1):
-        sums = plane(r, sums)
+    sums = lax.fori_loop(2, nr - 2, plane, tuple(sums))
 
     groups = nx // BLK
     halves_a = na // BLK
@@ -449,36 +587,42 @@
         compiler_params=pltpu.CompilerParams(vmem_limit_bytes=16 << 20),
         name="own",
     )(primal, adjoint, ax_s, near, refine_flag, owner_map, migrate_weight)
-    bw = pl.pallas_call(
+    part_bw = pl.pallas_call(
+        functools.partial(inner_kernel, dims),
+        out_shape=f32((2 * F, nr, na, nx)),
+        in_specs=[vmem] * 3,
+        out_specs=vmem,
+        scratch_shapes=[
+            pltpu.VMEM((F, tiles, 8, nx), jnp.float32),
+            pltpu.VMEM((F, 8 + na, nx), jnp.float32),
+        ],
+        compiler_params=pltpu.CompilerParams(vmem_limit_bytes=16 << 20),
+        name="inner",
+    )(primal, adjoint, row)
+    bw, done = pl.pallas_call(
         functools.partial(axial_kernel, dims, n_ax),
-        out_shape=f32((2 * F, nr, na, nx)),
-        in_specs=[vmem] * 4,
-        out_specs=vmem,
+        out_shape=(f32((2 * F, nr, na, nx)), f32(dims)),
+        in_specs=[vmem] * 5,
+        out_specs=(vmem, vmem),
         scratch_shapes=[
             pltpu.VMEM((3, 2 * F, halves, 8, nx), jnp.float32),
             pltpu.VMEM((2 * cells, nx), jnp.bfloat16),
             pltpu.VMEM((nx, 3 * nx), jnp.bfloat16),
             pltpu.VMEM((cells, 2 * nx), jnp.float32),
+            pltpu.VMEM((cells, nx), jnp.float32),
         ],
         compiler_params=pltpu.CompilerParams(vmem_limit_bytes=16 << 20),
         name="axial",
-    )(sums, fourth, ax_a, ax_b)
+    )(sums, fourth, part_bw, ax_a, ax_b)
 
     indicator, send = pl.pallas_call(
         functools.partial(main_kernel, dims, n_rad),
         out_shape=(f32(dims), f32((2 * n_dev, nx))),
-        in_specs=[vmem] * 8,
+        in_specs=[vmem] * 9,
         out_specs=(vmem, vmem),
-        scratch_shapes=[
-            pltpu.VMEM((2 * F, 4, na, nx), jnp.float32),
-            pltpu.VMEM((2 * F, nr, 24, nx), jnp.float32),
-            pltpu.VMEM((2 * F, nr, 16, nx), jnp.float32),
-            pltpu.VMEM((F, tiles, 8, nx), jnp.float32),
-            pltpu.VMEM((F, 8 + na, nx), jnp.float32),
-        ],
-        compiler_params=pltpu.CompilerParams(vmem_limit_bytes=32 << 20),
+        compiler_params=pltpu.CompilerParams(vmem_limit_bytes=16 << 20),
         name="stencil",
-    )(primal, adjoint, bw, rad_a, rad_b, azi_l, azi_r, row)
+    )(primal, adjoint, bw, done, rad_a, rad_b, azi_l, azi_r, row)
 
     data = lax.all_to_all(send, AXES, 0, 0, tiled=True)
 

time: 33.1 us -> 31 us (0.937)
  waiting for transfers between devices: 2.14 us -> 0.28 us
    pallas_call x1, Pallas kernels: 3.66 us -> 1.62 us  [on_device(): pl.pallas_call(functools.partial(main_kernel, dims, n_rad), out_shape=(f3...]
    pallas_call x1 -> x2, Pallas kernels: 1.9 us -> 3.76 us  [the longest x1 1.96 us: on_device(): pl.pallas_call(functools.partial(axial_kernel, dims, n_ax), out_shape=(f3...]
    ppermute x1, waiting for transfers between devices: 1.5 us -> 0.27 us  [on_device(): azi_l = lax.ppermute(azi_s, 'azi', ring(n_azi, 1))]
    ppermute x1, waiting for transfers between devices: 0.63 us -> 0.01 us  [on_device(): ax_b = lax.ppermute(ax_s, AXES, pair_round(sizes, 2, 1))]
  transfers between devices with their start and end apart: 5 -> 5, of which waited for: 2 -> 1; matrix products, arithmetic and copies ran while one was open for 0% -> 0% of each run, Pallas kernels for 15% -> 22%
where the time goes in v5:
time: 31 us; the launch traced here: 30.9 us
  Pallas kernels  11.8 us (38%)
  blocking collectives  11.8 us (38%)
  starting transfers between devices  6.28 us (20%)
  between operations  0.75 us (2%)
    all_to_all x1, blocking collectives, on_device(): data = lax.all_to_all(send, AXES, 0, 0, tiled=True)  11.8 us
    ppermute x1, starting transfers between devices, on_device(): rad_a = lax.ppermute(rad_a, AXES, pair_round(sizes, 0, 0))  3.09 us
    pallas_call x1, Pallas kernels, on_device(): pl.pallas_call(functools.partial(edge_kernel, dims), out_shape=(f32((2 *...  2.46 us
    pallas_call x1, Pallas kernels, on_device(): pl.pallas_call(functools.partial(own_kernel, dims, ((per_rad, per_azi, pe...  2.29 us
    pallas_call x1, Pallas kernels, on_device(): pl.pallas_call(functools.partial(axial_kernel, dims, n_ax), out_shape=(f3...  1.96 us
    pallas_call x1, Pallas kernels, on_device(): pl.pallas_call(functools.partial(inner_kernel, dims), out_shape=f32((2 *...  1.8 us
    pallas_call x1, Pallas kernels, on_device(): pl.pallas_call(functools.partial(main_kernel, dims, n_rad), out_shape=(f3...  1.62 us
    ppermute x1, starting transfers between devices, on_device(): azi_l = lax.ppermute(azi_s, 'azi', ring(n_azi, 1))  1.52 us
  transfers between devices with their start and end apart: 5, of which 1 were waited for; matrix products, arithmetic and copies ran while one was open for 0% of the time, Pallas kernels for 22%

profile of v5, /device:TPU:0, one launch (start us, length us, event | category | flops | bytes accessed | tf_op | source)
XLA Modules:
  0.0 30.9 jit_solution(9305638437563847978)
XLA Ops:
  0.6 0.0 copy-start
  0.6 0.0 copy-start.1
  0.7 0.0 copy-start.2
  0.7 0.0 copy-start.5
  0.7 0.0 copy-start.3
  0.7 0.0 copy-start.4
  0.7 2.5 %edges.1 = (f32[10,2,32,128]{3,2,1,0:T(8,128)}, f32[10,2,32,128]{3,2,1,0:T(8,128)}, f32[10,16,4,128]{3,2,1,0:T(4,128)}) custom-call(f32[5,16,32,128]{3,2,1,0:T(8,128)} %prim.9, f32[5,16,32,128]{3,2,1,0:T(8,128)} %adj.9), custom_call_target="tpu_custom_call" | custom-call | tf_op jit(solution)/shard_map/edges/pallas_call | solution.py:549
  3.2 3.1 %collective-permute-start.2 = (f32[10,2,32,128]{3,2,1,0:T(8,128)}, f32[10,2,32,128]{3,2,1,0:T(8,128)S(1)}, u32[]{:S(2)}, u32[]{:S(2)}) collective-permute-start(f32[10,2,32,128]{3,2,1,0:T(8,128)} %get-tuple-element.20), channel_id=1, source_target_pairs={{0,8},{1,9},{2,10},{3,11},{4,12},{5,13},{6,14},{7,15},{8,0},{9,1},... | collective-permute-start | bytes 983048 | tf_op jit(solution)/shard_map/ppermute | solution.py:571
  6.2 0.0 collective-permute-start.3
  6.2 1.5 %collective-permute-start.4 = (f32[10,16,4,128]{3,2,1,0:T(4,128)}, f32[10,16,4,128]{3,2,1,0:T(4,128)S(1)}, u32[]{:S(2)}, u32[]{:S(2)}) collective-permute-start(f32[10,16,4,128]{3,2,1,0:T(4,128)} %get-tuple-element.22), channel_id=1, source_target_pairs={{0,4},{4,0},{1,5},{5,1},{2,6},{6,2},{3,7},{7,3},{8,12},{12,8},{9,1... | collective-permute-start | bytes 983048 | tf_op jit(solution)/shard_map/ppermute | solution.py:569
  7.8 0.0 copy-done
  7.8 0.0 copy-done.1
  7.8 0.7 %lanes.1.ax_s = f32[10,2,8,128]{3,2,1,0:T(8,128)S(1)} custom-call(f32[5,16,32,128]{3,2,1,0:T(8,128)S(1)} %copy-done, f32[5,16,32,128]{3,2,1,0:T(8,128)S(1)} %copy-done.1), custom_call_target="tpu_custom_call" | custom-call | tf_op jit(solution)/shard_map/lanes/pallas_call | solution.py:558
  8.5 0.3 collective-permute-start
  8.8 1.4 %collective-permute-start.1 = (f32[10,2,8,128]{3,2,1,0:T(8,128)S(1)}, f32[10,2,8,128]{3,2,1,0:T(8,128)S(1)}, u32[]{:S(2)}, u32[]{:S(2)}) collective-permute-start(f32[10,2,8,128]{3,2,1,0:T(8,128)S(1)} %lanes.1.ax_s), channel_id=1, source_target_pairs={{0,3},{1,2},{2,1},{3,0},{4,7},{5,6},{6,5},{7,4},{8,11},{9,10},{10,... | collective-permute-start | bytes 245768 | tf_op jit(solution)/shard_map/ppermute | solution.py:568
  10.2 0.0 copy-done.2
  10.2 0.0 copy-done.5
  10.2 0.0 copy-done.3
  10.2 0.0 copy-done.4
  10.2 2.3 %own.1 = (f32[2560,256]{1,0:T(8,128)S(1)}, f32[2560,128]{1,0:T(8,128)S(1)}, f32[1,256]{1,0:T(1,128)S(1)}) custom-call(f32[5,16,32,128]{3,2,1,0:T(8,128)S(1)} %copy-done, f32[5,16,32,128]{3,2,1,0:T(8,128)S(1)} %copy-done.1, f32[10,2,8,128]{3,2,1,0:T(8,128)S(1)} %lanes.1.ax_s, s32[1,6,2,8]{3,2,1,0:T(2,128)S(1)} %bitcast.5, s32[1,2,8]{2,1,0:T(2,128)S(1)} %copy-done.3, ...), custom_call_target="tpu_custom_call" | custom-call | tf_op jit(solution)/shard_map/own/pallas_call | solution.py:578
  12.5 1.8 %inner.1.part_bw = f32[10,16,32,128]{3,2,1,0:T(8,128)S(1)} custom-call(f32[5,16,32,128]{3,2,1,0:T(8,128)S(1)} %copy-done, f32[5,16,32,128]{3,2,1,0:T(8,128)S(1)} %copy-done.1, f32[1,256]{1,0:T(1,128)S(1)} %get-tuple-element.17.dep.row), custom_call_target="tpu_custom_call" | custom-call | tf_op jit(solution)/shard_map/inner/pallas_call | solution.py:590
  14.3 0.0 collective-permute-done.ax_a
  14.3 0.0 collective-permute-done.1.ax_b
  14.3 2.0 %axial.1 = (f32[10,16,32,128]{3,2,1,0:T(8,128)S(1)}, f32[16,32,128]{2,1,0:T(8,128)S(1)}) custom-call(f32[2560,256]{1,0:T(8,128)S(1)} %get-tuple-element.15.sums, f32[2560,128]{1,0:T(8,128)S(1)} %get-tuple-element.16.fourth, f32[10,16,32,128]{3,2,1,0:T(8,128)S(1)} %inner.1.part_bw, f32[10,2,8,128]{3,2,1,0:T(8,128)S(1)} %collective-permute-done.ax_a, ...), custom_call_target="tpu_custom_call" | custom-call | tf_op jit(solution)/shard_map/axial/pallas_call | solution.py:602
  16.3 0.0 collective-permute-done.2.rad_a
  16.3 0.0 collective-permute-done.3.rad_b
  16.3 0.3 collective-permute-done.4.azi_l.azi_r
  16.6 1.6 %stencil.1 = (f32[16,32,128]{2,1,0:T(8,128)}, f32[64,128]{1,0:T(8,128)S(1)}) custom-call(f32[5,16,32,128]{3,2,1,0:T(8,128)S(1)} %copy-done, f32[5,16,32,128]{3,2,1,0:T(8,128)S(1)} %copy-done.1, f32[10,16,32,128]{3,2,1,0:T(8,128)S(1)} %get-tuple-element.18.bw, f32[16,32,128]{2,1,0:T(8,128)S(1)} %get-tuple-element.19.done, ...), custom_call_target="tpu_custom_call" | custom-call | tf_op jit(solution)/shard_map/stencil/pallas_call | solution.py:618
  18.2 11.8 %all_to_all.11 = f32[32,2,128]{2,1,0:T(2,128)S(1)} all-to-all(f32[32,2,128]{2,1,0:T(2,128)S(1)} %bitcast.4), channel_id=1, replica_groups=mesh['rad'=4,'azi'=2,'ax'=4] {'rad','azi','ax'}, dimensions={0} | all-to-all | bytes 65536 | tf_op jit(solution)/shard_map/all_to_all | solution.py:627
  30.0 0.9 %blocks.1 = (f32[1,2,8]{2,1,0:T(2,128)}, f32[1,1,1]{2,1,0:T(1,128)}) custom-call(f32[64,128]{1,0:T(8,128)S(1)} %bitcast.3), custom_call_target="tpu_custom_call" | custom-call | tf_op jit(solution)/shard_map/blocks/pallas_call | solution.py:629
Async XLA Ops:
  0.6 7.1 %copy-start = (f32[5,16,32,128]{3,2,1,0:T(8,128)S(1)}, f32[5,16,32,128]{3,2,1,0:T(8,128)}, u32[]{:S(2)}) copy-start(f32[5,16,32,128]{3,2,1,0:T(8,128)} %prim.9) | copy-start | bytes 3932164
  0.6 7.1 %copy-start.1 = (f32[5,16,32,128]{3,2,1,0:T(8,128)S(1)}, f32[5,16,32,128]{3,2,1,0:T(8,128)}, u32[]{:S(2)}) copy-start(f32[5,16,32,128]{3,2,1,0:T(8,128)} %adj.9) | copy-start | bytes 3932164
  0.7 9.5 %copy-start.2 = (s32[1,2,8,6]{2,1,3,0:T(2,128)S(1)}, s32[1,2,8,6]{2,1,3,0:T(2,128)}, u32[]{:S(2)}) copy-start(s32[1,2,8,6]{2,1,3,0:T(2,128)} %param.11) | copy-start | bytes 1156
  0.7 9.5 %copy-start.5 = (s32[1,2,8]{2,1,0:T(2,128)S(1)}, s32[1,2,8]{2,1,0:T(2,128)}, u32[]{:S(2)}) copy-start(s32[1,2,8]{2,1,0:T(2,128)} %weight.1) | copy-start | bytes 196
  0.7 9.5 %copy-start.3 = (s32[1,2,8]{2,1,0:T(2,128)S(1)}, s32[1,2,8]{2,1,0:T(2,128)}, u32[]{:S(2)}) copy-start(s32[1,2,8]{2,1,0:T(2,128)} %refine.1) | copy-start | bytes 196
  0.7 9.5 %copy-start.4 = (s32[1,2,8]{2,1,0:T(2,128)S(1)}, s32[1,2,8]{2,1,0:T(2,128)}, u32[]{:S(2)}) copy-start(s32[1,2,8]{2,1,0:T(2,128)} %owner.1) | copy-start | bytes 196
  3.2 13.1 %collective-permute-start.2 = (f32[10,2,32,128]{3,2,1,0:T(8,128)}, f32[10,2,32,128]{3,2,1,0:T(8,128)S(1)}, u32[]{:S(2)}, u32[]{:S(2)}) collective-permute-start(f32[10,2,32,128]{3,2,1,0:T(8,128)} %get-tuple-element.20), channel_id=1, source_target_pairs={{0,8},{1,9},{2,10},{3,11},{4,12},{5,13},{6,14},{7,15},{8,0},{9,1},... | collective-permute-start | bytes 983048 | tf_op jit(solution)/shard_map/ppermute | solution.py:571
  6.2 10.1 %collective-permute-start.3 = (f32[10,2,32,128]{3,2,1,0:T(8,128)}, f32[10,2,32,128]{3,2,1,0:T(8,128)S(1)}, u32[]{:S(2)}, u32[]{:S(2)}) collective-permute-start(f32[10,2,32,128]{3,2,1,0:T(8,128)} %get-tuple-element.21), channel_id=1, source_target_pairs={{0,1},{1,0},{2,3},{3,2},{4,5},{5,4},{6,7},{7,6},{8,16},{9,17},{10,... | collective-permute-start | bytes 983048 | tf_op jit(solution)/shard_map/ppermute | solution.py:572
  6.2 10.3 %collective-permute-start.4 = (f32[10,16,4,128]{3,2,1,0:T(4,128)}, f32[10,16,4,128]{3,2,1,0:T(4,128)S(1)}, u32[]{:S(2)}, u32[]{:S(2)}) collective-permute-start(f32[10,16,4,128]{3,2,1,0:T(4,128)} %get-tuple-element.22), channel_id=1, source_target_pairs={{0,4},{4,0},{1,5},{5,1},{2,6},{6,2},{3,7},{7,3},{8,12},{12,8},{9,1... | collective-permute-start | bytes 983048 | tf_op jit(solution)/shard_map/ppermute | solution.py:569
  8.5 5.8 %collective-permute-start = (f32[10,2,8,128]{3,2,1,0:T(8,128)S(1)}, f32[10,2,8,128]{3,2,1,0:T(8,128)S(1)}, u32[]{:S(2)}, u32[]{:S(2)}) collective-permute-start(f32[10,2,8,128]{3,2,1,0:T(8,128)S(1)} %lanes.1.ax_s), channel_id=1, source_target_pairs={{0,1},{1,0},{2,3},{3,2},{4,5},{5,4},{6,7},{7,6},{8,9},{9,8},{10,11... | collective-permute-start | bytes 245768 | tf_op jit(solution)/shard_map/ppermute | solution.py:567
  8.8 5.5 %collective-permute-start.1 = (f32[10,2,8,128]{3,2,1,0:T(8,128)S(1)}, f32[10,2,8,128]{3,2,1,0:T(8,128)S(1)}, u32[]{:S(2)}, u32[]{:S(2)}) collective-permute-start(f32[10,2,8,128]{3,2,1,0:T(8,128)S(1)} %lanes.1.ax_s), channel_id=1, source_target_pairs={{0,3},{1,2},{2,1},{3,0},{4,7},{5,6},{6,5},{7,4},{8,11},{9,10},{10,... | collective-permute-start | bytes 245768 | tf_op jit(solution)/shard_map/ppermute | solution.py:568

commit v6 on v5

--- a/solution.py
+++ b/solution.py
@@ -552,9 +552,9 @@
         in_specs=[hbm, hbm],
         out_specs=(vmem, vmem, vmem),
         scratch_shapes=[pltpu.SemaphoreType.DMA((2, 4))],
-        compiler_params=pltpu.CompilerParams(vmem_limit_bytes=60 << 20),
+        compiler_params=pltpu.CompilerParams(vmem_limit_bytes=8 << 20),
         name="edges",
-    )(primal, adjoint)
+    )(*(pltpu.with_memory_space_constraint(x, pltpu.HBM) for x in (primal, adjoint)))
     ax_s = pl.pallas_call(
         functools.partial(lane_kernel, dims),
         out_shape=f32((2 * F, halves, 8, nx)),

time: 31 us -> 29.9 us (0.965)
  Pallas kernels: 11.8 us -> 10.8 us
    pallas_call x1, Pallas kernels: 2.46 us -> 1.53 us  [on_device(): pl.pallas_call(functools.partial(edge_kernel, dims), out_shape=(f32((2 *...]
  transfers between devices with their start and end apart: 5 -> 5, of which waited for: 1 -> 1; matrix products, arithmetic and copies ran while one was open for 0% -> 0% of each run, Pallas kernels for 22% -> 23%
where the time goes in v6:
time: 29.9 us; the launch traced here: 29.7 us
  blocking collectives  11.8 us (39%)
  Pallas kernels  10.8 us (36%)
  starting transfers between devices  6.28 us (21%)
  between operations  0.75 us (3%)
    all_to_all x1, blocking collectives, on_device(): data = lax.all_to_all(send, AXES, 0, 0, tiled=True)  11.8 us
    ppermute x1, starting transfers between devices, on_device(): rad_a = lax.ppermute(rad_a, AXES, pair_round(sizes, 0, 0))  3.09 us
    pallas_call x1, Pallas kernels, on_device(): pl.pallas_call(functools.partial(own_kernel, dims, ((per_rad, per_azi, pe...  2.29 us
    pallas_call x1, Pallas kernels, on_device(): pl.pallas_call(functools.partial(axial_kernel, dims, n_ax), out_shape=(f3...  1.96 us
    pallas_call x1, Pallas kernels, on_device(): pl.pallas_call(functools.partial(inner_kernel, dims), out_shape=f32((2 *...  1.8 us
    pallas_call x1, Pallas kernels, on_device(): pl.pallas_call(functools.partial(main_kernel, dims, n_rad), out_shape=(f3...  1.62 us
    pallas_call x1, Pallas kernels, on_device(): pl.pallas_call(functools.partial(edge_kernel, dims), out_shape=(f32((2 *...  1.53 us
    ppermute x1, starting transfers between devices, on_device(): azi_l = lax.ppermute(azi_s, 'azi', ring(n_azi, 1))  1.52 us
  transfers between devices with their start and end apart: 5, of which 1 were waited for; matrix products, arithmetic and copies ran while one was open for 0% of the time, Pallas kernels for 23%

profile of v6, /device:TPU:0, one launch (start us, length us, event | category | flops | bytes accessed | tf_op | source)
XLA Modules:
  0.0 29.7 jit_solution(15746243938656635955)
XLA Ops:
  0.6 0.0 copy-start
  0.6 0.0 copy-start.1
  0.7 0.0 copy-start.2
  0.7 0.0 copy-start.5
  0.7 0.0 copy-start.3
  0.7 0.0 copy-start.4
  0.7 1.5 %edges.1 = (f32[10,2,32,128]{3,2,1,0:T(8,128)S(1)}, f32[10,2,32,128]{3,2,1,0:T(8,128)S(1)}, f32[10,16,4,128]{3,2,1,0:T(4,128)S(1)}) custom-call(f32[5,16,32,128]{3,2,1,0:T(8,128)} %prim.9, f32[5,16,32,128]{3,2,1,0:T(8,128)} %adj.9), custom_call_target="tpu_custom_call" | custom-call | tf_op jit(solution)/shard_map/edges/pallas_call | solution.py:549
  2.2 3.1 %collective-permute-start.2 = (f32[10,2,32,128]{3,2,1,0:T(8,128)S(1)}, f32[10,2,32,128]{3,2,1,0:T(8,128)S(1)}, u32[]{:S(2)}, u32[]{:S(2)}) collective-permute-start(f32[10,2,32,128]{3,2,1,0:T(8,128)S(1)} %get-tuple-element.20), channel_id=1, source_target_pairs={{0,8},{1,9},{2,10},{3,11},{4,12},{5,13},{6,14},{7,15},{8,0},{9,1},... | collective-permute-start | bytes 983048 | tf_op jit(solution)/shard_map/ppermute | solution.py:571
  5.3 0.0 collective-permute-start.3
  5.3 1.5 %collective-permute-start.4 = (f32[10,16,4,128]{3,2,1,0:T(4,128)S(1)}, f32[10,16,4,128]{3,2,1,0:T(4,128)S(1)}, u32[]{:S(2)}, u32[]{:S(2)}) collective-permute-start(f32[10,16,4,128]{3,2,1,0:T(4,128)S(1)} %get-tuple-element.22), channel_id=1, source_target_pairs={{0,4},{4,0},{1,5},{5,1},{2,6},{6,2},{3,7},{7,3},{8,12},{12,8},{9,1... | collective-permute-start | bytes 983048 | tf_op jit(solution)/shard_map/ppermute | solution.py:569
  6.8 0.0 copy-done
  6.8 0.0 copy-done.1
  6.8 0.7 %lanes.1.ax_s = f32[10,2,8,128]{3,2,1,0:T(8,128)S(1)} custom-call(f32[5,16,32,128]{3,2,1,0:T(8,128)S(1)} %copy-done, f32[5,16,32,128]{3,2,1,0:T(8,128)S(1)} %copy-done.1), custom_call_target="tpu_custom_call" | custom-call | tf_op jit(solution)/shard_map/lanes/pallas_call | solution.py:558
  7.6 0.3 collective-permute-start
  7.9 1.4 %collective-permute-start.1 = (f32[10,2,8,128]{3,2,1,0:T(8,128)S(1)}, f32[10,2,8,128]{3,2,1,0:T(8,128)S(1)}, u32[]{:S(2)}, u32[]{:S(2)}) collective-permute-start(f32[10,2,8,128]{3,2,1,0:T(8,128)S(1)} %lanes.1.ax_s), channel_id=1, source_target_pairs={{0,3},{1,2},{2,1},{3,0},{4,7},{5,6},{6,5},{7,4},{8,11},{9,10},{10,... | collective-permute-start | bytes 245768 | tf_op jit(solution)/shard_map/ppermute | solution.py:568
  9.3 0.0 copy-done.2
  9.3 0.0 copy-done.5
  9.3 0.0 copy-done.3
  9.3 0.0 copy-done.4
  9.3 2.3 %own.1 = (f32[2560,256]{1,0:T(8,128)S(1)}, f32[2560,128]{1,0:T(8,128)S(1)}, f32[1,256]{1,0:T(1,128)S(1)}) custom-call(f32[5,16,32,128]{3,2,1,0:T(8,128)S(1)} %copy-done, f32[5,16,32,128]{3,2,1,0:T(8,128)S(1)} %copy-done.1, f32[10,2,8,128]{3,2,1,0:T(8,128)S(1)} %lanes.1.ax_s, s32[1,6,2,8]{3,2,1,0:T(2,128)S(1)} %bitcast.5, s32[1,2,8]{2,1,0:T(2,128)S(1)} %copy-done.3, ...), custom_call_target="tpu_custom_call" | custom-call | tf_op jit(solution)/shard_map/own/pallas_call | solution.py:578
  11.6 1.8 %inner.1.part_bw = f32[10,16,32,128]{3,2,1,0:T(8,128)S(1)} custom-call(f32[5,16,32,128]{3,2,1,0:T(8,128)S(1)} %copy-done, f32[5,16,32,128]{3,2,1,0:T(8,128)S(1)} %copy-done.1, f32[1,256]{1,0:T(1,128)S(1)} %get-tuple-element.17.dep.row), custom_call_target="tpu_custom_call" | custom-call | tf_op jit(solution)/shard_map/inner/pallas_call | solution.py:590
  13.4 0.0 collective-permute-done.ax_a
  13.4 0.0 collective-permute-done.1.ax_b
  13.4 2.0 %axial.1 = (f32[10,16,32,128]{3,2,1,0:T(8,128)S(1)}, f32[16,32,128]{2,1,0:T(8,128)S(1)}) custom-call(f32[2560,256]{1,0:T(8,128)S(1)} %get-tuple-element.15.sums, f32[2560,128]{1,0:T(8,128)S(1)} %get-tuple-element.16.fourth, f32[10,16,32,128]{3,2,1,0:T(8,128)S(1)} %inner.1.part_bw, f32[10,2,8,128]{3,2,1,0:T(8,128)S(1)} %collective-permute-done.ax_a, ...), custom_call_target="tpu_custom_call" | custom-call | tf_op jit(solution)/shard_map/axial/pallas_call | solution.py:602
  15.4 0.0 collective-permute-done.2.rad_a
  15.4 0.0 collective-permute-done.3.rad_b
  15.4 0.1 collective-permute-done.4.azi_l.azi_r
  15.4 1.6 %stencil.1 = (f32[16,32,128]{2,1,0:T(8,128)}, f32[64,128]{1,0:T(8,128)S(1)}) custom-call(f32[5,16,32,128]{3,2,1,0:T(8,128)S(1)} %copy-done, f32[5,16,32,128]{3,2,1,0:T(8,128)S(1)} %copy-done.1, f32[10,16,32,128]{3,2,1,0:T(8,128)S(1)} %get-tuple-element.18.bw, f32[16,32,128]{2,1,0:T(8,128)S(1)} %get-tuple-element.19.done, ...), custom_call_target="tpu_custom_call" | custom-call | tf_op jit(solution)/shard_map/stencil/pallas_call | solution.py:618
  17.1 11.8 %all_to_all.11 = f32[32,2,128]{2,1,0:T(2,128)S(1)} all-to-all(f32[32,2,128]{2,1,0:T(2,128)S(1)} %bitcast.4), channel_id=1, replica_groups=mesh['rad'=4,'azi'=2,'ax'=4] {'rad','azi','ax'}, dimensions={0} | all-to-all | bytes 65536 | tf_op jit(solution)/shard_map/all_to_all | solution.py:627
  28.8 0.9 %blocks.1 = (f32[1,2,8]{2,1,0:T(2,128)}, f32[1,1,1]{2,1,0:T(1,128)}) custom-call(f32[64,128]{1,0:T(8,128)S(1)} %bitcast.3), custom_call_target="tpu_custom_call" | custom-call | tf_op jit(solution)/shard_map/blocks/pallas_call | solution.py:629
Async XLA Ops:
  0.6 6.2 %copy-start = (f32[5,16,32,128]{3,2,1,0:T(8,128)S(1)}, f32[5,16,32,128]{3,2,1,0:T(8,128)}, u32[]{:S(2)}) copy-start(f32[5,16,32,128]{3,2,1,0:T(8,128)} %prim.9) | copy-start | bytes 3932164
  0.6 6.2 %copy-start.1 = (f32[5,16,32,128]{3,2,1,0:T(8,128)S(1)}, f32[5,16,32,128]{3,2,1,0:T(8,128)}, u32[]{:S(2)}) copy-start(f32[5,16,32,128]{3,2,1,0:T(8,128)} %adj.9) | copy-start | bytes 3932164
  0.7 8.6 %copy-start.2 = (s32[1,2,8,6]{2,1,3,0:T(2,128)S(1)}, s32[1,2,8,6]{2,1,3,0:T(2,128)}, u32[]{:S(2)}) copy-start(s32[1,2,8,6]{2,1,3,0:T(2,128)} %param.11) | copy-start | bytes 1156
  0.7 8.6 %copy-start.5 = (s32[1,2,8]{2,1,0:T(2,128)S(1)}, s32[1,2,8]{2,1,0:T(2,128)}, u32[]{:S(2)}) copy-start(s32[1,2,8]{2,1,0:T(2,128)} %weight.1) | copy-start | bytes 196
  0.7 8.6 %copy-start.3 = (s32[1,2,8]{2,1,0:T(2,128)S(1)}, s32[1,2,8]{2,1,0:T(2,128)}, u32[]{:S(2)}) copy-start(s32[1,2,8]{2,1,0:T(2,128)} %refine.1) | copy-start | bytes 196
  0.7 8.6 %copy-start.4 = (s32[1,2,8]{2,1,0:T(2,128)S(1)}, s32[1,2,8]{2,1,0:T(2,128)}, u32[]{:S(2)}) copy-start(s32[1,2,8]{2,1,0:T(2,128)} %owner.1) | copy-start | bytes 196
  2.2 13.1 %collective-permute-start.2 = (f32[10,2,32,128]{3,2,1,0:T(8,128)S(1)}, f32[10,2,32,128]{3,2,1,0:T(8,128)S(1)}, u32[]{:S(2)}, u32[]{:S(2)}) collective-permute-start(f32[10,2,32,128]{3,2,1,0:T(8,128)S(1)} %get-tuple-element.20), channel_id=1, source_target_pairs={{0,8},{1,9},{2,10},{3,11},{4,12},{5,13},{6,14},{7,15},{8,0},{9,1},... | collective-permute-start | bytes 983048 | tf_op jit(solution)/shard_map/ppermute | solution.py:571
  5.3 10.1 %collective-permute-start.3 = (f32[10,2,32,128]{3,2,1,0:T(8,128)S(1)}, f32[10,2,32,128]{3,2,1,0:T(8,128)S(1)}, u32[]{:S(2)}, u32[]{:S(2)}) collective-permute-start(f32[10,2,32,128]{3,2,1,0:T(8,128)S(1)} %get-tuple-element.21), channel_id=1, source_target_pairs={{0,1},{1,0},{2,3},{3,2},{4,5},{5,4},{6,7},{7,6},{8,16},{9,17},{10,... | collective-permute-start | bytes 983048 | tf_op jit(solution)/shard_map/ppermute | solution.py:572
  5.3 10.1 %collective-permute-start.4 = (f32[10,16,4,128]{3,2,1,0:T(4,128)S(1)}, f32[10,16,4,128]{3,2,1,0:T(4,128)S(1)}, u32[]{:S(2)}, u32[]{:S(2)}) collective-permute-start(f32[10,16,4,128]{3,2,1,0:T(4,128)S(1)} %get-tuple-element.22), channel_id=1, source_target_pairs={{0,4},{4,0},{1,5},{5,1},{2,6},{6,2},{3,7},{7,3},{8,12},{12,8},{9,1... | collective-permute-start | bytes 983048 | tf_op jit(solution)/shard_map/ppermute | solution.py:569
  7.6 5.8 %collective-permute-start = (f32[10,2,8,128]{3,2,1,0:T(8,128)S(1)}, f32[10,2,8,128]{3,2,1,0:T(8,128)S(1)}, u32[]{:S(2)}, u32[]{:S(2)}) collective-permute-start(f32[10,2,8,128]{3,2,1,0:T(8,128)S(1)} %lanes.1.ax_s), channel_id=1, source_target_pairs={{0,1},{1,0},{2,3},{3,2},{4,5},{5,4},{6,7},{7,6},{8,9},{9,8},{10,11... | collective-permute-start | bytes 245768 | tf_op jit(solution)/shard_map/ppermute | solution.py:567
  7.9 5.5 %collective-permute-start.1 = (f32[10,2,8,128]{3,2,1,0:T(8,128)S(1)}, f32[10,2,8,128]{3,2,1,0:T(8,128)S(1)}, u32[]{:S(2)}, u32[]{:S(2)}) collective-permute-start(f32[10,2,8,128]{3,2,1,0:T(8,128)S(1)} %lanes.1.ax_s), channel_id=1, source_target_pairs={{0,3},{1,2},{2,1},{3,0},{4,7},{5,6},{6,5},{7,4},{8,11},{9,10},{10,... | collective-permute-start | bytes 245768 | tf_op jit(solution)/shard_map/ppermute | solution.py:568

commit v7 on v6

--- a/solution.py
+++ b/solution.py
@@ -411,7 +411,7 @@
     return radial, azimuthal
 
 
-def main_kernel(dims, n_rad, prim, adj, bw, done, rad_a, rad_b, azi_l, azi_r, row, ind, send):
+def main_kernel(dims, n_rad, prim, adj, bw, done, azi_l, azi_r, rad_a, rad_b, row, ind, send):
     nr, na, nx = dims
     tiles = na // 8
     lane = lax.broadcasted_iota(jnp.int32, (8, nx), 1)
@@ -476,7 +476,9 @@
         send[pl.ds(8 * d, 8), :] = both
 
 
-def final_kernel(n_loc, per_ax, data, cost, load, means):
+def final_kernel(n_loc, per_ax, data, ind_in, cost_out, load_out, ind, cost, load, means, sems):
+    leave = [pltpu.make_async_copy(ind_in, ind, sems.at[0])]
+    leave[0].start()
     n_dev, nx = data.shape[0] // 2, data.shape[1]
     me = (lax.axis_index("rad") * lax.axis_size("azi") + lax.axis_index("azi")) * lax.axis_size(
         "ax"
@@ -532,6 +534,11 @@
         cost[0, pl.ds(b, 1), :] = x[:, 0:per_ax]
     total = jnp.sum(jnp.sum(acc_load, axis=0, keepdims=True), axis=1, keepdims=True) * (1.0 / n_loc)
     load[0] = total
+    for i, (x, y) in enumerate(((cost, cost_out), (load, load_out))):
+        leave.append(pltpu.make_async_copy(x, y, sems.at[1 + i]))
+        leave[-1].start()
+    for c in leave:
+        c.wait()
 
 
 def on_device(primal, adjoint, refine_flag, owner_map, migrate_weight, neighbor_list):
@@ -622,19 +629,24 @@
         out_specs=(vmem, vmem),
         compiler_params=pltpu.CompilerParams(vmem_limit_bytes=16 << 20),
         name="stencil",
-    )(primal, adjoint, bw, done, rad_a, rad_b, azi_l, azi_r, row)
+    )(primal, adjoint, bw, done, azi_l, azi_r, rad_a, rad_b, row)
 
     data = lax.all_to_all(send, AXES, 0, 0, tiled=True)
 
-    cost, load = pl.pallas_call(
+    cost, load, indicator = pl.pallas_call(
         functools.partial(final_kernel, n_loc, per_ax),
-        out_shape=(f32((per_rad, per_azi, per_ax)), f32((1, 1, 1))),
-        in_specs=[vmem],
-        out_specs=(vmem, vmem),
-        scratch_shapes=[pltpu.VMEM((n_dev // 8, 8, nx), jnp.float32)],
+        out_shape=(f32((per_rad, per_azi, per_ax)), f32((1, 1, 1)), f32(dims)),
+        in_specs=[vmem, anyspec],
+        out_specs=(anyspec,) * 3,
+        scratch_shapes=[
+            pltpu.VMEM((per_rad, per_azi, per_ax), jnp.float32),
+            pltpu.VMEM((1, 1, 1), jnp.float32),
+            pltpu.VMEM((n_dev // 8, 8, nx), jnp.float32),
+            pltpu.SemaphoreType.DMA((3,)),
+        ],
         compiler_params=pltpu.CompilerParams(vmem_limit_bytes=4 << 20),
         name="blocks",
-    )(data)
+    )(data, indicator)
     return indicator, cost, load
 
 

time: 29.9 us -> 29 us (0.970)
  blocking collectives: 11.8 us -> 11.2 us
    ppermute x1, starting transfers between devices: 3.09 us -> 1.58 us  [on_device(): rad_a = lax.ppermute(rad_a, AXES, pair_round(sizes, 0, 0))]
    ppermute x1, starting transfers between devices: 1.52 us -> 3.03 us  [on_device(): azi_l = lax.ppermute(azi_s, 'azi', ring(n_azi, 1))]
    all_to_all x1, blocking collectives: 11.8 us -> 11.2 us  [on_device(): data = lax.all_to_all(send, AXES, 0, 0, tiled=True)]
    pallas_call x1, Pallas kernels: 1.62 us -> 1.29 us  [on_device(): pl.pallas_call(functools.partial(main_kernel, dims, n_rad), out_shape=(f3...]
  transfers between devices with their start and end apart: 5 -> 5, of which waited for: 1 -> 0; matrix products, arithmetic and copies ran while one was open for 0% -> 0% of each run, Pallas kernels for 23% -> 24%
where the time goes in v7:
time: 29 us; the launch traced here: 28.9 us
  blocking collectives  11.2 us (39%)
  Pallas kernels  10.6 us (37%)
  starting transfers between devices  6.35 us (22%)
  between operations  0.76 us (3%)
    all_to_all x1, blocking collectives, on_device(): data = lax.all_to_all(send, AXES, 0, 0, tiled=True)  11.2 us
    ppermute x1, starting transfers between devices, on_device(): azi_l = lax.ppermute(azi_s, 'azi', ring(n_azi, 1))  3.03 us
    pallas_call x1, Pallas kernels, on_device(): pl.pallas_call(functools.partial(own_kernel, dims, ((per_rad, per_azi, pe...  2.29 us
    pallas_call x1, Pallas kernels, on_device(): pl.pallas_call(functools.partial(axial_kernel, dims, n_ax), out_shape=(f3...  1.98 us
    pallas_call x1, Pallas kernels, on_device(): pl.pallas_call(functools.partial(inner_kernel, dims), out_shape=f32((2 *...  1.8 us
    ppermute x1, starting transfers between devices, on_device(): rad_a = lax.ppermute(rad_a, AXES, pair_round(sizes, 0, 0))  1.58 us
    pallas_call x1, Pallas kernels, on_device(): pl.pallas_call(functools.partial(edge_kernel, dims), out_shape=(f32((2 *...  1.53 us
    pallas_call x1, Pallas kernels, on_device(): pl.pallas_call(functools.partial(main_kernel, dims, n_rad), out_shape=(f3...  1.29 us
  transfers between devices with their start and end apart: 5, of which 0 were waited for; matrix products, arithmetic and copies ran while one was open for 0% of the time, Pallas kernels for 24%

profile of v7, /device:TPU:0, one launch (start us, length us, event | category | flops | bytes accessed | tf_op | source)
XLA Modules:
  0.0 28.9 jit_solution(17509801306792402016)
XLA Ops:
  0.6 0.0 copy-start
  0.6 0.0 copy-start.1
  0.7 0.0 copy-start.2
  0.7 0.0 copy-start.5
  0.7 0.0 copy-start.3
  0.7 0.0 copy-start.4
  0.7 1.5 %edges.1 = (f32[10,2,32,128]{3,2,1,0:T(8,128)S(1)}, f32[10,2,32,128]{3,2,1,0:T(8,128)S(1)}, f32[10,16,4,128]{3,2,1,0:T(4,128)S(1)}) custom-call(f32[5,16,32,128]{3,2,1,0:T(8,128)} %prim.9, f32[5,16,32,128]{3,2,1,0:T(8,128)} %adj.9), custom_call_target="tpu_custom_call" | custom-call | tf_op jit(solution)/shard_map/edges/pallas_call | solution.py:556
  2.2 3.0 %collective-permute-start.2 = (f32[10,16,4,128]{3,2,1,0:T(4,128)S(1)}, f32[10,16,4,128]{3,2,1,0:T(4,128)S(1)}, u32[]{:S(2)}, u32[]{:S(2)}) collective-permute-start(f32[10,16,4,128]{3,2,1,0:T(4,128)S(1)} %get-tuple-element.21), channel_id=1, source_target_pairs={{0,4},{4,0},{1,5},{5,1},{2,6},{6,2},{3,7},{7,3},{8,12},{12,8},{9,1... | collective-permute-start | bytes 983048 | tf_op jit(solution)/shard_map/ppermute | solution.py:576
  5.3 1.6 %collective-permute-start.3 = (f32[10,2,32,128]{3,2,1,0:T(8,128)S(1)}, f32[10,2,32,128]{3,2,1,0:T(8,128)S(1)}, u32[]{:S(2)}, u32[]{:S(2)}) collective-permute-start(f32[10,2,32,128]{3,2,1,0:T(8,128)S(1)} %get-tuple-element.22), channel_id=1, source_target_pairs={{0,8},{1,9},{2,10},{3,11},{4,12},{5,13},{6,14},{7,15},{8,0},{9,1},... | collective-permute-start | bytes 983048 | tf_op jit(solution)/shard_map/ppermute | solution.py:578
  6.8 0.0 collective-permute-start.4
  6.8 0.0 copy-done
  6.8 0.0 copy-done.1
  6.8 0.7 %lanes.1.ax_s = f32[10,2,8,128]{3,2,1,0:T(8,128)S(1)} custom-call(f32[5,16,32,128]{3,2,1,0:T(8,128)S(1)} %copy-done, f32[5,16,32,128]{3,2,1,0:T(8,128)S(1)} %copy-done.1), custom_call_target="tpu_custom_call" | custom-call | tf_op jit(solution)/shard_map/lanes/pallas_call | solution.py:565
  7.6 0.6 %collective-permute-start = (f32[10,2,8,128]{3,2,1,0:T(8,128)S(1)}, f32[10,2,8,128]{3,2,1,0:T(8,128)S(1)}, u32[]{:S(2)}, u32[]{:S(2)}) collective-permute-start(f32[10,2,8,128]{3,2,1,0:T(8,128)S(1)} %lanes.1.ax_s), channel_id=1, source_target_pairs={{0,1},{1,0},{2,3},{3,2},{4,5},{5,4},{6,7},{7,6},{8,9},{9,8},{10,11... | collective-permute-start | bytes 245768 | tf_op jit(solution)/shard_map/ppermute | solution.py:574
  8.2 1.2 %collective-permute-start.1 = (f32[10,2,8,128]{3,2,1,0:T(8,128)S(1)}, f32[10,2,8,128]{3,2,1,0:T(8,128)S(1)}, u32[]{:S(2)}, u32[]{:S(2)}) collective-permute-start(f32[10,2,8,128]{3,2,1,0:T(8,128)S(1)} %lanes.1.ax_s), channel_id=1, source_target_pairs={{0,3},{1,2},{2,1},{3,0},{4,7},{5,6},{6,5},{7,4},{8,11},{9,10},{10,... | collective-permute-start | bytes 245768 | tf_op jit(solution)/shard_map/ppermute | solution.py:575
  9.3 0.0 copy-done.2
  9.3 0.0 copy-done.5
  9.3 0.0 copy-done.3
  9.3 0.0 copy-done.4
  9.3 2.3 %own.1 = (f32[2560,256]{1,0:T(8,128)S(1)}, f32[2560,128]{1,0:T(8,128)S(1)}, f32[1,256]{1,0:T(1,128)S(1)}) custom-call(f32[5,16,32,128]{3,2,1,0:T(8,128)S(1)} %copy-done, f32[5,16,32,128]{3,2,1,0:T(8,128)S(1)} %copy-done.1, f32[10,2,8,128]{3,2,1,0:T(8,128)S(1)} %lanes.1.ax_s, s32[1,6,2,8]{3,2,1,0:T(2,128)S(1)} %bitcast.5, s32[1,2,8]{2,1,0:T(2,128)S(1)} %copy-done.3, ...), custom_call_target="tpu_custom_call" | custom-call | tf_op jit(solution)/shard_map/own/pallas_call | solution.py:585
  11.6 1.8 %inner.1.part_bw = f32[10,16,32,128]{3,2,1,0:T(8,128)S(1)} custom-call(f32[5,16,32,128]{3,2,1,0:T(8,128)S(1)} %copy-done, f32[5,16,32,128]{3,2,1,0:T(8,128)S(1)} %copy-done.1, f32[1,256]{1,0:T(1,128)S(1)} %get-tuple-element.18.dep.row), custom_call_target="tpu_custom_call" | custom-call | tf_op jit(solution)/shard_map/inner/pallas_call | solution.py:597
  13.4 0.0 collective-permute-done.ax_a
  13.5 0.0 collective-permute-done.1.ax_b
  13.5 2.0 %axial.1 = (f32[10,16,32,128]{3,2,1,0:T(8,128)S(1)}, f32[16,32,128]{2,1,0:T(8,128)S(1)}) custom-call(f32[2560,256]{1,0:T(8,128)S(1)} %get-tuple-element.16.sums, f32[2560,128]{1,0:T(8,128)S(1)} %get-tuple-element.17.fourth, f32[10,16,32,128]{3,2,1,0:T(8,128)S(1)} %inner.1.part_bw, f32[10,2,8,128]{3,2,1,0:T(8,128)S(1)} %collective-permute-done.ax_a, ...), custom_call_target="tpu_custom_call" | custom-call | tf_op jit(solution)/shard_map/axial/pallas_call | solution.py:609
  15.5 0.0 collective-permute-done.2.azi_l.azi_r
  15.5 0.0 collective-permute-done.3.rad_a
  15.5 0.0 collective-permute-done.4.rad_b
  15.5 1.3 %stencil.1 = (f32[16,32,128]{2,1,0:T(8,128)S(1)}, f32[64,128]{1,0:T(8,128)S(1)}) custom-call(f32[5,16,32,128]{3,2,1,0:T(8,128)S(1)} %copy-done, f32[5,16,32,128]{3,2,1,0:T(8,128)S(1)} %copy-done.1, f32[10,16,32,128]{3,2,1,0:T(8,128)S(1)} %get-tuple-element.19.bw, f32[16,32,128]{2,1,0:T(8,128)S(1)} %get-tuple-element.20.done, ...), custom_call_target="tpu_custom_call" | custom-call | tf_op jit(solution)/shard_map/stencil/pallas_call | solution.py:625
  16.8 11.2 %all_to_all.11 = f32[32,2,128]{2,1,0:T(2,128)S(1)} all-to-all(f32[32,2,128]{2,1,0:T(2,128)S(1)} %bitcast.4), channel_id=1, replica_groups=mesh['rad'=4,'azi'=2,'ax'=4] {'rad','azi','ax'}, dimensions={0} | all-to-all | bytes 65536 | tf_op jit(solution)/shard_map/all_to_all | solution.py:634
  27.9 0.9 %blocks.1 = (f32[1,2,8]{2,1,0:T(2,128)}, f32[1,1,1]{2,1,0:T(1,128)}, f32[16,32,128]{2,1,0:T(8,128)}) custom-call(f32[64,128]{1,0:T(8,128)S(1)} %bitcast.3, f32[16,32,128]{2,1,0:T(8,128)S(1)} %get-tuple-element.25.ind_in), custom_call_target="tpu_custom_call" | custom-call | tf_op jit(solution)/shard_map/blocks/pallas_call | solution.py:636
Async XLA Ops:
  0.6 6.2 %copy-start = (f32[5,16,32,128]{3,2,1,0:T(8,128)S(1)}, f32[5,16,32,128]{3,2,1,0:T(8,128)}, u32[]{:S(2)}) copy-start(f32[5,16,32,128]{3,2,1,0:T(8,128)} %prim.9) | copy-start | bytes 3932164
  0.6 6.2 %copy-start.1 = (f32[5,16,32,128]{3,2,1,0:T(8,128)S(1)}, f32[5,16,32,128]{3,2,1,0:T(8,128)}, u32[]{:S(2)}) copy-start(f32[5,16,32,128]{3,2,1,0:T(8,128)} %adj.9) | copy-start | bytes 3932164
  0.7 8.7 %copy-start.2 = (s32[1,2,8,6]{2,1,3,0:T(2,128)S(1)}, s32[1,2,8,6]{2,1,3,0:T(2,128)}, u32[]{:S(2)}) copy-start(s32[1,2,8,6]{2,1,3,0:T(2,128)} %param.11) | copy-start | bytes 1156
  0.7 8.7 %copy-start.5 = (s32[1,2,8]{2,1,0:T(2,128)S(1)}, s32[1,2,8]{2,1,0:T(2,128)}, u32[]{:S(2)}) copy-start(s32[1,2,8]{2,1,0:T(2,128)} %weight.1) | copy-start | bytes 196
  0.7 8.7 %copy-start.3 = (s32[1,2,8]{2,1,0:T(2,128)S(1)}, s32[1,2,8]{2,1,0:T(2,128)}, u32[]{:S(2)}) copy-start(s32[1,2,8]{2,1,0:T(2,128)} %refine.1) | copy-start | bytes 196
  0.7 8.7 %copy-start.4 = (s32[1,2,8]{2,1,0:T(2,128)S(1)}, s32[1,2,8]{2,1,0:T(2,128)}, u32[]{:S(2)}) copy-start(s32[1,2,8]{2,1,0:T(2,128)} %owner.1) | copy-start | bytes 196
  2.2 13.2 %collective-permute-start.2 = (f32[10,16,4,128]{3,2,1,0:T(4,128)S(1)}, f32[10,16,4,128]{3,2,1,0:T(4,128)S(1)}, u32[]{:S(2)}, u32[]{:S(2)}) collective-permute-start(f32[10,16,4,128]{3,2,1,0:T(4,128)S(1)} %get-tuple-element.21), channel_id=1, source_target_pairs={{0,4},{4,0},{1,5},{5,1},{2,6},{6,2},{3,7},{7,3},{8,12},{12,8},{9,1... | collective-permute-start | bytes 983048 | tf_op jit(solution)/shard_map/ppermute | solution.py:576
  5.3 10.2 %collective-permute-start.3 = (f32[10,2,32,128]{3,2,1,0:T(8,128)S(1)}, f32[10,2,32,128]{3,2,1,0:T(8,128)S(1)}, u32[]{:S(2)}, u32[]{:S(2)}) collective-permute-start(f32[10,2,32,128]{3,2,1,0:T(8,128)S(1)} %get-tuple-element.22), channel_id=1, source_target_pairs={{0,8},{1,9},{2,10},{3,11},{4,12},{5,13},{6,14},{7,15},{8,0},{9,1},... | collective-permute-start | bytes 983048 | tf_op jit(solution)/shard_map/ppermute | solution.py:578
  6.8 8.6 %collective-permute-start.4 = (f32[10,2,32,128]{3,2,1,0:T(8,128)S(1)}, f32[10,2,32,128]{3,2,1,0:T(8,128)S(1)}, u32[]{:S(2)}, u32[]{:S(2)}) collective-permute-start(f32[10,2,32,128]{3,2,1,0:T(8,128)S(1)} %get-tuple-element.23), channel_id=1, source_target_pairs={{0,1},{1,0},{2,3},{3,2},{4,5},{5,4},{6,7},{7,6},{8,16},{9,17},{10,... | collective-permute-start | bytes 983048 | tf_op jit(solution)/shard_map/ppermute | solution.py:579
  7.6 5.9 %collective-permute-start = (f32[10,2,8,128]{3,2,1,0:T(8,128)S(1)}, f32[10,2,8,128]{3,2,1,0:T(8,128)S(1)}, u32[]{:S(2)}, u32[]{:S(2)}) collective-permute-start(f32[10,2,8,128]{3,2,1,0:T(8,128)S(1)} %lanes.1.ax_s), channel_id=1, source_target_pairs={{0,1},{1,0},{2,3},{3,2},{4,5},{5,4},{6,7},{7,6},{8,9},{9,8},{10,11... | collective-permute-start | bytes 245768 | tf_op jit(solution)/shard_map/ppermute | solution.py:574
  8.2 5.3 %collective-permute-start.1 = (f32[10,2,8,128]{3,2,1,0:T(8,128)S(1)}, f32[10,2,8,128]{3,2,1,0:T(8,128)S(1)}, u32[]{:S(2)}, u32[]{:S(2)}) collective-permute-start(f32[10,2,8,128]{3,2,1,0:T(8,128)S(1)} %lanes.1.ax_s), channel_id=1, source_target_pairs={{0,3},{1,2},{2,1},{3,0},{4,7},{5,6},{6,5},{7,4},{8,11},{9,10},{10,... | collective-permute-start | bytes 245768 | tf_op jit(solution)/shard_map/ppermute | solution.py:575

commit v8 on v7

--- a/solution.py
+++ b/solution.py
@@ -56,20 +56,24 @@
         c.wait()
 
 
-def lane_kernel(dims, prim, adj, ax_s):
+def lane_kernel(dims, prim, adj, first, second):
     nr, na, nx = dims
-    slot = lax.broadcasted_iota(jnp.int32, (8, nx), 1) >> 2
+    even = lax.rem(lax.axis_index("ax"), 2) == 0
+    slot = lax.broadcasted_iota(jnp.int32, (8, nx), 1) >> 1
     tiles = na // 8
-    per = nx // 4
+    per = nx // 2
     for t, src in enumerate((prim, adj)):
         for f in range(F):
             for h in range(nr * tiles // per):
-                acc = jnp.zeros((8, nx), jnp.float32)
+                upper = lower = jnp.zeros((8, nx), jnp.float32)
                 for j in range(per):
                     k = h * per + j
                     x = src[f, k // tiles, pl.ds(8 * (k % tiles), 8), :]
-                    acc = jnp.where(slot == j, pltpu.roll(x, (4 * j + 2) % nx, 1), acc)
-                ax_s[t * F + f, h] = acc
+                    x = pltpu.roll(x, (2 * j + 2) % nx, 1)
+                    upper = jnp.where(slot == j, x, upper)
+                    lower = jnp.where(slot == (j + 1) % per, x, lower)
+                first[t * F + f, h] = jnp.where(even, upper, lower)
+                second[t * F + f, h] = jnp.where(even, lower, upper)
 
 
 def flux(s, along):
@@ -133,36 +137,15 @@
     return head, tail
 
 
-def own_kernel(
-    dims, grid, prim, adj, ax_s, near, refine, owner, weight, sums, fourth, row, lhs, rhs
-):
-    del ax_s
-    nr, na, nx = dims
-    head, tail = block_row(grid, near, refine, owner, weight, nx)
-    row[:, 0:nx] = head
-    row[:, nx:2 * nx] = tail
-    size = nr * na
-    i = lax.broadcasted_iota(jnp.int32, (nx, nx), 0)
-    c = lax.broadcasted_iota(jnp.int32, (nx, nx), 1)
-    for n, table in enumerate((UPPER, LOWER, FOURTH)):
-        own = taps(i, c, table).astype(jnp.bfloat16)
-        for k in range(3):
-            rhs[pl.ds(k * nx, nx), pl.ds(n * nx, nx)] = own
-
-    def build(t, src, f):
-        for r in range(nr):
-            rows = pl.ds(pl.multiple_of((t * F + f) * size, size) + r * na, na)
-            for k, x in enumerate(split3(src[f, r])):
-                lhs[rows, pl.ds(k * nx, nx)] = x
-
-    for t, src in enumerate((prim, adj)):
-        lax.fori_loop(0, F, lambda f, c, t=t, src=src: (build(t, src, f), c)[1], 0)
-    sums[...] = jnp.dot(
-        lhs[0:F * size, :], rhs[:, 0:2 * nx], preferred_element_type=jnp.float32
-    )
-    fourth[...] = jnp.dot(
-        lhs[F * size:2 * F * size, :], rhs[:, 2 * nx:3 * nx], preferred_element_type=jnp.float32
-    )
+PLANES = 4
+
+
+def place_of(dims, f, r, a):
+    _, na, _ = dims
+    group = PLANES * na
+    if isinstance(r, int):
+        return (r // PLANES * F + f) * group + r % PLANES * na + 8 * a
+    return pl.multiple_of((lax.div(r, PLANES) * F + f) * group + lax.rem(r, PLANES) * na, na) + 8 * a
 
 
 def axial_kernel(dims, n_ax, sums, fourth, part_bw, ax_a, ax_b, bw, done, got, lhs, rhs, far, far_w):
@@ -186,9 +169,12 @@
 
     for h in range(halves):
         for f in range(2 * F):
-            a, b = ax_a[f, h], ax_b[f, h]
+            a, b = ax_a[f, h // 2], ax_b[f, h // 2]
             left = jnp.where(i_ax == 0, 0.0, jnp.where(even_ax, b, a))
             right = jnp.where(i_ax == n_ax - 1, 0.0, jnp.where(even_ax, a, b))
+            at = h % 2 * (nx // 2) + 2 * slot + (lane & 1)
+            left = jnp.take_along_axis(left, at, axis=1)
+            right = jnp.take_along_axis(right, (at + 2) & (nx - 1), axis=1)
             for k, x in enumerate(split3(jnp.where(part < 2, left, right))):
                 x = x.astype(jnp.float32)
                 got[k, f, h] = pltpu.roll(x, 4 * third * k, 1) if k else x
@@ -215,12 +201,13 @@
     def tile(r, a, whole):
         mine = pl.ds(8 * a, 8)
         at = [pl.ds(f * size + r * na + 8 * a, 8) for f in range(F)]
-        up = flux([sums[q, 0:nx] + far[q, 0:nx] for q in at], 2)
-        low = flux([sums[q, nx:2 * nx] + far[q, nx:2 * nx] for q in at], 2)
+        own = [pl.ds(place_of(dims, f, r, a), 8) for f in range(F)]
+        up = flux([sums[p, 0:nx] + far[q, 0:nx] for p, q in zip(own, at)], 2)
+        low = flux([sums[p, nx:2 * nx] + far[q, nx:2 * nx] for p, q in zip(own, at)], 2)
         total = None
         for f in range(F):
             bal = part_bw[f, r, mine, :] + (up[f] - low[f])
-            w = part_bw[F + f, r, mine, :] + (fourth[at[f], :] + far_w[at[f], :])
+            w = part_bw[F + f, r, mine, :] + (fourth[own[f], :] + far_w[at[f], :])
             if whole:
                 total = w * bal if total is None else total + w * bal
             else:
@@ -246,12 +233,36 @@
     return src[f, r, pl.ds(8 * a + da, 8), :]
 
 
-def inner_kernel(dims, prim, adj, dep, bw, frad, fazi):
-    del dep
+def inner_kernel(
+    dims, grid, prim, adj, ax_s, near, refine, owner, weight, sums, fourth, row, bw, lhs, rhs, frad, fazi
+):
+    del ax_s
     nr, na, nx = dims
     tiles = na // 8
     sub = lax.broadcasted_iota(jnp.int32, (8, nx), 0)
     zero = jnp.zeros((8, nx), jnp.float32)
+    head, tail = block_row(grid, near, refine, owner, weight, nx)
+    row[:, 0:nx] = head
+    row[:, nx:2 * nx] = tail
+    i = lax.broadcasted_iota(jnp.int32, (nx, nx), 0)
+    c = lax.broadcasted_iota(jnp.int32, (nx, nx), 1)
+    for n, table in enumerate((UPPER, LOWER, FOURTH)):
+        own = taps(i, c, table).astype(jnp.bfloat16)
+        for k in range(3):
+            rhs[pl.ds(k * nx, nx), pl.ds(n * nx, nx)] = own
+
+    def products(group):
+        size = PLANES * na
+        for t, src in enumerate((prim, adj)):
+            for f in range(F):
+                for i in range(PLANES):
+                    for k, x in enumerate(split3(src[f, group * PLANES + i])):
+                        lhs[group, t, pl.ds(f * size + i * na, na), pl.ds(k * nx, nx)] = x
+        rows = pl.ds(group * F * size, F * size)
+        sums[rows, :] = jnp.dot(lhs[group, 0], rhs[:, 0:2 * nx], preferred_element_type=jnp.float32)
+        fourth[rows, :] = jnp.dot(
+            lhs[group, 1], rhs[:, 2 * nx:3 * nx], preferred_element_type=jnp.float32
+        )
 
     def rad_flux(r, a):
         rows = pl.ds(8 * a, 8)
@@ -309,19 +320,16 @@
                 bw[F + f, r, mine, :] = two - 4.0 * one + 12.0 * adj[f, r, mine, :]
         return carry
 
-    for r in (0, 1):
-        plane(r, 0)
-    lax.fori_loop(2, nr - 2, plane, 0)
-    for r in (nr - 2, nr - 1):
-        plane(r, 0)
-
-
-def edge_terms(dims, n_rad, prim, adj, rad_a, rad_b, azi_l, azi_r):
+    for group in range(nr // PLANES):
+        products(group)
+        for i in range(PLANES):
+            plane(group * PLANES + i, 0)
+
+
+def radial_terms(dims, n_rad, prim, rad_a, rad_b):
     nr, na, nx = dims
     i_rad = lax.axis_index("rad")
     odd = lax.rem(i_rad, 2) == 1
-    tiles = na // 8
-    sub = lax.broadcasted_iota(jnp.int32, (8, nx), 0)
 
     def before(g, i, rows):
         return jnp.where(i_rad == 0, 0.0, jnp.where(odd, rad_a[g, i, rows, :], rad_b[g, i, rows, :]))
@@ -357,6 +365,13 @@
             w[nr - 1].append(h1 - 4.0 * h0)
         return bal, w
 
+    return radial
+
+
+def azimuthal_terms(dims, prim, azi_l, azi_r):
+    na, nx = dims[1:]
+    sub = lax.broadcasted_iota(jnp.int32, (8, nx), 0)
+
     def azimuthal(r, a):
         if a == 0:
             def layer(g, i):
@@ -408,51 +423,71 @@
             w.append(jnp.where(sub == 7, h1 - 4.0 * h0, jnp.where(sub == 6, h0, 0.0)))
         return bal, w
 
-    return radial, azimuthal
-
-
-def main_kernel(dims, n_rad, prim, adj, bw, done, azi_l, azi_r, rad_a, rad_b, row, ind, send):
+    return azimuthal
+
+
+def indicator_of(bal, w):
+    total = w[0] * bal[0]
+    for f in range(1, F):
+        total = total + w[f] * bal[f]
+    return jnp.abs(total) * (1.0 / 144.0)
+
+
+def rows_kernel(dims, prim, bw, done, azi_l, azi_r, ind, ends, part_sums):
+    nr, na, nx = dims
+    tiles = na // 8
+    azimuthal = azimuthal_terms(dims, prim, azi_l, azi_r)
+
+    def outer(r, a):
+        mine = pl.ds(8 * a, 8)
+        more_bal, more_w = azimuthal(r, a)
+        bal = [bw[f, r, mine, :] + more_bal[f] for f in range(F)]
+        return bal, [bw[F + f, r, mine, :] + more_w[f] for f in range(F)]
+
+    for i, r in enumerate((0, 1, nr - 2, nr - 1)):
+        for a in range(tiles):
+            mine = pl.ds(8 * a, 8)
+            if a in (0, tiles - 1):
+                bal, w = outer(r, a)
+                for f in range(F):
+                    ends[f, i, mine, :] = bal[f]
+                    ends[F + f, i, mine, :] = w[f]
+            else:
+                for g in range(2 * F):
+                    ends[g, i, mine, :] = bw[g, r, mine, :]
+
+    def plane(r, sums):
+        out = []
+        for a in range(tiles):
+            mine = pl.ds(8 * a, 8)
+            x = indicator_of(*outer(r, a)) if a in (0, tiles - 1) else done[r, mine, :]
+            ind[r, mine, :] = x
+            out.append(sums[a] + x)
+        return tuple(out)
+
+    zero = jnp.zeros((8, nx), jnp.float32)
+    sums = lax.fori_loop(2, nr - 2, plane, (zero,) * tiles)
+    for a in range(tiles):
+        part_sums[a] = sums[a]
+
+
+def main_kernel(dims, n_rad, prim, ends, part_sums, rad_a, rad_b, row, ind, send):
     nr, na, nx = dims
     tiles = na // 8
     lane = lax.broadcasted_iota(jnp.int32, (8, nx), 1)
-    radial, azimuthal = edge_terms(dims, n_rad, prim, adj, rad_a, rad_b, azi_l, azi_r)
-
-    def outer(r, a, extra):
+    radial = radial_terms(dims, n_rad, prim, rad_a, rad_b)
+    sums = []
+    for a in range(tiles):
         mine = pl.ds(8 * a, 8)
-        bal = [bw[f, r, mine, :] for f in range(F)]
-        w = [bw[F + f, r, mine, :] for f in range(F)]
-        for more_bal, more_w in extra:
-            bal = [x + y for x, y in zip(bal, more_bal)]
-            w = [x + y for x, y in zip(w, more_w)]
-        total = w[0] * bal[0]
-        for f in range(1, F):
-            total = total + w[f] * bal[f]
-        total = jnp.abs(total) * (1.0 / 144.0)
-        ind[r, mine, :] = total
-        return total
-
-    ends = (0, 1, nr - 2, nr - 1)
-    sums = [jnp.zeros((8, nx), jnp.float32) for _ in range(tiles)]
-    for a in range(tiles):
-        bal, w = radial(a)
-        for r in ends:
-            extra = [(bal[r], w[r])]
-            if a in (0, tiles - 1):
-                extra.append(azimuthal(r, a))
-            sums[a] = sums[a] + outer(r, a, extra)
-
-    def plane(r, sums):
-        out = []
-        for a in range(tiles):
-            if a in (0, tiles - 1):
-                x = outer(r, a, [azimuthal(r, a)])
-            else:
-                x = done[r, pl.ds(8 * a, 8), :]
-                ind[r, pl.ds(8 * a, 8), :] = x
-            out.append(sums[a] + x)
-        return tuple(out)
-
-    sums = lax.fori_loop(2, nr - 2, plane, tuple(sums))
+        more_bal, more_w = radial(a)
+        t = part_sums[a]
+        for i, r in enumerate((0, 1, nr - 2, nr - 1)):
+            bal = [ends[f, i, mine, :] + more_bal[r][f] for f in range(F)]
+            w = [ends[F + f, i, mine, :] + more_w[r][f] for f in range(F)]
+            x = indicator_of(bal, w)
+            ind[i, mine, :] = x
+            t = t + x
+        sums.append(t)
 
     groups = nx // BLK
     halves_a = na // BLK
@@ -476,9 +511,16 @@
         send[pl.ds(8 * d, 8), :] = both
 
 
-def final_kernel(n_loc, per_ax, data, ind_in, cost_out, load_out, ind, cost, load, means, sems):
-    leave = [pltpu.make_async_copy(ind_in, ind, sems.at[0])]
-    leave[0].start()
+def final_kernel(n_loc, per_ax, data, inside, outside, cost_out, load_out, ind, cost, load, means, sems):
+    nr = ind.shape[0]
+    inner = pl.ds(2, nr - 4)
+    leave = [
+        pltpu.make_async_copy(inside.at[inner], ind.at[inner], sems.at[0]),
+        pltpu.make_async_copy(outside.at[pl.ds(0, 2)], ind.at[pl.ds(0, 2)], sems.at[1]),
+        pltpu.make_async_copy(outside.at[pl.ds(2, 2)], ind.at[pl.ds(nr - 2, 2)], sems.at[2]),
+    ]
+    for c in leave:
+        c.start()
     n_dev, nx = data.shape[0] // 2, data.shape[1]
     me = (lax.axis_index("rad") * lax.axis_size("azi") + lax.axis_index("azi")) * lax.axis_size(
         "ax"
@@ -535,7 +577,7 @@
     total = jnp.sum(jnp.sum(acc_load, axis=0, keepdims=True), axis=1, keepdims=True) * (1.0 / n_loc)
     load[0] = total
     for i, (x, y) in enumerate(((cost, cost_out), (load, load_out))):
-        leave.append(pltpu.make_async_copy(x, y, sems.at[1 + i]))
+        leave.append(pltpu.make_async_copy(x, y, sems.at[3 + i]))
         leave[-1].start()
     for c in leave:
         c.wait()
@@ -562,17 +604,17 @@
         compiler_params=pltpu.CompilerParams(vmem_limit_bytes=8 << 20),
         name="edges",
     )(*(pltpu.with_memory_space_constraint(x, pltpu.HBM) for x in (primal, adjoint)))
-    ax_s = pl.pallas_call(
+    ax_first, ax_second = pl.pallas_call(
         functools.partial(lane_kernel, dims),
-        out_shape=f32((2 * F, halves, 8, nx)),
+        out_shape=(f32((2 * F, halves // 2, 8, nx)),) * 2,
         in_specs=[vmem, vmem],
-        out_specs=vmem,
+        out_specs=(vmem, vmem),
         compiler_params=pltpu.CompilerParams(vmem_limit_bytes=16 << 20),
         name="lanes",
     )(primal, adjoint)
 
-    ax_a = lax.ppermute(ax_s, AXES, pair_round(sizes, 2, 0))
-    ax_b = lax.ppermute(ax_s, AXES, pair_round(sizes, 2, 1))
+    ax_a = lax.ppermute(ax_first, AXES, pair_round(sizes, 2, 0))
+    ax_b = lax.ppermute(ax_second, AXES, pair_round(sizes, 2, 1))
     azi_l = lax.ppermute(azi_s, "azi", ring(n_azi, 1))
     azi_r = azi_l if n_azi == 2 else lax.ppermute(azi_s, "azi", ring(n_azi, -1))
     rad_a = lax.ppermute(rad_a, AXES, pair_round(sizes, 0, 0))
@@ -582,30 +624,25 @@
     n_loc = per_rad * per_azi * per_ax
     near = neighbor_list.transpose(0, 3, 1, 2)
     cells = F * nr * na
-    sums, fourth, row = pl.pallas_call(
-        functools.partial(own_kernel, dims, ((per_rad, per_azi, per_ax), (n_azi, n_ax))),
-        out_shape=(f32((cells, 2 * nx)), f32((cells, nx)), f32((1, 2 * nx))),
+    sums, fourth, row, part_bw = pl.pallas_call(
+        functools.partial(inner_kernel, dims, ((per_rad, per_azi, per_ax), (n_azi, n_ax))),
+        out_shape=(
+            f32((cells, 2 * nx)),
+            f32((cells, nx)),
+            f32((1, 2 * nx)),
+            f32((2 * F, nr, na, nx)),
+        ),
         in_specs=[vmem] * 7,
-        out_specs=(vmem, vmem, vmem),
+        out_specs=(vmem,) * 4,
         scratch_shapes=[
-            pltpu.VMEM((2 * cells, 3 * nx), jnp.bfloat16),
+            pltpu.VMEM((nr // PLANES, 2, F * PLANES * na, 3 * nx), jnp.bfloat16),
             pltpu.VMEM((3 * nx, 3 * nx), jnp.bfloat16),
-        ],
-        compiler_params=pltpu.CompilerParams(vmem_limit_bytes=16 << 20),
-        name="own",
-    )(primal, adjoint, ax_s, near, refine_flag, owner_map, migrate_weight)
-    part_bw = pl.pallas_call(
-        functools.partial(inner_kernel, dims),
-        out_shape=f32((2 * F, nr, na, nx)),
-        in_specs=[vmem] * 3,
-        out_specs=vmem,
-        scratch_shapes=[
             pltpu.VMEM((F, tiles, 8, nx), jnp.float32),
             pltpu.VMEM((F, 8 + na, nx), jnp.float32),
         ],
         compiler_params=pltpu.CompilerParams(vmem_limit_bytes=16 << 20),
         name="inner",
-    )(primal, adjoint, row)
+    )(primal, adjoint, ax_first, near, refine_flag, owner_map, migrate_weight)
     bw, done = pl.pallas_call(
         functools.partial(axial_kernel, dims, n_ax),
         out_shape=(f32((2 * F, nr, na, nx)), f32(dims)),
@@ -622,31 +659,39 @@
         name="axial",
     )(sums, fourth, part_bw, ax_a, ax_b)
 
-    indicator, send = pl.pallas_call(
+    inside, ends, part_sums = pl.pallas_call(
+        functools.partial(rows_kernel, dims),
+        out_shape=(f32(dims), f32((2 * F, 4, na, nx)), f32((tiles, 8, nx))),
+        in_specs=[vmem] * 5,
+        out_specs=(vmem,) * 3,
+        compiler_params=pltpu.CompilerParams(vmem_limit_bytes=16 << 20),
+        name="rows",
+    )(primal, bw, done, azi_l, azi_r)
+    outside, send = pl.pallas_call(
         functools.partial(main_kernel, dims, n_rad),
-        out_shape=(f32(dims), f32((2 * n_dev, nx))),
-        in_specs=[vmem] * 9,
+        out_shape=(f32((4, na, nx)), f32((2 * n_dev, nx))),
+        in_specs=[vmem] * 6,
         out_specs=(vmem, vmem),
         compiler_params=pltpu.CompilerParams(vmem_limit_bytes=16 << 20),
-        name="stencil",
-    )(primal, adjoint, bw, done, azi_l, azi_r, rad_a, rad_b, row)
+        name="planes",
+    )(primal, ends, part_sums, rad_a, rad_b, row)
 
     data = lax.all_to_all(send, AXES, 0, 0, tiled=True)
 
     cost, load, indicator = pl.pallas_call(
         functools.partial(final_kernel, n_loc, per_ax),
         out_shape=(f32((per_rad, per_azi, per_ax)), f32((1, 1, 1)), f32(dims)),
-        in_specs=[vmem, anyspec],
+        in_specs=[vmem, anyspec, anyspec],
         out_specs=(anyspec,) * 3,
         scratch_shapes=[
             pltpu.VMEM((per_rad, per_azi, per_ax), jnp.float32),
             pltpu.VMEM((1, 1, 1), jnp.float32),
             pltpu.VMEM((n_dev // 8, 8, nx), jnp.float32),
-            pltpu.SemaphoreType.DMA((3,)),
+            pltpu.SemaphoreType.DMA((5,)),
         ],
         compiler_params=pltpu.CompilerParams(vmem_limit_bytes=4 << 20),
         name="blocks",
-    )(data, indicator)
+    )(data, inside, outside)
     return indicator, cost, load
 
 

time: 29 us -> 28.5 us (0.983)
  Pallas kernels: 10.6 us -> 9.49 us
  blocking collectives: 11.2 us -> 11.7 us
    pallas_call x1, Pallas kernels: 1.29 us -> 0.58 us  [on_device(): pl.pallas_call(functools.partial(main_kernel, dims, n_rad), out_shape=(f3...]
    all_to_all x1, blocking collectives: 11.2 us -> 11.7 us  [on_device(): data = lax.all_to_all(send, AXES, 0, 0, tiled=True)]
    pallas_call x3, Pallas kernels: 4.83 us -> 4.31 us  [the longest x1 2.88 us: on_device(): pl.pallas_call(functools.partial(inner_kernel, dims, ((per_rad, per_azi,...]
  transfers between devices with their start and end apart: 5 -> 5, of which waited for: 0 -> 0; matrix products, arithmetic and copies ran while one was open for 0% -> 0% of each run, Pallas kernels for 24% -> 23%
where the time goes in v8:
time: 28.5 us; the launch traced here: 28.3 us
  blocking collectives  11.7 us (41%)
  Pallas kernels  9.49 us (33%)
  starting transfers between devices  6.35 us (22%)
  between operations  0.76 us (3%)
    all_to_all x1, blocking collectives, on_device(): data = lax.all_to_all(send, AXES, 0, 0, tiled=True)  11.7 us
    ppermute x1, starting transfers between devices, on_device(): azi_l = lax.ppermute(azi_s, 'azi', ring(n_azi, 1))  3.03 us
    pallas_call x1, Pallas kernels, on_device(): pl.pallas_call(functools.partial(inner_kernel, dims, ((per_rad, per_azi,...  2.88 us
    pallas_call x1, Pallas kernels, on_device(): pl.pallas_call(functools.partial(axial_kernel, dims, n_ax), out_shape=(f3...  2.13 us
    ppermute x1, starting transfers between devices, on_device(): rad_a = lax.ppermute(rad_a, AXES, pair_round(sizes, 0, 0))  1.58 us
    pallas_call x1, Pallas kernels, on_device(): pl.pallas_call(functools.partial(edge_kernel, dims), out_shape=(f32((2 *...  1.53 us
    ppermute x1, starting transfers between devices, on_device(): ax_b = lax.ppermute(ax_second, AXES, pair_round(sizes, 2, 1))  1.17 us
    pallas_call x1, Pallas kernels, on_device(): pl.pallas_call(functools.partial(final_kernel, n_loc, per_ax), out_shape=...  0.94 us
  transfers between devices with their start and end apart: 5, of which 0 were waited for; matrix products, arithmetic and copies ran while one was open for 0% of the time, Pallas kernels for 23%

profile of v8, /device:TPU:0, one launch (start us, length us, event | category | flops | bytes accessed | tf_op | source)
XLA Modules:
  0.0 28.3 jit_solution(4975055849909535651)
XLA Ops:
  0.6 0.0 copy-start
  0.6 0.0 copy-start.1
  0.7 0.0 copy-start.2
  0.7 0.0 copy-start.5
  0.7 0.0 copy-start.3
  0.7 0.0 copy-start.4
  0.7 1.5 %edges.1 = (f32[10,2,32,128]{3,2,1,0:T(8,128)S(1)}, f32[10,2,32,128]{3,2,1,0:T(8,128)S(1)}, f32[10,16,4,128]{3,2,1,0:T(4,128)S(1)}) custom-call(f32[5,16,32,128]{3,2,1,0:T(8,128)} %prim.9, f32[5,16,32,128]{3,2,1,0:T(8,128)} %adj.5), custom_call_target="tpu_custom_call" | custom-call | tf_op jit(solution)/shard_map/edges/pallas_call | solution.py:598
  2.2 3.0 %collective-permute-start.2 = (f32[10,16,4,128]{3,2,1,0:T(4,128)S(1)}, f32[10,16,4,128]{3,2,1,0:T(4,128)S(1)}, u32[]{:S(2)}, u32[]{:S(2)}) collective-permute-start(f32[10,16,4,128]{3,2,1,0:T(4,128)S(1)} %get-tuple-element.29), channel_id=1, source_target_pairs={{0,4},{4,0},{1,5},{5,1},{2,6},{6,2},{3,7},{7,3},{8,12},{12,8},{9,1... | collective-permute-start | bytes 983048 | tf_op jit(solution)/shard_map/ppermute | solution.py:618
  5.3 1.6 %collective-permute-start.3 = (f32[10,2,32,128]{3,2,1,0:T(8,128)S(1)}, f32[10,2,32,128]{3,2,1,0:T(8,128)S(1)}, u32[]{:S(2)}, u32[]{:S(2)}) collective-permute-start(f32[10,2,32,128]{3,2,1,0:T(8,128)S(1)} %get-tuple-element.32), channel_id=1, source_target_pairs={{0,8},{1,9},{2,10},{3,11},{4,12},{5,13},{6,14},{7,15},{8,0},{9,1},... | collective-permute-start | bytes 983048 | tf_op jit(solution)/shard_map/ppermute | solution.py:620
  6.8 0.0 collective-permute-start.4
  6.8 0.0 copy-done
  6.8 0.0 copy-done.1
  6.8 0.7 %lanes.1 = (f32[10,1,8,128]{3,2,1,0:T(8,128)S(1)}, f32[10,1,8,128]{3,2,1,0:T(8,128)S(1)}) custom-call(f32[5,16,32,128]{3,2,1,0:T(8,128)S(1)} %copy-done, f32[5,16,32,128]{3,2,1,0:T(8,128)S(1)} %copy-done.1), custom_call_target="tpu_custom_call" | custom-call | tf_op jit(solution)/shard_map/lanes/pallas_call | solution.py:607
  7.6 0.6 %collective-permute-start = (f32[10,1,8,128]{3,2,1,0:T(8,128)S(1)}, f32[10,1,8,128]{3,2,1,0:T(8,128)S(1)}, u32[]{:S(2)}, u32[]{:S(2)}) collective-permute-start(f32[10,1,8,128]{3,2,1,0:T(8,128)S(1)} %get-tuple-element.22.ax_s), channel_id=1, source_target_pairs={{0,1},{1,0},{2,3},{3,2},{4,5},{5,4},{6,7},{7,6},{8,9},{9,8},{10,11... | collective-permute-start | bytes 122888 | tf_op jit(solution)/shard_map/ppermute | solution.py:616
  8.2 1.2 %collective-permute-start.1 = (f32[10,1,8,128]{3,2,1,0:T(8,128)S(1)}, f32[10,1,8,128]{3,2,1,0:T(8,128)S(1)}, u32[]{:S(2)}, u32[]{:S(2)}) collective-permute-start(f32[10,1,8,128]{3,2,1,0:T(8,128)S(1)} %get-tuple-element.26), channel_id=1, source_target_pairs={{0,3},{1,2},{2,1},{3,0},{4,7},{5,6},{6,5},{7,4},{8,11},{9,10},{10,... | collective-permute-start | bytes 122888 | tf_op jit(solution)/shard_map/ppermute | solution.py:617
  9.3 0.0 copy-done.2
  9.3 0.0 copy-done.5
  9.3 0.0 copy-done.3
  9.3 0.0 copy-done.4
  9.3 2.9 %inner.1 = (f32[2560,256]{1,0:T(8,128)S(1)}, f32[2560,128]{1,0:T(8,128)S(1)}, f32[1,256]{1,0:T(1,128)S(1)}, f32[10,16,32,128]{3,2,1,0:T(8,128)S(1)}) custom-call(f32[5,16,32,128]{3,2,1,0:T(8,128)S(1)} %copy-done, f32[5,16,32,128]{3,2,1,0:T(8,128)S(1)} %copy-done.1, f32[10,1,8,128]{3,2,1,0:T(8,128)S(1)} %get-tuple-element.22.ax_s, ...), custom_call_target="tpu_custom_call" | custom-call | tf_op jit(solution)/shard_map/inner/pallas_call | solution.py:627
  12.2 0.0 collective-permute-done.ax_a
  12.2 0.0 collective-permute-done.1.ax_b
  12.2 2.1 %axial.1 = (f32[10,16,32,128]{3,2,1,0:T(8,128)S(1)}, f32[16,32,128]{2,1,0:T(8,128)S(1)}) custom-call(f32[2560,256]{1,0:T(8,128)S(1)} %get-tuple-element.23.sums, f32[2560,128]{1,0:T(8,128)S(1)} %get-tuple-element.24.fourth, f32[10,16,32,128]{3,2,1,0:T(8,128)S(1)} %get-tuple-element.25.part_bw, f32[10,1,8,128]{3,2,1,0:T(8,128)S(1)} %collective-permute-done.ax_a, ...), custom_call_target="tpu_custom_call" | custom-call | tf_op jit(solution)/shard_map/axial/pallas_call | solution.py:646
  14.4 0.0 collective-permute-done.2.azi_l.azi_r
  14.4 0.7 %rows.1 = (f32[16,32,128]{2,1,0:T(8,128)S(1)}, f32[10,4,32,128]{3,2,1,0:T(8,128)S(1)}, f32[4,8,128]{2,1,0:T(8,128)S(1)}) custom-call(f32[5,16,32,128]{3,2,1,0:T(8,128)S(1)} %copy-done, f32[10,16,32,128]{3,2,1,0:T(8,128)S(1)} %get-tuple-element.27.bw, f32[16,32,128]{2,1,0:T(8,128)S(1)} %get-tuple-element.28.done, ...), custom_call_target="tpu_custom_call" | custom-call | tf_op jit(solution)/shard_map/rows/pallas_call | solution.py:662
  15.1 0.0 collective-permute-done.3.rad_a
  15.1 0.0 collective-permute-done.4.rad_b
  15.1 0.6 %planes.1 = (f32[4,32,128]{2,1,0:T(8,128)S(1)}, f32[64,128]{1,0:T(8,128)S(1)}) custom-call(f32[5,16,32,128]{3,2,1,0:T(8,128)S(1)} %copy-done, f32[10,4,32,128]{3,2,1,0:T(8,128)S(1)} %get-tuple-element.30.ends, f32[4,8,128]{2,1,0:T(8,128)S(1)} %get-tuple-element.31.part_sums, f32[10,2,32,128]{3,2,1,0:T(8,128)S(1)} %collective-permute-done.3.rad_a, ...), custom_call_target="tpu_custom_call" | custom-call | tf_op jit(solution)/shard_map/planes/pallas_call | solution.py:670
  15.7 11.7 %all_to_all.11 = f32[32,2,128]{2,1,0:T(2,128)S(1)} all-to-all(f32[32,2,128]{2,1,0:T(2,128)S(1)} %bitcast.4), channel_id=1, replica_groups=mesh['rad'=4,'azi'=2,'ax'=4] {'rad','azi','ax'}, dimensions={0} | all-to-all | bytes 65536 | tf_op jit(solution)/shard_map/all_to_all | solution.py:679
  27.4 0.9 %blocks.1 = (f32[1,2,8]{2,1,0:T(2,128)}, f32[1,1,1]{2,1,0:T(1,128)}, f32[16,32,128]{2,1,0:T(8,128)}) custom-call(f32[64,128]{1,0:T(8,128)S(1)} %bitcast.3, f32[16,32,128]{2,1,0:T(8,128)S(1)} %get-tuple-element.36.inside, f32[4,32,128]{2,1,0:T(8,128)S(1)} %get-tuple-element.37.outside), custom_call_target="tpu_custom_call" | custom-call | tf_op jit(solution)/shard_map/blocks/pallas_call | solution.py:681
Async XLA Ops:
  0.6 6.2 %copy-start = (f32[5,16,32,128]{3,2,1,0:T(8,128)S(1)}, f32[5,16,32,128]{3,2,1,0:T(8,128)}, u32[]{:S(2)}) copy-start(f32[5,16,32,128]{3,2,1,0:T(8,128)} %prim.9) | copy-start | bytes 3932164
  0.6 6.2 %copy-start.1 = (f32[5,16,32,128]{3,2,1,0:T(8,128)S(1)}, f32[5,16,32,128]{3,2,1,0:T(8,128)}, u32[]{:S(2)}) copy-start(f32[5,16,32,128]{3,2,1,0:T(8,128)} %adj.5) | copy-start | bytes 3932164
  0.7 8.7 %copy-start.2 = (s32[1,2,8,6]{2,1,3,0:T(2,128)S(1)}, s32[1,2,8,6]{2,1,3,0:T(2,128)}, u32[]{:S(2)}) copy-start(s32[1,2,8,6]{2,1,3,0:T(2,128)} %param.11) | copy-start | bytes 1156
  0.7 8.7 %copy-start.5 = (s32[1,2,8]{2,1,0:T(2,128)S(1)}, s32[1,2,8]{2,1,0:T(2,128)}, u32[]{:S(2)}) copy-start(s32[1,2,8]{2,1,0:T(2,128)} %weight.1) | copy-start | bytes 196
  0.7 8.7 %copy-start.3 = (s32[1,2,8]{2,1,0:T(2,128)S(1)}, s32[1,2,8]{2,1,0:T(2,128)}, u32[]{:S(2)}) copy-start(s32[1,2,8]{2,1,0:T(2,128)} %refine.1) | copy-start | bytes 196
  0.7 8.7 %copy-start.4 = (s32[1,2,8]{2,1,0:T(2,128)S(1)}, s32[1,2,8]{2,1,0:T(2,128)}, u32[]{:S(2)}) copy-start(s32[1,2,8]{2,1,0:T(2,128)} %owner.1) | copy-start | bytes 196
  2.2 12.2 %collective-permute-start.2 = (f32[10,16,4,128]{3,2,1,0:T(4,128)S(1)}, f32[10,16,4,128]{3,2,1,0:T(4,128)S(1)}, u32[]{:S(2)}, u32[]{:S(2)}) collective-permute-start(f32[10,16,4,128]{3,2,1,0:T(4,128)S(1)} %get-tuple-element.29), channel_id=1, source_target_pairs={{0,4},{4,0},{1,5},{5,1},{2,6},{6,2},{3,7},{7,3},{8,12},{12,8},{9,1... | collective-permute-start | bytes 983048 | tf_op jit(solution)/shard_map/ppermute | solution.py:618
  5.3 9.8 %collective-permute-start.3 = (f32[10,2,32,128]{3,2,1,0:T(8,128)S(1)}, f32[10,2,32,128]{3,2,1,0:T(8,128)S(1)}, u32[]{:S(2)}, u32[]{:S(2)}) collective-permute-start(f32[10,2,32,128]{3,2,1,0:T(8,128)S(1)} %get-tuple-element.32), channel_id=1, source_target_pairs={{0,8},{1,9},{2,10},{3,11},{4,12},{5,13},{6,14},{7,15},{8,0},{9,1},... | collective-permute-start | bytes 983048 | tf_op jit(solution)/shard_map/ppermute | solution.py:620
  6.8 8.3 %collective-permute-start.4 = (f32[10,2,32,128]{3,2,1,0:T(8,128)S(1)}, f32[10,2,32,128]{3,2,1,0:T(8,128)S(1)}, u32[]{:S(2)}, u32[]{:S(2)}) collective-permute-start(f32[10,2,32,128]{3,2,1,0:T(8,128)S(1)} %get-tuple-element.33), channel_id=1, source_target_pairs={{0,1},{1,0},{2,3},{3,2},{4,5},{5,4},{6,7},{7,6},{8,16},{9,17},{10,... | collective-permute-start | bytes 983048 | tf_op jit(solution)/shard_map/ppermute | solution.py:621
  7.6 4.6 %collective-permute-start = (f32[10,1,8,128]{3,2,1,0:T(8,128)S(1)}, f32[10,1,8,128]{3,2,1,0:T(8,128)S(1)}, u32[]{:S(2)}, u32[]{:S(2)}) collective-permute-start(f32[10,1,8,128]{3,2,1,0:T(8,128)S(1)} %get-tuple-element.22.ax_s), channel_id=1, source_target_pairs={{0,1},{1,0},{2,3},{3,2},{4,5},{5,4},{6,7},{7,6},{8,9},{9,8},{10,11... | collective-permute-start | bytes 122888 | tf_op jit(solution)/shard_map/ppermute | solution.py:616
  8.2 4.1 %collective-permute-start.1 = (f32[10,1,8,128]{3,2,1,0:T(8,128)S(1)}, f32[10,1,8,128]{3,2,1,0:T(8,128)S(1)}, u32[]{:S(2)}, u32[]{:S(2)}) collective-permute-start(f32[10,1,8,128]{3,2,1,0:T(8,128)S(1)} %get-tuple-element.26), channel_id=1, source_target_pairs={{0,3},{1,2},{2,1},{3,0},{4,7},{5,6},{6,5},{7,4},{8,11},{9,10},{10,... | collective-permute-start | bytes 122888 | tf_op jit(solution)/shard_map/ppermute | solution.py:617

commit v9 on v8

--- a/solution.py
+++ b/solution.py
@@ -224,7 +224,7 @@
     for r in (0, 1, nr - 2, nr - 1):
         for a in range(tiles):
             tile(r, a, False)
-    lax.fori_loop(2, nr - 2, body, 0)
+    lax.fori_loop(2, nr - 2, body, 0, unroll=True)
 
 
 def shifted(src, f, r, a, tiles, da):
@@ -466,7 +466,7 @@
         return tuple(out)
 
     zero = jnp.zeros((8, nx), jnp.float32)
-    sums = lax.fori_loop(2, nr - 2, plane, (zero,) * tiles)
+    sums = lax.fori_loop(2, nr - 2, plane, (zero,) * tiles, unroll=True)
     for a in range(tiles):
         part_sums[a] = sums[a]
 
@@ -492,16 +492,25 @@
     groups = nx // BLK
     halves_a = na // BLK
     per_tile = BLK // 8
-    means = jnp.zeros((8, nx), jnp.float32)
+    i = lax.broadcasted_iota(jnp.int32, (nx, nx), 0)
+    c = lax.broadcasted_iota(jnp.int32, (nx, nx), 1)
+    gather = jnp.where(i // BLK == c % groups, 1.0, 0.0)
+    rows = []
     for b in range(halves_a):
         t = sums[b * per_tile]
         for i in range(1, per_tile):
             t = t + sums[b * per_tile + i]
-        t = jnp.broadcast_to(jnp.sum(t, axis=0, keepdims=True), (8, nx))
-        for sh in (8, 4, 2, 1):
-            t = t + pltpu.roll(t, nx - sh, 1)
-        t = jnp.take_along_axis(t, (lane % groups) * BLK, axis=1)
-        means = jnp.where(lane // groups == b, t, means)
+        rows.append(t)
+    rows = jnp.dot(
+        jnp.concatenate(rows, axis=0),
+        gather,
+        precision=lax.Precision.HIGHEST,
+        preferred_element_type=jnp.float32,
+    )
+    means = jnp.zeros((8, nx), jnp.float32)
+    for b in range(halves_a):
+        t = jnp.sum(rows[8 * b:8 * b + 8], axis=0, keepdims=True)
+        means = jnp.where(lane // groups == b, jnp.broadcast_to(t, (8, nx)), means)
     means = means * (1.0 / BLK**3)
     head = jnp.broadcast_to(row[:, 0:nx], (8, nx))
     head = jnp.where(lane < groups * halves_a, means, head)

time: 28.5 us -> 28.2 us (0.989)
  Pallas kernels: 9.49 us -> 8.77 us
  blocking collectives: 11.7 us -> 12.1 us
    all_to_all x1, blocking collectives: 11.7 us -> 12.1 us  [on_device(): data = lax.all_to_all(send, AXES, 0, 0, tiled=True)]
    pallas_call x1, Pallas kernels: 2.13 us -> 1.76 us  [on_device(): pl.pallas_call(functools.partial(axial_kernel, dims, n_ax), out_shape=(f3...]
  transfers between devices with their start and end apart: 5 -> 5, of which waited for: 0 -> 0; matrix products, arithmetic and copies ran while one was open for 0% -> 0% of each run, Pallas kernels for 23% -> 21%
where the time goes in v9:
time: 28.2 us; the launch traced here: 28 us
  blocking collectives  12.1 us (43%)
  Pallas kernels  8.77 us (31%)
  starting transfers between devices  6.35 us (23%)
  between operations  0.77 us (3%)
    all_to_all x1, blocking collectives, on_device(): data = lax.all_to_all(send, AXES, 0, 0, tiled=True)  12.1 us
    ppermute x1, starting transfers between devices, on_device(): azi_l = lax.ppermute(azi_s, 'azi', ring(n_azi, 1))  3.03 us
    pallas_call x1, Pallas kernels, on_device(): pl.pallas_call(functools.partial(inner_kernel, dims, ((per_rad, per_azi,...  2.88 us
    pallas_call x1, Pallas kernels, on_device(): pl.pallas_call(functools.partial(axial_kernel, dims, n_ax), out_shape=(f3...  1.76 us
    ppermute x1, starting transfers between devices, on_device(): rad_a = lax.ppermute(rad_a, AXES, pair_round(sizes, 0, 0))  1.58 us
    pallas_call x1, Pallas kernels, on_device(): pl.pallas_call(functools.partial(edge_kernel, dims), out_shape=(f32((2 *...  1.53 us
    ppermute x1, starting transfers between devices, on_device(): ax_b = lax.ppermute(ax_second, AXES, pair_round(sizes, 2, 1))  1.17 us
    pallas_call x1, Pallas kernels, on_device(): pl.pallas_call(functools.partial(final_kernel, n_loc, per_ax), out_shape=...  0.94 us
  transfers between devices with their start and end apart: 5, of which 0 were waited for; matrix products, arithmetic and copies ran while one was open for 0% of the time, Pallas kernels for 21%

profile of v9, /device:TPU:0, one launch (start us, length us, event | category | flops | bytes accessed | tf_op | source)
XLA Modules:
  0.0 28.0 jit_solution(12053092157269748732)
XLA Ops:
  0.6 0.0 copy-start
  0.6 0.0 copy-start.1
  0.7 0.0 copy-start.2
  0.7 0.0 copy-start.5
  0.7 0.0 copy-start.3
  0.7 0.0 copy-start.4
  0.7 1.5 %edges.1 = (f32[10,2,32,128]{3,2,1,0:T(8,128)S(1)}, f32[10,2,32,128]{3,2,1,0:T(8,128)S(1)}, f32[10,16,4,128]{3,2,1,0:T(4,128)S(1)}) custom-call(f32[5,16,32,128]{3,2,1,0:T(8,128)} %prim.9, f32[5,16,32,128]{3,2,1,0:T(8,128)} %adj.5), custom_call_target="tpu_custom_call" | custom-call | tf_op jit(solution)/shard_map/edges/pallas_call | solution.py:607
  2.2 3.0 %collective-permute-start.2 = (f32[10,16,4,128]{3,2,1,0:T(4,128)S(1)}, f32[10,16,4,128]{3,2,1,0:T(4,128)S(1)}, u32[]{:S(2)}, u32[]{:S(2)}) collective-permute-start(f32[10,16,4,128]{3,2,1,0:T(4,128)S(1)} %get-tuple-element.29), channel_id=1, source_target_pairs={{0,4},{4,0},{1,5},{5,1},{2,6},{6,2},{3,7},{7,3},{8,12},{12,8},{9,1... | collective-permute-start | bytes 983048 | tf_op jit(solution)/shard_map/ppermute | solution.py:627
  5.3 1.6 %collective-permute-start.3 = (f32[10,2,32,128]{3,2,1,0:T(8,128)S(1)}, f32[10,2,32,128]{3,2,1,0:T(8,128)S(1)}, u32[]{:S(2)}, u32[]{:S(2)}) collective-permute-start(f32[10,2,32,128]{3,2,1,0:T(8,128)S(1)} %get-tuple-element.32), channel_id=1, source_target_pairs={{0,8},{1,9},{2,10},{3,11},{4,12},{5,13},{6,14},{7,15},{8,0},{9,1},... | collective-permute-start | bytes 983048 | tf_op jit(solution)/shard_map/ppermute | solution.py:629
  6.8 0.0 collective-permute-start.4
  6.8 0.0 copy-done
  6.8 0.0 copy-done.1
  6.8 0.7 %lanes.1 = (f32[10,1,8,128]{3,2,1,0:T(8,128)S(1)}, f32[10,1,8,128]{3,2,1,0:T(8,128)S(1)}) custom-call(f32[5,16,32,128]{3,2,1,0:T(8,128)S(1)} %copy-done, f32[5,16,32,128]{3,2,1,0:T(8,128)S(1)} %copy-done.1), custom_call_target="tpu_custom_call" | custom-call | tf_op jit(solution)/shard_map/lanes/pallas_call | solution.py:616
  7.6 0.6 %collective-permute-start = (f32[10,1,8,128]{3,2,1,0:T(8,128)S(1)}, f32[10,1,8,128]{3,2,1,0:T(8,128)S(1)}, u32[]{:S(2)}, u32[]{:S(2)}) collective-permute-start(f32[10,1,8,128]{3,2,1,0:T(8,128)S(1)} %get-tuple-element.22.ax_s), channel_id=1, source_target_pairs={{0,1},{1,0},{2,3},{3,2},{4,5},{5,4},{6,7},{7,6},{8,9},{9,8},{10,11... | collective-permute-start | bytes 122888 | tf_op jit(solution)/shard_map/ppermute | solution.py:625
  8.2 1.2 %collective-permute-start.1 = (f32[10,1,8,128]{3,2,1,0:T(8,128)S(1)}, f32[10,1,8,128]{3,2,1,0:T(8,128)S(1)}, u32[]{:S(2)}, u32[]{:S(2)}) collective-permute-start(f32[10,1,8,128]{3,2,1,0:T(8,128)S(1)} %get-tuple-element.26), channel_id=1, source_target_pairs={{0,3},{1,2},{2,1},{3,0},{4,7},{5,6},{6,5},{7,4},{8,11},{9,10},{10,... | collective-permute-start | bytes 122888 | tf_op jit(solution)/shard_map/ppermute | solution.py:626
  9.3 0.0 copy-done.2
  9.3 0.0 copy-done.5
  9.3 0.0 copy-done.3
  9.3 0.0 copy-done.4
  9.3 2.9 %inner.1 = (f32[2560,256]{1,0:T(8,128)S(1)}, f32[2560,128]{1,0:T(8,128)S(1)}, f32[1,256]{1,0:T(1,128)S(1)}, f32[10,16,32,128]{3,2,1,0:T(8,128)S(1)}) custom-call(f32[5,16,32,128]{3,2,1,0:T(8,128)S(1)} %copy-done, f32[5,16,32,128]{3,2,1,0:T(8,128)S(1)} %copy-done.1, f32[10,1,8,128]{3,2,1,0:T(8,128)S(1)} %get-tuple-element.22.ax_s, ...), custom_call_target="tpu_custom_call" | custom-call | tf_op jit(solution)/shard_map/inner/pallas_call | solution.py:636
  12.2 0.0 collective-permute-done.ax_a
  12.2 0.0 collective-permute-done.1.ax_b
  12.2 1.8 %axial.1 = (f32[10,16,32,128]{3,2,1,0:T(8,128)S(1)}, f32[16,32,128]{2,1,0:T(8,128)S(1)}) custom-call(f32[2560,256]{1,0:T(8,128)S(1)} %get-tuple-element.23.sums, f32[2560,128]{1,0:T(8,128)S(1)} %get-tuple-element.24.fourth, f32[10,16,32,128]{3,2,1,0:T(8,128)S(1)} %get-tuple-element.25.part_bw, f32[10,1,8,128]{3,2,1,0:T(8,128)S(1)} %collective-permute-done.ax_a, ...), custom_call_target="tpu_custom_call" | custom-call | tf_op jit(solution)/shard_map/axial/pallas_call | solution.py:655
  14.0 0.0 collective-permute-done.2.azi_l.azi_r
  14.0 0.5 %rows.1 = (f32[16,32,128]{2,1,0:T(8,128)S(1)}, f32[10,4,32,128]{3,2,1,0:T(8,128)S(1)}, f32[4,8,128]{2,1,0:T(8,128)S(1)}) custom-call(f32[5,16,32,128]{3,2,1,0:T(8,128)S(1)} %copy-done, f32[10,16,32,128]{3,2,1,0:T(8,128)S(1)} %get-tuple-element.27.bw, f32[16,32,128]{2,1,0:T(8,128)S(1)} %get-tuple-element.28.done, ...), custom_call_target="tpu_custom_call" | custom-call | tf_op jit(solution)/shard_map/rows/pallas_call | solution.py:671
  14.6 0.0 collective-permute-done.3.rad_a
  14.6 0.0 collective-permute-done.4.rad_b
  14.6 0.4 %planes.1 = (f32[4,32,128]{2,1,0:T(8,128)S(1)}, f32[64,128]{1,0:T(8,128)S(1)}) custom-call(f32[5,16,32,128]{3,2,1,0:T(8,128)S(1)} %copy-done, f32[10,4,32,128]{3,2,1,0:T(8,128)S(1)} %get-tuple-element.30.ends, f32[4,8,128]{2,1,0:T(8,128)S(1)} %get-tuple-element.31.part_sums, f32[10,2,32,128]{3,2,1,0:T(8,128)S(1)} %collective-permute-done.3.rad_a, ...), custom_call_target="tpu_custom_call" | custom-call | tf_op jit(solution)/shard_map/planes/pallas_call | solution.py:679
  15.0 12.1 %all_to_all.11 = f32[32,2,128]{2,1,0:T(2,128)S(1)} all-to-all(f32[32,2,128]{2,1,0:T(2,128)S(1)} %bitcast.4), channel_id=1, replica_groups=mesh['rad'=4,'azi'=2,'ax'=4] {'rad','azi','ax'}, dimensions={0} | all-to-all | bytes 65536 | tf_op jit(solution)/shard_map/all_to_all | solution.py:688
  27.1 0.9 %blocks.1 = (f32[1,2,8]{2,1,0:T(2,128)}, f32[1,1,1]{2,1,0:T(1,128)}, f32[16,32,128]{2,1,0:T(8,128)}) custom-call(f32[64,128]{1,0:T(8,128)S(1)} %bitcast.3, f32[16,32,128]{2,1,0:T(8,128)S(1)} %get-tuple-element.36.inside, f32[4,32,128]{2,1,0:T(8,128)S(1)} %get-tuple-element.37.outside), custom_call_target="tpu_custom_call" | custom-call | tf_op jit(solution)/shard_map/blocks/pallas_call | solution.py:690
Async XLA Ops:
  0.6 6.2 %copy-start = (f32[5,16,32,128]{3,2,1,0:T(8,128)S(1)}, f32[5,16,32,128]{3,2,1,0:T(8,128)}, u32[]{:S(2)}) copy-start(f32[5,16,32,128]{3,2,1,0:T(8,128)} %prim.9) | copy-start | bytes 3932164
  0.6 6.2 %copy-start.1 = (f32[5,16,32,128]{3,2,1,0:T(8,128)S(1)}, f32[5,16,32,128]{3,2,1,0:T(8,128)}, u32[]{:S(2)}) copy-start(f32[5,16,32,128]{3,2,1,0:T(8,128)} %adj.5) | copy-start | bytes 3932164
  0.7 8.7 %copy-start.2 = (s32[1,2,8,6]{2,1,3,0:T(2,128)S(1)}, s32[1,2,8,6]{2,1,3,0:T(2,128)}, u32[]{:S(2)}) copy-start(s32[1,2,8,6]{2,1,3,0:T(2,128)} %param.11) | copy-start | bytes 1156
  0.7 8.7 %copy-start.5 = (s32[1,2,8]{2,1,0:T(2,128)S(1)}, s32[1,2,8]{2,1,0:T(2,128)}, u32[]{:S(2)}) copy-start(s32[1,2,8]{2,1,0:T(2,128)} %weight.1) | copy-start | bytes 196
  0.7 8.7 %copy-start.3 = (s32[1,2,8]{2,1,0:T(2,128)S(1)}, s32[1,2,8]{2,1,0:T(2,128)}, u32[]{:S(2)}) copy-start(s32[1,2,8]{2,1,0:T(2,128)} %refine.1) | copy-start | bytes 196
  0.7 8.7 %copy-start.4 = (s32[1,2,8]{2,1,0:T(2,128)S(1)}, s32[1,2,8]{2,1,0:T(2,128)}, u32[]{:S(2)}) copy-start(s32[1,2,8]{2,1,0:T(2,128)} %owner.1) | copy-start | bytes 196
  2.2 11.8 %collective-permute-start.2 = (f32[10,16,4,128]{3,2,1,0:T(4,128)S(1)}, f32[10,16,4,128]{3,2,1,0:T(4,128)S(1)}, u32[]{:S(2)}, u32[]{:S(2)}) collective-permute-start(f32[10,16,4,128]{3,2,1,0:T(4,128)S(1)} %get-tuple-element.29), channel_id=1, source_target_pairs={{0,4},{4,0},{1,5},{5,1},{2,6},{6,2},{3,7},{7,3},{8,12},{12,8},{9,1... | collective-permute-start | bytes 983048 | tf_op jit(solution)/shard_map/ppermute | solution.py:627
  5.3 9.3 %collective-permute-start.3 = (f32[10,2,32,128]{3,2,1,0:T(8,128)S(1)}, f32[10,2,32,128]{3,2,1,0:T(8,128)S(1)}, u32[]{:S(2)}, u32[]{:S(2)}) collective-permute-start(f32[10,2,32,128]{3,2,1,0:T(8,128)S(1)} %get-tuple-element.32), channel_id=1, source_target_pairs={{0,8},{1,9},{2,10},{3,11},{4,12},{5,13},{6,14},{7,15},{8,0},{9,1},... | collective-permute-start | bytes 983048 | tf_op jit(solution)/shard_map/ppermute | solution.py:629
  6.8 7.7 %collective-permute-start.4 = (f32[10,2,32,128]{3,2,1,0:T(8,128)S(1)}, f32[10,2,32,128]{3,2,1,0:T(8,128)S(1)}, u32[]{:S(2)}, u32[]{:S(2)}) collective-permute-start(f32[10,2,32,128]{3,2,1,0:T(8,128)S(1)} %get-tuple-element.33), channel_id=1, source_target_pairs={{0,1},{1,0},{2,3},{3,2},{4,5},{5,4},{6,7},{7,6},{8,16},{9,17},{10,... | collective-permute-start | bytes 983048 | tf_op jit(solution)/shard_map/ppermute | solution.py:630
  7.6 4.6 %collective-permute-start = (f32[10,1,8,128]{3,2,1,0:T(8,128)S(1)}, f32[10,1,8,128]{3,2,1,0:T(8,128)S(1)}, u32[]{:S(2)}, u32[]{:S(2)}) collective-permute-start(f32[10,1,8,128]{3,2,1,0:T(8,128)S(1)} %get-tuple-element.22.ax_s), channel_id=1, source_target_pairs={{0,1},{1,0},{2,3},{3,2},{4,5},{5,4},{6,7},{7,6},{8,9},{9,8},{10,11... | collective-permute-start | bytes 122888 | tf_op jit(solution)/shard_map/ppermute | solution.py:625
  8.2 4.1 %collective-permute-start.1 = (f32[10,1,8,128]{3,2,1,0:T(8,128)S(1)}, f32[10,1,8,128]{3,2,1,0:T(8,128)S(1)}, u32[]{:S(2)}, u32[]{:S(2)}) collective-permute-start(f32[10,1,8,128]{3,2,1,0:T(8,128)S(1)} %get-tuple-element.26), channel_id=1, source_target_pairs={{0,3},{1,2},{2,1},{3,0},{4,7},{5,6},{6,5},{7,4},{8,11},{9,10},{10,... | collective-permute-start | bytes 122888 | tf_op jit(solution)/shard_map/ppermute | solution.py:626

commit v10 on v9

--- a/solution.py
+++ b/solution.py
@@ -56,14 +56,21 @@
         c.wait()
 
 
-def lane_kernel(dims, prim, adj, first, second):
+def lane_kernel(dims, prim_in, adj_in, dep, prim, adj, first, second, sems):
     nr, na, nx = dims
+    del dep
+    loads = {}
+    for t, (src, dst) in enumerate(((prim_in, prim), (adj_in, adj))):
+        for f in range(F):
+            loads[t, f] = pltpu.make_async_copy(src.at[f], dst.at[f], sems.at[t, f])
+            loads[t, f].start()
     even = lax.rem(lax.axis_index("ax"), 2) == 0
     slot = lax.broadcasted_iota(jnp.int32, (8, nx), 1) >> 1
     tiles = na // 8
     per = nx // 2
     for t, src in enumerate((prim, adj)):
         for f in range(F):
+            loads[t, f].wait()
             for h in range(nr * tiles // per):
                 upper = lower = jnp.zeros((8, nx), jnp.float32)
                 for j in range(per):
@@ -613,14 +620,16 @@
         compiler_params=pltpu.CompilerParams(vmem_limit_bytes=8 << 20),
         name="edges",
     )(*(pltpu.with_memory_space_constraint(x, pltpu.HBM) for x in (primal, adjoint)))
-    ax_first, ax_second = pl.pallas_call(
+    field = f32(primal.shape)
+    primal, adjoint, ax_first, ax_second = pl.pallas_call(
         functools.partial(lane_kernel, dims),
-        out_shape=(f32((2 * F, halves // 2, 8, nx)),) * 2,
-        in_specs=[vmem, vmem],
-        out_specs=(vmem, vmem),
+        out_shape=(field, field) + (f32((2 * F, halves // 2, 8, nx)),) * 2,
+        in_specs=[hbm, hbm, anyspec],
+        out_specs=(vmem,) * 4,
+        scratch_shapes=[pltpu.SemaphoreType.DMA((2, F))],
         compiler_params=pltpu.CompilerParams(vmem_limit_bytes=16 << 20),
         name="lanes",
-    )(primal, adjoint)
+    )(*(pltpu.with_memory_space_constraint(x, pltpu.HBM) for x in (primal, adjoint)), rad_b)
 
     ax_a = lax.ppermute(ax_first, AXES, pair_round(sizes, 2, 0))
     ax_b = lax.ppermute(ax_second, AXES, pair_round(sizes, 2, 1))

time: 28.2 us -> 28.2 us (level)
  Pallas kernels: 8.77 us -> 10.3 us
  blocking collectives: 12.1 us -> 10.6 us
    pallas_call x1, Pallas kernels: 0.73 us -> 2.41 us  [on_device(): pl.pallas_call(functools.partial(lane_kernel, dims), out_shape=(field, fi...]
    all_to_all x1, blocking collectives: 12.1 us -> 10.6 us  [on_device(): data = lax.all_to_all(send, AXES, 0, 0, tiled=True)]
    ppermute x1, starting transfers between devices: 0.57 us -> 0.02 us  [on_device(): ax_a = lax.ppermute(ax_first, AXES, pair_round(sizes, 2, 0))]
    ppermute x1, starting transfers between devices: 1.17 us -> 1.65 us  [on_device(): ax_b = lax.ppermute(ax_second, AXES, pair_round(sizes, 2, 1))]
  transfers between devices with their start and end apart: 5 -> 5, of which waited for: 0 -> 0; matrix products, arithmetic and copies ran while one was open for 0% -> 0% of each run, Pallas kernels for 21% -> 27%
where the time goes in v10:
time: 28.2 us; the launch traced here: 28 us
  blocking collectives  10.6 us (38%)
  Pallas kernels  10.3 us (37%)
  starting transfers between devices  6.35 us (23%)
  between operations  0.73 us (3%)
    all_to_all x1, blocking collectives, on_device(): data = lax.all_to_all(send, AXES, 0, 0, tiled=True)  10.6 us
    ppermute x1, starting transfers between devices, on_device(): azi_l = lax.ppermute(azi_s, 'azi', ring(n_azi, 1))  3.03 us
    pallas_call x1, Pallas kernels, on_device(): pl.pallas_call(functools.partial(inner_kernel, dims, ((per_rad, per_azi,...  2.88 us
    pallas_call x1, Pallas kernels, on_device(): pl.pallas_call(functools.partial(lane_kernel, dims), out_shape=(field, fi...  2.41 us
    pallas_call x1, Pallas kernels, on_device(): pl.pallas_call(functools.partial(axial_kernel, dims, n_ax), out_shape=(f3...  1.76 us
    ppermute x1, starting transfers between devices, on_device(): ax_b = lax.ppermute(ax_second, AXES, pair_round(sizes, 2, 1))  1.65 us
    ppermute x1, starting transfers between devices, on_device(): rad_a = lax.ppermute(rad_a, AXES, pair_round(sizes, 0, 0))  1.58 us
    pallas_call x1, Pallas kernels, on_device(): pl.pallas_call(functools.partial(edge_kernel, dims), out_shape=(f32((2 *...  1.38 us
  transfers between devices with their start and end apart: 5, of which 0 were waited for; matrix products, arithmetic and copies ran while one was open for 0% of the time, Pallas kernels for 27%

profile of v10, /device:TPU:0, one launch (start us, length us, event | category | flops | bytes accessed | tf_op | source)
XLA Modules:
  0.0 28.0 jit_solution(16129081098898385344)
XLA Ops:
  0.6 1.4 %edges.1 = (f32[10,2,32,128]{3,2,1,0:T(8,128)S(1)}, f32[10,2,32,128]{3,2,1,0:T(8,128)S(1)}, f32[10,16,4,128]{3,2,1,0:T(4,128)S(1)}) custom-call(f32[5,16,32,128]{3,2,1,0:T(8,128)} %prim_in.1, f32[5,16,32,128]{3,2,1,0:T(8,128)} %adj_in.1), custom_call_target="tpu_custom_call" | custom-call | tf_op jit(solution)/shard_map/edges/pallas_call | solution.py:614
  2.0 3.0 %collective-permute-start.2 = (f32[10,16,4,128]{3,2,1,0:T(4,128)S(1)}, f32[10,16,4,128]{3,2,1,0:T(4,128)S(1)}, u32[]{:S(2)}, u32[]{:S(2)}) collective-permute-start(f32[10,16,4,128]{3,2,1,0:T(4,128)S(1)} %get-tuple-element.34), channel_id=1, source_target_pairs={{0,4},{4,0},{1,5},{5,1},{2,6},{6,2},{3,7},{7,3},{8,12},{12,8},{9,1... | collective-permute-start | bytes 983048 | tf_op jit(solution)/shard_map/ppermute | solution.py:636
  5.1 1.6 %collective-permute-start.3 = (f32[10,2,32,128]{3,2,1,0:T(8,128)S(1)}, f32[10,2,32,128]{3,2,1,0:T(8,128)S(1)}, u32[]{:S(2)}, u32[]{:S(2)}) collective-permute-start(f32[10,2,32,128]{3,2,1,0:T(8,128)S(1)} %get-tuple-element.37), channel_id=1, source_target_pairs={{0,8},{1,9},{2,10},{3,11},{4,12},{5,13},{6,14},{7,15},{8,0},{9,1},... | collective-permute-start | bytes 983048 | tf_op jit(solution)/shard_map/ppermute | solution.py:638
  6.6 0.0 copy-start
  6.6 0.0 copy-start.1
  6.6 0.0 copy-start.2
  6.6 0.0 copy-start.3
  6.6 0.1 collective-permute-start.4
  6.7 2.4 %lanes.1 = (f32[5,16,32,128]{3,2,1,0:T(8,128)S(1)}, f32[5,16,32,128]{3,2,1,0:T(8,128)S(1)}, f32[10,1,8,128]{3,2,1,0:T(8,128)S(1)}, f32[10,1,8,128]{3,2,1,0:T(8,128)S(1)}) custom-call(f32[5,16,32,128]{3,2,1,0:T(8,128)} %prim_in.1, f32[5,16,32,128]{3,2,1,0:T(8,128)} %adj_in.1, f32[10,2,32,128]{3,2,1,0:T(8,128)S(1)} %get-tuple-element.24.dep), custom_call_target="tpu_custom_call" | custom-call | tf_op jit(solution)/shard_map/lanes/pallas_call | solution.py:624
  9.1 1.7 %collective-permute-start.1 = (f32[10,1,8,128]{3,2,1,0:T(8,128)S(1)}, f32[10,1,8,128]{3,2,1,0:T(8,128)S(1)}, u32[]{:S(2)}, u32[]{:S(2)}) collective-permute-start(f32[10,1,8,128]{3,2,1,0:T(8,128)S(1)} %get-tuple-element.31), channel_id=1, source_target_pairs={{0,3},{1,2},{2,1},{3,0},{4,7},{5,6},{6,5},{7,4},{8,11},{9,10},{10,... | collective-permute-start | bytes 122888 | tf_op jit(solution)/shard_map/ppermute | solution.py:635
  10.8 0.0 collective-permute-start
  10.8 0.0 copy-done
  10.8 0.0 copy-done.1
  10.8 0.0 copy-done.2
  10.8 0.0 copy-done.3
  10.8 2.9 %inner.1 = (f32[2560,256]{1,0:T(8,128)S(1)}, f32[2560,128]{1,0:T(8,128)S(1)}, f32[1,256]{1,0:T(1,128)S(1)}, f32[10,16,32,128]{3,2,1,0:T(8,128)S(1)}) custom-call(f32[5,16,32,128]{3,2,1,0:T(8,128)S(1)} %get-tuple-element.25.prim, f32[5,16,32,128]{3,2,1,0:T(8,128)S(1)} %get-tuple-element.26.adj, f32[10,1,8,128]{3,2,1,0:T(8,128)S(1)} %get-tuple-element.27.ax_s, ...), custom_call_target="tpu_custom_call" | custom-call | tf_op jit(solution)/shard_map/inner/pallas_call | solution.py:645
  13.7 0.0 collective-permute-done.1.ax_b
  13.7 0.0 collective-permute-done.ax_a
  13.7 1.8 %axial.1 = (f32[10,16,32,128]{3,2,1,0:T(8,128)S(1)}, f32[16,32,128]{2,1,0:T(8,128)S(1)}) custom-call(f32[2560,256]{1,0:T(8,128)S(1)} %get-tuple-element.28.sums, f32[2560,128]{1,0:T(8,128)S(1)} %get-tuple-element.29.fourth, f32[10,16,32,128]{3,2,1,0:T(8,128)S(1)} %get-tuple-element.30.part_bw, f32[10,1,8,128]{3,2,1,0:T(8,128)S(1)} %collective-permute-done.ax_a, ...), custom_call_target="tpu_custom_call" | custom-call | tf_op jit(solution)/shard_map/axial/pallas_call | solution.py:664
  15.5 0.0 collective-permute-done.2.azi_l.azi_r
  15.5 0.5 %rows.1 = (f32[16,32,128]{2,1,0:T(8,128)S(1)}, f32[10,4,32,128]{3,2,1,0:T(8,128)S(1)}, f32[4,8,128]{2,1,0:T(8,128)S(1)}) custom-call(f32[5,16,32,128]{3,2,1,0:T(8,128)S(1)} %get-tuple-element.25.prim, f32[10,16,32,128]{3,2,1,0:T(8,128)S(1)} %get-tuple-element.32.bw, f32[16,32,128]{2,1,0:T(8,128)S(1)} %get-tuple-element.33.done, ...), custom_call_target="tpu_custom_call" | custom-call | tf_op jit(solution)/shard_map/rows/pallas_call | solution.py:680
  16.1 0.0 collective-permute-done.3.rad_a
  16.1 0.0 collective-permute-done.4.rad_b
  16.1 0.4 %planes.1 = (f32[4,32,128]{2,1,0:T(8,128)S(1)}, f32[64,128]{1,0:T(8,128)S(1)}) custom-call(f32[5,16,32,128]{3,2,1,0:T(8,128)S(1)} %get-tuple-element.25.prim, f32[10,4,32,128]{3,2,1,0:T(8,128)S(1)} %get-tuple-element.35.ends, f32[4,8,128]{2,1,0:T(8,128)S(1)} %get-tuple-element.36.part_sums, f32[10,2,32,128]{3,2,1,0:T(8,128)S(1)} %collective-permute-done.3.rad_a, ...), custom_call_target="tpu_custom_call" | custom-call | tf_op jit(solution)/shard_map/planes/pallas_call | solution.py:688
  16.5 10.6 %all_to_all.11 = f32[32,2,128]{2,1,0:T(2,128)S(1)} all-to-all(f32[32,2,128]{2,1,0:T(2,128)S(1)} %bitcast.4), channel_id=1, replica_groups=mesh['rad'=4,'azi'=2,'ax'=4] {'rad','azi','ax'}, dimensions={0} | all-to-all | bytes 65536 | tf_op jit(solution)/shard_map/all_to_all | solution.py:697
  27.0 0.9 %blocks.1 = (f32[1,2,8]{2,1,0:T(2,128)}, f32[1,1,1]{2,1,0:T(1,128)}, f32[16,32,128]{2,1,0:T(8,128)}) custom-call(f32[64,128]{1,0:T(8,128)S(1)} %bitcast.3, f32[16,32,128]{2,1,0:T(8,128)S(1)} %get-tuple-element.40.inside, f32[4,32,128]{2,1,0:T(8,128)S(1)} %get-tuple-element.41.outside), custom_call_target="tpu_custom_call" | custom-call | tf_op jit(solution)/shard_map/blocks/pallas_call | solution.py:699
Async XLA Ops:
  2.0 13.5 %collective-permute-start.2 = (f32[10,16,4,128]{3,2,1,0:T(4,128)S(1)}, f32[10,16,4,128]{3,2,1,0:T(4,128)S(1)}, u32[]{:S(2)}, u32[]{:S(2)}) collective-permute-start(f32[10,16,4,128]{3,2,1,0:T(4,128)S(1)} %get-tuple-element.34), channel_id=1, source_target_pairs={{0,4},{4,0},{1,5},{5,1},{2,6},{6,2},{3,7},{7,3},{8,12},{12,8},{9,1... | collective-permute-start | bytes 983048 | tf_op jit(solution)/shard_map/ppermute | solution.py:636
  5.1 11.0 %collective-permute-start.3 = (f32[10,2,32,128]{3,2,1,0:T(8,128)S(1)}, f32[10,2,32,128]{3,2,1,0:T(8,128)S(1)}, u32[]{:S(2)}, u32[]{:S(2)}) collective-permute-start(f32[10,2,32,128]{3,2,1,0:T(8,128)S(1)} %get-tuple-element.37), channel_id=1, source_target_pairs={{0,8},{1,9},{2,10},{3,11},{4,12},{5,13},{6,14},{7,15},{8,0},{9,1},... | collective-permute-start | bytes 983048 | tf_op jit(solution)/shard_map/ppermute | solution.py:638
  6.6 4.2 %copy-start = (s32[1,2,8,6]{2,1,3,0:T(2,128)S(1)}, s32[1,2,8,6]{2,1,3,0:T(2,128)}, u32[]{:S(2)}) copy-start(s32[1,2,8,6]{2,1,3,0:T(2,128)} %param.11) | copy-start | bytes 1156
  6.6 4.2 %copy-start.1 = (s32[1,2,8]{2,1,0:T(2,128)S(1)}, s32[1,2,8]{2,1,0:T(2,128)}, u32[]{:S(2)}) copy-start(s32[1,2,8]{2,1,0:T(2,128)} %refine.1) | copy-start | bytes 196
  6.6 4.2 %copy-start.2 = (s32[1,2,8]{2,1,0:T(2,128)S(1)}, s32[1,2,8]{2,1,0:T(2,128)}, u32[]{:S(2)}) copy-start(s32[1,2,8]{2,1,0:T(2,128)} %owner.1) | copy-start | bytes 196
  6.6 4.2 %copy-start.3 = (s32[1,2,8]{2,1,0:T(2,128)S(1)}, s32[1,2,8]{2,1,0:T(2,128)}, u32[]{:S(2)}) copy-start(s32[1,2,8]{2,1,0:T(2,128)} %weight.1) | copy-start | bytes 196
  6.6 9.4 %collective-permute-start.4 = (f32[10,2,32,128]{3,2,1,0:T(8,128)S(1)}, f32[10,2,32,128]{3,2,1,0:T(8,128)S(1)}, u32[]{:S(2)}, u32[]{:S(2)}) collective-permute-start(f32[10,2,32,128]{3,2,1,0:T(8,128)S(1)} %get-tuple-element.24.dep), channel_id=1, source_target_pairs={{0,1},{1,0},{2,3},{3,2},{4,5},{5,4},{6,7},{7,6},{8,16},{9,17},{10,... | collective-permute-start | bytes 983048 | tf_op jit(solution)/shard_map/ppermute | solution.py:639
  9.1 4.6 %collective-permute-start.1 = (f32[10,1,8,128]{3,2,1,0:T(8,128)S(1)}, f32[10,1,8,128]{3,2,1,0:T(8,128)S(1)}, u32[]{:S(2)}, u32[]{:S(2)}) collective-permute-start(f32[10,1,8,128]{3,2,1,0:T(8,128)S(1)} %get-tuple-element.31), channel_id=1, source_target_pairs={{0,3},{1,2},{2,1},{3,0},{4,7},{5,6},{6,5},{7,4},{8,11},{9,10},{10,... | collective-permute-start | bytes 122888 | tf_op jit(solution)/shard_map/ppermute | solution.py:635
  10.8 2.9 %collective-permute-start = (f32[10,1,8,128]{3,2,1,0:T(8,128)S(1)}, f32[10,1,8,128]{3,2,1,0:T(8,128)S(1)}, u32[]{:S(2)}, u32[]{:S(2)}) collective-permute-start(f32[10,1,8,128]{3,2,1,0:T(8,128)S(1)} %get-tuple-element.27.ax_s), channel_id=1, source_target_pairs={{0,1},{1,0},{2,3},{3,2},{4,5},{5,4},{6,7},{7,6},{8,9},{9,8},{10,11... | collective-permute-start | bytes 122888 | tf_op jit(solution)/shard_map/ppermute | solution.py:634

commit v11 on v9

--- a/solution.py
+++ b/solution.py
@@ -34,7 +34,7 @@
     return [(i, (i + step) % count) for i in range(count)]
 
 
-def edge_kernel(dims, prim, adj, rad_a, rad_b, azi_s, sems):
+def edge_kernel(dims, n_rad, prim, adj, rad_a, rad_b, azi_s, sems):
     nr, na, nx = dims
     odd = lax.rem(lax.axis_index("rad"), 2)
     first = jnp.where(odd == 0, nr - 2, 0)
@@ -49,11 +49,19 @@
                 (src.at[:, :, pl.ds(na - 2, 2)], azi_s.at[rows, :, pl.ds(2, 2)]),
             )
         ):
-            copies.append(pltpu.make_async_copy(a, b, sems.at[t, i]))
-    for c in copies:
-        c.start()
-    for c in copies:
-        c.wait()
+            copies.append((i, pltpu.make_async_copy(a, b, sems.at[t, i])))
+    i_rad = lax.axis_index("rad")
+    alone = (i_rad == 0) | ((i_rad == n_rad - 1) & (odd == 1))
+    for act in ("start", "wait"):
+        for i, c in copies:
+            if i != 1:
+                getattr(c, act)()
+
+        @pl.when(jnp.logical_not(alone))
+        def _():
+            for i, c in copies:
+                if i == 1:
+                    getattr(c, act)()
 
 
 def lane_kernel(dims, prim, adj, first, second):
@@ -605,7 +613,7 @@
     vmem = pl.BlockSpec(memory_space=pltpu.VMEM)
 
     rad_a, rad_b, azi_s = pl.pallas_call(
-        functools.partial(edge_kernel, dims),
+        functools.partial(edge_kernel, dims, n_rad),
         out_shape=(f32((2 * F, 2, na, nx)), f32((2 * F, 2, na, nx)), f32((2 * F, nr, 4, nx))),
         in_specs=[hbm, hbm],
         out_specs=(vmem, vmem, vmem),

time: 28.2 us -> 28.1 us (level)
  no operation moved by 1% of the time
where the time goes in v11:
time: 28.1 us; the launch traced here: 27.9 us
  blocking collectives  12 us (43%)
  Pallas kernels  8.66 us (31%)
  starting transfers between devices  6.46 us (23%)
  between operations  0.77 us (3%)
    all_to_all x1, blocking collectives, on_device(): data = lax.all_to_all(send, AXES, 0, 0, tiled=True)  12 us
    ppermute x1, starting transfers between devices, on_device(): azi_l = lax.ppermute(azi_s, 'azi', ring(n_azi, 1))  3.03 us
    pallas_call x1, Pallas kernels, on_device(): pl.pallas_call(functools.partial(inner_kernel, dims, ((per_rad, per_azi,...  2.88 us
    pallas_call x1, Pallas kernels, on_device(): pl.pallas_call(functools.partial(axial_kernel, dims, n_ax), out_shape=(f3...  1.76 us
    ppermute x1, starting transfers between devices, on_device(): rad_a = lax.ppermute(rad_a, AXES, pair_round(sizes, 0, 0))  1.68 us
    pallas_call x1, Pallas kernels, on_device(): pl.pallas_call(functools.partial(edge_kernel, dims, n_rad), out_shape=(f3...  1.41 us
    ppermute x1, starting transfers between devices, on_device(): ax_b = lax.ppermute(ax_second, AXES, pair_round(sizes, 2, 1))  1.17 us
    pallas_call x1, Pallas kernels, on_device(): pl.pallas_call(functools.partial(final_kernel, n_loc, per_ax), out_shape=...  0.94 us
  transfers between devices with their start and end apart: 5, of which 0 were waited for; matrix products, arithmetic and copies ran while one was open for 0% of the time, Pallas kernels for 21%

profile of v11, /device:TPU:0, one launch (start us, length us, event | category | flops | bytes accessed | tf_op | source)
XLA Modules:
  0.0 27.9 jit_solution(16983587615428582302)
XLA Ops:
  0.6 0.0 copy-start
  0.6 0.0 copy-start.1
  0.7 0.0 copy-start.2
  0.7 0.0 copy-start.5
  0.7 0.0 copy-start.3
  0.7 0.0 copy-start.4
  0.7 1.4 %edges.1 = (f32[10,2,32,128]{3,2,1,0:T(8,128)S(1)}, f32[10,2,32,128]{3,2,1,0:T(8,128)S(1)}, f32[10,16,4,128]{3,2,1,0:T(4,128)S(1)}) custom-call(f32[5,16,32,128]{3,2,1,0:T(8,128)} %prim.9, f32[5,16,32,128]{3,2,1,0:T(8,128)} %adj.5), custom_call_target="tpu_custom_call" | custom-call | tf_op jit(solution)/shard_map/edges/pallas_call | solution.py:615
  2.1 3.0 %collective-permute-start.2 = (f32[10,16,4,128]{3,2,1,0:T(4,128)S(1)}, f32[10,16,4,128]{3,2,1,0:T(4,128)S(1)}, u32[]{:S(2)}, u32[]{:S(2)}) collective-permute-start(f32[10,16,4,128]{3,2,1,0:T(4,128)S(1)} %get-tuple-element.29), channel_id=1, source_target_pairs={{0,4},{4,0},{1,5},{5,1},{2,6},{6,2},{3,7},{7,3},{8,12},{12,8},{9,1... | collective-permute-start | bytes 983048 | tf_op jit(solution)/shard_map/ppermute | solution.py:635
  5.1 1.7 %collective-permute-start.3 = (f32[10,2,32,128]{3,2,1,0:T(8,128)S(1)}, f32[10,2,32,128]{3,2,1,0:T(8,128)S(1)}, u32[]{:S(2)}, u32[]{:S(2)}) collective-permute-start(f32[10,2,32,128]{3,2,1,0:T(8,128)S(1)} %get-tuple-element.32), channel_id=1, source_target_pairs={{0,8},{1,9},{2,10},{3,11},{4,12},{5,13},{6,14},{7,15},{8,0},{9,1},... | collective-permute-start | bytes 983048 | tf_op jit(solution)/shard_map/ppermute | solution.py:637
  6.8 0.0 collective-permute-start.4
  6.8 0.0 copy-done
  6.8 0.0 copy-done.1
  6.8 0.7 %lanes.1 = (f32[10,1,8,128]{3,2,1,0:T(8,128)S(1)}, f32[10,1,8,128]{3,2,1,0:T(8,128)S(1)}) custom-call(f32[5,16,32,128]{3,2,1,0:T(8,128)S(1)} %copy-done, f32[5,16,32,128]{3,2,1,0:T(8,128)S(1)} %copy-done.1), custom_call_target="tpu_custom_call" | custom-call | tf_op jit(solution)/shard_map/lanes/pallas_call | solution.py:624
  7.6 0.6 %collective-permute-start = (f32[10,1,8,128]{3,2,1,0:T(8,128)S(1)}, f32[10,1,8,128]{3,2,1,0:T(8,128)S(1)}, u32[]{:S(2)}, u32[]{:S(2)}) collective-permute-start(f32[10,1,8,128]{3,2,1,0:T(8,128)S(1)} %get-tuple-element.22.ax_s), channel_id=1, source_target_pairs={{0,1},{1,0},{2,3},{3,2},{4,5},{5,4},{6,7},{7,6},{8,9},{9,8},{10,11... | collective-permute-start | bytes 122888 | tf_op jit(solution)/shard_map/ppermute | solution.py:633
  8.1 1.2 %collective-permute-start.1 = (f32[10,1,8,128]{3,2,1,0:T(8,128)S(1)}, f32[10,1,8,128]{3,2,1,0:T(8,128)S(1)}, u32[]{:S(2)}, u32[]{:S(2)}) collective-permute-start(f32[10,1,8,128]{3,2,1,0:T(8,128)S(1)} %get-tuple-element.26), channel_id=1, source_target_pairs={{0,3},{1,2},{2,1},{3,0},{4,7},{5,6},{6,5},{7,4},{8,11},{9,10},{10,... | collective-permute-start | bytes 122888 | tf_op jit(solution)/shard_map/ppermute | solution.py:634
  9.3 0.0 copy-done.2
  9.3 0.0 copy-done.5
  9.3 0.0 copy-done.3
  9.3 0.0 copy-done.4
  9.3 2.9 %inner.1 = (f32[2560,256]{1,0:T(8,128)S(1)}, f32[2560,128]{1,0:T(8,128)S(1)}, f32[1,256]{1,0:T(1,128)S(1)}, f32[10,16,32,128]{3,2,1,0:T(8,128)S(1)}) custom-call(f32[5,16,32,128]{3,2,1,0:T(8,128)S(1)} %copy-done, f32[5,16,32,128]{3,2,1,0:T(8,128)S(1)} %copy-done.1, f32[10,1,8,128]{3,2,1,0:T(8,128)S(1)} %get-tuple-element.22.ax_s, ...), custom_call_target="tpu_custom_call" | custom-call | tf_op jit(solution)/shard_map/inner/pallas_call | solution.py:644
  12.2 0.0 collective-permute-done.ax_a
  12.2 0.0 collective-permute-done.1.ax_b
  12.2 1.8 %axial.1 = (f32[10,16,32,128]{3,2,1,0:T(8,128)S(1)}, f32[16,32,128]{2,1,0:T(8,128)S(1)}) custom-call(f32[2560,256]{1,0:T(8,128)S(1)} %get-tuple-element.23.sums, f32[2560,128]{1,0:T(8,128)S(1)} %get-tuple-element.24.fourth, f32[10,16,32,128]{3,2,1,0:T(8,128)S(1)} %get-tuple-element.25.part_bw, f32[10,1,8,128]{3,2,1,0:T(8,128)S(1)} %collective-permute-done.ax_a, ...), custom_call_target="tpu_custom_call" | custom-call | tf_op jit(solution)/shard_map/axial/pallas_call | solution.py:663
  14.0 0.0 collective-permute-done.2.azi_l.azi_r
  14.0 0.5 %rows.1 = (f32[16,32,128]{2,1,0:T(8,128)S(1)}, f32[10,4,32,128]{3,2,1,0:T(8,128)S(1)}, f32[4,8,128]{2,1,0:T(8,128)S(1)}) custom-call(f32[5,16,32,128]{3,2,1,0:T(8,128)S(1)} %copy-done, f32[10,16,32,128]{3,2,1,0:T(8,128)S(1)} %get-tuple-element.27.bw, f32[16,32,128]{2,1,0:T(8,128)S(1)} %get-tuple-element.28.done, ...), custom_call_target="tpu_custom_call" | custom-call | tf_op jit(solution)/shard_map/rows/pallas_call | solution.py:679
  14.6 0.0 collective-permute-done.3.rad_a
  14.6 0.0 collective-permute-done.4.rad_b
  14.6 0.4 %planes.1 = (f32[4,32,128]{2,1,0:T(8,128)S(1)}, f32[64,128]{1,0:T(8,128)S(1)}) custom-call(f32[5,16,32,128]{3,2,1,0:T(8,128)S(1)} %copy-done, f32[10,4,32,128]{3,2,1,0:T(8,128)S(1)} %get-tuple-element.30.ends, f32[4,8,128]{2,1,0:T(8,128)S(1)} %get-tuple-element.31.part_sums, f32[10,2,32,128]{3,2,1,0:T(8,128)S(1)} %collective-permute-done.3.rad_a, ...), custom_call_target="tpu_custom_call" | custom-call | tf_op jit(solution)/shard_map/planes/pallas_call | solution.py:687
  15.0 12.0 %all_to_all.11 = f32[32,2,128]{2,1,0:T(2,128)S(1)} all-to-all(f32[32,2,128]{2,1,0:T(2,128)S(1)} %bitcast.4), channel_id=1, replica_groups=mesh['rad'=4,'azi'=2,'ax'=4] {'rad','azi','ax'}, dimensions={0} | all-to-all | bytes 65536 | tf_op jit(solution)/shard_map/all_to_all | solution.py:696
  27.0 0.9 %blocks.1 = (f32[1,2,8]{2,1,0:T(2,128)}, f32[1,1,1]{2,1,0:T(1,128)}, f32[16,32,128]{2,1,0:T(8,128)}) custom-call(f32[64,128]{1,0:T(8,128)S(1)} %bitcast.3, f32[16,32,128]{2,1,0:T(8,128)S(1)} %get-tuple-element.36.inside, f32[4,32,128]{2,1,0:T(8,128)S(1)} %get-tuple-element.37.outside), custom_call_target="tpu_custom_call" | custom-call | tf_op jit(solution)/shard_map/blocks/pallas_call | solution.py:698
Async XLA Ops:
  0.6 6.2 %copy-start = (f32[5,16,32,128]{3,2,1,0:T(8,128)S(1)}, f32[5,16,32,128]{3,2,1,0:T(8,128)}, u32[]{:S(2)}) copy-start(f32[5,16,32,128]{3,2,1,0:T(8,128)} %prim.9) | copy-start | bytes 3932164
  0.6 6.2 %copy-start.1 = (f32[5,16,32,128]{3,2,1,0:T(8,128)S(1)}, f32[5,16,32,128]{3,2,1,0:T(8,128)}, u32[]{:S(2)}) copy-start(f32[5,16,32,128]{3,2,1,0:T(8,128)} %adj.5) | copy-start | bytes 3932164
  0.7 8.7 %copy-start.2 = (s32[1,2,8,6]{2,1,3,0:T(2,128)S(1)}, s32[1,2,8,6]{2,1,3,0:T(2,128)}, u32[]{:S(2)}) copy-start(s32[1,2,8,6]{2,1,3,0:T(2,128)} %param.11) | copy-start | bytes 1156
  0.7 8.7 %copy-start.5 = (s32[1,2,8]{2,1,0:T(2,128)S(1)}, s32[1,2,8]{2,1,0:T(2,128)}, u32[]{:S(2)}) copy-start(s32[1,2,8]{2,1,0:T(2,128)} %weight.1) | copy-start | bytes 196
  0.7 8.7 %copy-start.3 = (s32[1,2,8]{2,1,0:T(2,128)S(1)}, s32[1,2,8]{2,1,0:T(2,128)}, u32[]{:S(2)}) copy-start(s32[1,2,8]{2,1,0:T(2,128)} %refine.1) | copy-start | bytes 196
  0.7 8.6 %copy-start.4 = (s32[1,2,8]{2,1,0:T(2,128)S(1)}, s32[1,2,8]{2,1,0:T(2,128)}, u32[]{:S(2)}) copy-start(s32[1,2,8]{2,1,0:T(2,128)} %owner.1) | copy-start | bytes 196
  2.1 11.9 %collective-permute-start.2 = (f32[10,16,4,128]{3,2,1,0:T(4,128)S(1)}, f32[10,16,4,128]{3,2,1,0:T(4,128)S(1)}, u32[]{:S(2)}, u32[]{:S(2)}) collective-permute-start(f32[10,16,4,128]{3,2,1,0:T(4,128)S(1)} %get-tuple-element.29), channel_id=1, source_target_pairs={{0,4},{4,0},{1,5},{5,1},{2,6},{6,2},{3,7},{7,3},{8,12},{12,8},{9,1... | collective-permute-start | bytes 983048 | tf_op jit(solution)/shard_map/ppermute | solution.py:635
  5.1 9.4 %collective-permute-start.3 = (f32[10,2,32,128]{3,2,1,0:T(8,128)S(1)}, f32[10,2,32,128]{3,2,1,0:T(8,128)S(1)}, u32[]{:S(2)}, u32[]{:S(2)}) collective-permute-start(f32[10,2,32,128]{3,2,1,0:T(8,128)S(1)} %get-tuple-element.32), channel_id=1, source_target_pairs={{0,8},{1,9},{2,10},{3,11},{4,12},{5,13},{6,14},{7,15},{8,0},{9,1},... | collective-permute-start | bytes 983048 | tf_op jit(solution)/shard_map/ppermute | solution.py:637
  6.8 7.8 %collective-permute-start.4 = (f32[10,2,32,128]{3,2,1,0:T(8,128)S(1)}, f32[10,2,32,128]{3,2,1,0:T(8,128)S(1)}, u32[]{:S(2)}, u32[]{:S(2)}) collective-permute-start(f32[10,2,32,128]{3,2,1,0:T(8,128)S(1)} %get-tuple-element.33), channel_id=1, source_target_pairs={{0,1},{1,0},{2,3},{3,2},{4,5},{5,4},{6,7},{7,6},{8,16},{9,17},{10,... | collective-permute-start | bytes 983048 | tf_op jit(solution)/shard_map/ppermute | solution.py:638
  7.6 4.7 %collective-permute-start = (f32[10,1,8,128]{3,2,1,0:T(8,128)S(1)}, f32[10,1,8,128]{3,2,1,0:T(8,128)S(1)}, u32[]{:S(2)}, u32[]{:S(2)}) collective-permute-start(f32[10,1,8,128]{3,2,1,0:T(8,128)S(1)} %get-tuple-element.22.ax_s), channel_id=1, source_target_pairs={{0,1},{1,0},{2,3},{3,2},{4,5},{5,4},{6,7},{7,6},{8,9},{9,8},{10,11... | collective-permute-start | bytes 122888 | tf_op jit(solution)/shard_map/ppermute | solution.py:633
  8.1 4.1 %collective-permute-start.1 = (f32[10,1,8,128]{3,2,1,0:T(8,128)S(1)}, f32[10,1,8,128]{3,2,1,0:T(8,128)S(1)}, u32[]{:S(2)}, u32[]{:S(2)}) collective-permute-start(f32[10,1,8,128]{3,2,1,0:T(8,128)S(1)} %get-tuple-element.26), channel_id=1, source_target_pairs={{0,3},{1,2},{2,1},{3,0},{4,7},{5,6},{6,5},{7,4},{8,11},{9,10},{10,... | collective-permute-start | bytes 122888 | tf_op jit(solution)/shard_map/ppermute | solution.py:634
